TPU v7x, 256 devices: a whole 4x4x8 slice. The times are simulated.
256 devices in a mesh: ens: 8 (over z_lo, y), space: 32 (over x, z_hi, core).
Axes of the slice: x: 4, y: 4, z: 8 (z_hi: 4, z_lo: 2; z = z_hi * 2 + z_lo), core: 2. Of those that a mesh axis runs over, the one named last changes fastest.
Arguments:
- hidden: bfloat16 [8, 1024, 32768], P('ens', None, 'space'), may hold values from -6 to 6
- target: float32 [100, 32768], P(None, 'space'), may hold values from -6 to 6
- area_index: int32 [32768], P('space'), may hold values from 0 to 720
- area_table: float32 [721], replicated, may hold values from 0.1 to 3
- var_weight: float32 [100], replicated, may hold values from 0.25 to 2
- w_first: bfloat16 [1024, 1024], replicated, may hold values from -0.1875 to 0.1875
- b_first: float32 [1024], replicated, may hold values from -3 to 3
- w_second: bfloat16 [1024, 100], replicated, may hold values from -0.1875 to 0.1875
- b_second: float32 [100], replicated, may hold values from -3 to 3
Outputs:
- loss: float32 [], replicated
- grad_hidden: bfloat16 [8, 1024, 32768], P('ens', None, 'space')
- grad_w_first: float32 [1024, 1024], P('space')
- grad_b_first: float32 [1024], P('space')
- grad_w_second: float32 [1024, 100], P('space')
- grad_b_second: float32 [100], replicated
All inputs are finite; a program needn't handle non-finite values.
Results may differ from a plain program's by a relative error of at most 0.011.
Values sent between devices are 32-bit elements; how exact they have to be, the bound alone decides.
No kernel may reach another device: no remote copies, remote signals or barrier semaphores. Data moves between devices by JAX's collectives and lax.ppermute only.
A program may use at most 64 MiB of HBM per device.

v0:
```python
import math

import jax
import jax.numpy as jnp
from jax import lax
from jax.sharding import PartitionSpec as P

smoothing = 0.0025
loss_scale = 64.0


def pair_terms(fields, others):
    differ = fields - others
    radius = jnp.sqrt(differ * differ + smoothing)
    return (jnp.sum(radius, axis=0), jnp.sum(differ / radius, axis=0))


def on_device(
    hidden, target, area_index, area_table, var_weight, w_first, b_first, w_second, b_second
):
    members = lax.axis_size("ens")
    columns = hidden.shape[2]
    features = hidden[0]
    pre = (
        jnp.einsum("io,ip->op", w_first, features, preferred_element_type=jnp.float32)
        + b_first[:, None]
    )
    hidden_act = jax.nn.gelu(pre).astype(jnp.bfloat16)
    mine = (
        jnp.einsum("ov,op->vp", w_second, hidden_act, preferred_element_type=jnp.float32)
        + b_second[:, None]
    )
    table_rows = area_table.shape[0]
    onehot = (area_index[:, None] == jnp.arange(table_rows, dtype=jnp.int32)[None, :]).astype(
        jnp.float32
    )
    area = jnp.dot(onehot, area_table, precision=lax.Precision.HIGHEST)
    coef = var_weight[:, None] * area[None, :]
    spread_add, pull_add = pair_terms(
        mine[None], lax.all_gather(mine[None], "ens", axis=0, tiled=True)
    )
    miss = mine - target
    skill = jnp.sqrt(miss * miss + smoothing)
    crps = skill / members - spread_add / (2.0 * members * (members - 1))
    loss_part = jnp.sum(coef * crps)
    slope = miss / skill / members - pull_add / (1.0 * members * (members - 1))
    grad_x = (loss_scale * coef * slope).astype(jnp.bfloat16)
    grad_z = jnp.einsum("ov,vp->op", w_second, grad_x, preferred_element_type=jnp.float32)
    grad_pre = jax.vjp(jax.nn.gelu, pre)[1](grad_z)[0].astype(jnp.bfloat16)
    grad_feat = jnp.einsum(
        "io,op->ip", w_first, grad_pre, preferred_element_type=jnp.float32
    ).astype(jnp.bfloat16)
    part_w1 = jnp.einsum("ip,op->io", features, grad_pre, preferred_element_type=jnp.float32)
    part_w2 = jnp.einsum("op,vp->ov", hidden_act, grad_x, preferred_element_type=jnp.float32)
    part_b1 = jnp.sum(grad_pre.astype(jnp.float32), axis=1)
    part_b2 = jnp.sum(grad_x.astype(jnp.float32), axis=1)
    loss_sum, bias_sum = lax.psum((loss_part, part_b2), ("ens", "space"))
    whole_w1, whole_w2, whole_b1 = lax.psum((part_w1, part_w2, part_b1), ("ens", "space"))
    share = whole_w1.shape[0] // lax.axis_size("space")
    offset = lax.axis_index("space") * share
    sum_w1 = lax.dynamic_slice_in_dim(whole_w1, offset, share, 0)
    sum_w2 = lax.dynamic_slice_in_dim(whole_w2, offset, share, 0)
    sum_b1 = lax.dynamic_slice_in_dim(whole_b1, offset, share, 0)
    total_points = columns * lax.axis_size("space")
    factor = 1.0 / math.sqrt(members * total_points)
    loss = loss_sum / total_points
    return (
        loss,
        grad_feat[None],
        sum_w1 * factor,
        sum_b1 * factor,
        sum_w2 * factor,
        bias_sum * factor,
    )


def solution(mesh):
    in_specs = (P("ens", None, "space"), P(None, "space"), P("space"), P(), P(), P(), P(), P(), P())
    out_specs = (P(), P("ens", None, "space"), P("space", None), P("space"), P("space", None), P())
    return jax.shard_map(
        on_device, mesh=mesh, in_specs=in_specs, out_specs=out_specs, check_vma=False
    )
```

profile of v0, /device:TPU:2, one launch (start us, length us, event | category | flops | bytes accessed | tf_op | source)
XLA Modules:
  0.0 368.4 jit_solution(254239383439733305)
XLA Ops:
  7.2 0.0 copy-start
  7.2 0.0 copy-start.5
  7.2 0.0 all-gather.4.cloned.1.call-start
  7.3 1.5 copy-done
  8.8 7.0 %multiply_convert_fusion = (bf16[1024,1024]{0,1:T(8,128)(2,1)S(1)}, f32[1024,1024]{0,1:T(8,128)}) fusion(f32[1024]{0:T(1024)} %param.15, bf16[1024,1024]{1,0:T(8,128)(2,1)} %param.14, bf16[1,1024,1024]{2,1,0:T(8,128)(2,1)S(1)} %copy-done), kind=kOutput, calls=%fused_computation.15 | convolution fusion | flops 2157969408 | bytes 10489856 | tf_op jit(solution)/shard_map/io,ip->op/dot_general | solution.py:25
  15.7 1.3 copy-done.1
  17.1 0.0 copy-done.7
  17.1 1.6 convolution_add_fusion
  18.6 0.0 all-gather.4.cloned.1.call-update
  18.7 0.2 all-reduce.4.cloned.1.call-start
  18.9 0.0 copy-done.6
  18.9 1.5 fusion.13
  20.5 49.2 %all-gather.4.cloned.1.call-done = f32[8,100,1024]{2,1,0:T(8,128)} async-done(((f32[1,100,1024]{2,1,0:T(8,128)}), f32[8,100,1024]{2,1,0:T(8,128)}) %all-gather.4.cloned.1.call-update) | async-done | bytes 3276816 | tf_op jit(solution)/shard_map/all_gather | solution.py:40
  69.6 4.1 %fusion.12 = (f32[100,1024]{1,0:T(8,128)S(1)}, f32[100,1024]{1,0:T(8,128)S(1)}) fusion(f32[8,100,1024]{2,1,0:T(8,128)} %all-gather.4.cloned.1.call-done, f32[100,1024]{1,0:T(8,128)} %bitcast.45), kind=kLoop, calls=%fused_computation.19 | loop fusion | flops 4710400 | bytes 4505600 | tf_op jit(solution)/shard_map/reduce_sum | solution.py:15
  73.8 0.0 copy-start.10
  73.8 1.0 convert_reduce_fusion.1
  74.9 1.6 fusion.22
  76.4 0.0 copy-done.12
  76.4 3.5 convert_reduce_fusion
  79.9 0.0 copy-start.11
  79.9 1.3 copy-done.11
  81.2 4.4 %convolution_bitcast_fusion = f32[1024,1024]{0,1:T(8,128)} fusion(bf16[1024,1024]{0,1:T(8,128)(2,1)S(1)} %get-tuple-element.31, bf16[1,1024,1024]{2,1,0:T(8,128)(2,1)S(1)} %copy-done), kind=kOutput, calls=%fused_computation.22 | convolution fusion | flops 2147483648 | bytes 8388608 | tf_op jit(solution)/shard_map/ip,op->io/dot_general | solution.py:53
  85.6 0.0 all-reduce.4.cloned.1.call-update
  85.7 76.1 %all-reduce = (f32[]{:T(128)}, f32[1024]{0:T(1024)S(1)}, f32[100]{0:T(128)S(1)}) all-reduce(f32[]{:T(128)} %get-tuple-element.27, f32[1024]{0:T(1024)S(1)} %get-tuple-element.30, f32[100]{0:T(128)S(1)} %get-tuple-element.25), channel_id=1, replica_groups=mesh['ens'=8,'space'=32] {'ens','space'}, use_global_device_ids=true, to_apply=%region_2.0 | all-reduce | flops 1125 | bytes 9000 | tf_op jit(solution)/shard_map/psum | solution.py:57
  161.7 6.0 %convert_bitcast_fusion = bf16[1,1024,1024]{1,2,0:T(8,128)(2,1)} fusion(bf16[1024,1024]{0,1:T(8,128)(2,1)} %copy-done.11, bf16[1024,1024]{1,0:T(8,128)(2,1)} %param.14), kind=kOutput, calls=%fused_computation.26 | convolution fusion | flops 2148532224 | bytes 6291456 | tf_op jit(solution)/shard_map/io,op->ip/dot_general | solution.py:50
  167.7 3.9 %copy.17 = bf16[1,1024,1024]{2,1,0:T(8,128)(2,1)} copy(bf16[1,1024,1024]{1,2,0:T(8,128)(2,1)} %convert_bitcast_fusion) | data formatting | bytes 4194304
  172.3 0.6 dynamic-slice_multiply_fusion.2
  172.9 0.5 broadcast_multiply_fusion
  173.4 183.6 %all-reduce.4.cloned.1.call-done = (f32[1024,1024]{0,1:T(8,128)}, f32[1024,100]{1,0:T(8,128)}) async-done(((f32[1024,1024]{0,1:T(8,128)}, f32[1024,100]{1,0:T(8,128)}), (f32[1024,1024]{0,1:T(8,128)}, f32[1024,100]{1,0:T(8,128)})) %all-reduce.4.cloned.1.call-update) | async-done | bytes 4603920 | tf_op jit(solution)/shard_map/psum | solution.py:58
  357.0 1.2 dynamic-slice_multiply_fusion
  358.2 1.3 dynamic-slice_multiply_fusion.1
  359.6 0.8 copy.18
  (17 shorter events, 0.0 us)
Async XLA Ops:
  7.2 1.6 copy-start
  7.2 9.9 %copy-start.5 = (bf16[1024,100]{0,1:T(8,128)(2,1)S(1)}, bf16[1024,100]{0,1:T(8,128)(2,1)}, u32[]{:S(2)}) copy-start(bf16[1024,100]{0,1:T(8,128)(2,1)} %param.16) | copy-start | bytes 614404
  7.2 9.9 %copy-start.7 = (f32[100]{0:T(128)S(1)}, f32[100]{0:T(128)}, u32[]{:S(2)}) copy-start(f32[100]{0:T(128)} %param.17) | copy-start | bytes 1204
  7.2 11.7 %copy-start.6 = (f32[721]{0:T(1024)S(1)}, f32[721]{0:T(1024)}, u32[]{:S(2)}) copy-start(f32[721]{0:T(1024)} %param.12) | copy-start | bytes 8656
  7.2 11.7 %copy-start.9 = (s32[1024]{0:T(1024)S(1)}, s32[1024]{0:T(1024)}, u32[]{:S(2)}) copy-start(s32[1024]{0:T(1024)} %param.11) | copy-start | bytes 12292
  7.2 62.4 %all-gather.4.cloned.1.call-start = ((), (), s32[]{:S(2)}) async-start(), calls=%async_computation | async-start | bytes 3833856 | tf_op jit(solution)/shard_map/all_gather | solution.py:40
  15.7 1.3 copy-start.1
  17.1 56.7 %copy-start.4 = (f32[100,1024]{1,0:T(8,128)S(1)}, f32[100,1024]{1,0:T(8,128)}, u32[]{:S(2)}) copy-start(f32[100,1024]{1,0:T(8,128)} %param.10) | copy-start | bytes 1228804
  17.1 56.8 %copy-start.8 = (f32[100]{0:T(128)S(1)}, f32[100]{0:T(128)}, u32[]{:S(2)}) copy-start(f32[100]{0:T(128)} %param.13) | copy-start | bytes 1204
  18.6 55.2 %copy-start.3 = (f32[1024,100]{0,1:T(8,128)S(1)}, f32[1024,100]{0,1:T(8,128)}, u32[]{:S(2)}) copy-start(f32[1024,100]{0,1:T(8,128)} %convolution_add_fusion) | copy-start | bytes 1228804
  18.7 338.3 %all-reduce.4.cloned.1.call-start = ((), (), s32[]{:S(2)}) async-start(), calls=%async_computation.1 | async-start | bytes 9437184 | tf_op jit(solution)/shard_map/psum | solution.py:58
  69.6 5.2 %copy-start.2 = (bf16[1024,1024]{0,1:T(8,128)(2,1)S(1)}, bf16[1024,1024]{0,1:T(8,128)(2,1)}, u32[]{:S(2)}) copy-start(bf16[1024,1024]{0,1:T(8,128)(2,1)} %copy-done.1) | copy-start | bytes 6291460
  73.8 2.6 copy-start.10
  73.8 2.6 copy-start.12
  79.9 1.3 copy-start.11
Sparse Core Ops, SparseCore 0:
  18.8 50.7 all-gather.3
  85.8 271.1 all-reduce.3
where the time goes:
time: 369 us; the launch traced here: 368 us
  waiting for transfers between devices  233 us (63%)
  blocking collectives  76.1 us (21%)
  matrix products  25.5 us (7%)
  between operations  16 us (4%)
  local copies, waits for them, and re-layouts  8.95 us (2%)
  other arithmetic  8.84 us (2%)
    psum x1, waiting for transfers between devices, on_device(): lax.psum((part_w1, part_w2, part_b1), ('ens', 'space'))  184 us
    psum x1, blocking collectives, on_device(): loss_sum, bias_sum = lax.psum((loss_part, part_b2), ('ens', 'space'))  76.1 us
    all_gather x1, waiting for transfers between devices, on_device(): lax.all_gather(mine[None], 'ens', axis=0, tiled=True)  49.2 us
    unnamed x29, local copies, waits for them, and re-layouts  8.95 us
  transfers between devices with their start and end apart: 2, of which 2 were waited for; matrix products, arithmetic and copies ran while one was open for 3% of the time, Pallas kernels for 0%

commit v1 on v0

v1 whole, which is shorter than its diff:
```python
import math

import jax
import jax.numpy as jnp
from jax import lax
from jax.sharding import Mesh, PartitionSpec as P

smoothing = 0.0025
loss_scale = 64.0
ens = ("zl", "y")
space = ("x", "zh", "c")
plane = ("y", "x")
wide = 1152


def on_device(
    hidden, target, area_index, area_table, var_weight, w_first, b_first, w_second, b_second
):
    f32, bf16 = jnp.float32, jnp.bfloat16
    members = lax.axis_size(ens)
    columns = hidden.shape[2]
    variables = target.shape[0]
    channels = w_first.shape[0]
    slab = columns // members
    me = lax.axis_index(ens)
    features = hidden[0]
    pre = jnp.einsum("io,ip->op", w_first, features, preferred_element_type=f32) + b_first[:, None]
    hidden_act = jax.nn.gelu(pre).astype(bf16)
    mine = (
        jnp.einsum("ov,op->vp", w_second, hidden_act, preferred_element_type=f32)
        + b_second[:, None]
    )
    pieces = mine.reshape(variables, members, slab).transpose(1, 0, 2)
    fields = lax.all_to_all(pieces, ens, 0, 0)
    rows = lax.dynamic_slice_in_dim(area_index, me * slab, slab, 0)
    goal = lax.dynamic_slice_in_dim(target, me * slab, slab, 1)
    table_rows = area_table.shape[0]
    onehot = (rows[:, None] == jnp.arange(table_rows, dtype=jnp.int32)[None, :]).astype(f32)
    area = jnp.dot(onehot, area_table, precision=lax.Precision.HIGHEST)
    coef = var_weight[:, None] * area[None, :]
    differ = fields[:, None] - fields[None, :]
    radius = jnp.sqrt(differ * differ + smoothing)
    spread = jnp.sum(radius, axis=1)
    pull = jnp.sum(differ / radius, axis=1)
    miss = fields - goal[None]
    skill = jnp.sqrt(miss * miss + smoothing)
    crps = skill / members - spread / (2.0 * members * (members - 1))
    loss_part = jnp.sum(coef[None] * crps)
    slope = miss / skill / members - pull / (1.0 * members * (members - 1))
    slope = coef[None] * slope
    part_b2 = jnp.sum((loss_scale * slope).astype(bf16).astype(f32), axis=(0, 2))
    back = loss_scale * lax.all_to_all(slope, ens, 0, 0)
    grad_x = back.transpose(1, 0, 2).reshape(variables, columns).astype(bf16)
    grad_z = jnp.einsum("ov,vp->op", w_second, grad_x, preferred_element_type=f32)
    grad_pre = jax.vjp(jax.nn.gelu, pre)[1](grad_z)[0].astype(bf16)
    part_w1 = jnp.einsum("ip,op->io", features, grad_pre, preferred_element_type=f32)
    part_w2 = jnp.einsum("op,vp->ov", hidden_act, grad_x, preferred_element_type=f32)
    part_b1 = jnp.sum(grad_pre.astype(f32), axis=1)
    nx, nzh, nc, ny = (lax.axis_size(a) for a in ("x", "zh", "c", "y"))
    share = channels // (nx * nzh * nc)
    misc = jnp.concatenate([part_b2, loss_part[None], jnp.zeros((27,), f32)]).reshape(4, share).T
    misc = jnp.tile(misc, (channels // share, 1))
    spare = wide - channels - variables - 1 - 4
    part = jnp.concatenate(
        [part_w1, part_w2, part_b1[:, None], misc, jnp.zeros((channels, spare), f32)], axis=1
    )
    part = part.reshape(nx, nzh, nc, ny, share // ny, wide)
    core = lax.axis_index("c")
    keep = lax.dynamic_index_in_dim(part, core, 2, keepdims=False)
    send = lax.dynamic_index_in_dim(part, 1 - core, 2, keepdims=False)
    other = lax.ppermute(send, "c", [(0, 1), (1, 0)])
    grad_feat = jnp.einsum("io,op->ip", w_first, grad_pre, preferred_element_type=f32).astype(bf16)
    half = (keep + other).transpose(2, 0, 1, 3, 4).reshape(ny * nx, nzh, share // ny, wide)
    half = jnp.sum(lax.all_to_all(half, plane, 0, 0), axis=0)
    half = jnp.sum(lax.all_to_all(half, "zh", 0, 0), axis=0)
    whole = lax.all_to_all(jnp.broadcast_to(half[None], (members,) + half.shape), ens, 0, 0)
    whole = whole.reshape(members // ny, ny, share // ny, wide).sum(0).reshape(share, wide)
    total_points = columns * lax.axis_size(space)
    factor = 1.0 / math.sqrt(members * total_points)
    sums = whole[:, channels + variables + 1 : channels + variables + 5].T.reshape(-1)
    return (
        sums[variables] / total_points,
        grad_feat[None],
        whole[:, :channels] * factor,
        whole[:, channels + variables] * factor,
        whole[:, channels : channels + variables] * factor,
        sums[:variables] * factor,
    )


def solution(mesh):
    fine = Mesh(mesh.devices.reshape(2, 4, 4, 4, 2), ("zl", "y", "x", "zh", "c"))
    in_specs = (P(ens, None, space), P(None, space), P(space), P(), P(), P(), P(), P(), P())
    out_specs = (P(), P(ens, None, space), P(space, None), P(space), P(space, None), P())
    return jax.shard_map(
        on_device, mesh=fine, in_specs=in_specs, out_specs=out_specs, check_vma=False
    )
```

time: 369 us -> 147 us (0.40)
  waiting for transfers between devices: 233 us -> 18.4 us
  blocking collectives: 76.1 us -> 51.9 us
  between operations: 16 us -> 2.64 us
  starting transfers between devices: 0.26 us -> 13.1 us
  local copies, waits for them, and re-layouts: 8.95 us -> 21 us
    psum x1 -> x0, waiting for transfers between devices: 184 us -> none  [on_device(): lax.psum((part_w1, part_w2, part_b1), ('ens', 'space'))]
    psum x1 -> x0, blocking collectives: 76.1 us -> none  [on_device(): loss_sum, bias_sum = lax.psum((loss_part, part_b2), ('ens', 'space'))]
    all_to_all x0 -> x2, blocking collectives: none -> 51.9 us  [the longest x1 35.5 us: on_device(): half = jnp.sum(lax.all_to_all(half, plane, 0, 0), axis=0)]
    all_gather x1 -> x0, waiting for transfers between devices: 49.2 us -> none  [on_device(): lax.all_gather(mine[None], 'ens', axis=0, tiled=True)]
    all_to_all x0 -> x3, waiting for transfers between devices: none -> 13.9 us  [the longest x1 7.2 us: on_device(): back = loss_scale * lax.all_to_all(slope, ens, 0, 0)]
    all_to_all x0 -> x3, starting transfers between devices: none -> 13 us  [the longest x1 5.96 us: on_device(): fields = lax.all_to_all(pieces, ens, 0, 0)]
    concatenate x0 -> x2, local copies, waits for them, and re-layouts: none -> 6.56 us  [on_device(): jnp.concatenate([part_w1, part_w2, part_b1[:, None], misc, jnp.zeros((cha...]
    ppermute x0 -> x1, waiting for transfers between devices: none -> 4.52 us  [on_device(): other = lax.ppermute(send, 'c', [(0, 1), (1, 0)])]
  transfers between devices with their start and end apart: 2 -> 4, of which waited for: 2 -> 3; matrix products, arithmetic and copies ran while one was open for 3% -> 9% of each run, Pallas kernels for 0% -> 0%
where the time goes in v1:
time: 147 us; the launch traced here: 145 us
  blocking collectives  51.9 us (35%)
  matrix products  26.5 us (18%)
  local copies, waits for them, and re-layouts  21 us (14%)
  waiting for transfers between devices  18.4 us (13%)
  starting transfers between devices  13.1 us (9%)
  other arithmetic  11.3 us (8%)
  between operations  2.64 us (2%)
    all_to_all x1, blocking collectives, on_device(): half = jnp.sum(lax.all_to_all(half, plane, 0, 0), axis=0)  35.5 us
    all_to_all x1, blocking collectives, on_device(): half = jnp.sum(lax.all_to_all(half, 'zh', 0, 0), axis=0)  16.4 us
    all_to_all x1, waiting for transfers between devices, on_device(): back = loss_scale * lax.all_to_all(slope, ens, 0, 0)  7.2 us
    dot_general x1, matrix products, on_device(): jnp.einsum('io,ip->op', w_first, features, preferred_element_type=f32)  6.97 us
    unnamed x21, local copies, waits for them, and re-layouts  6.97 us
    all_to_all x1, waiting for transfers between devices, on_device(): fields = lax.all_to_all(pieces, ens, 0, 0)  6.7 us
    concatenate x2, local copies, waits for them, and re-layouts, on_device(): jnp.concatenate([part_w1, part_w2, part_b1[:, None], misc, jnp.zeros((cha...  6.56 us
    all_to_all x1, starting transfers between devices, on_device(): fields = lax.all_to_all(pieces, ens, 0, 0)  5.96 us
  transfers between devices with their start and end apart: 4, of which 3 were waited for; matrix products, arithmetic and copies ran while one was open for 9% of the time, Pallas kernels for 0%

profile of v1, /device:TPU:2, one launch (start us, length us, event | category | flops | bytes accessed | tf_op | source)
XLA Modules:
  0.0 144.9 jit_solution(17921168048329329907)
XLA Ops:
  0.7 1.6 %copy-done = bf16[1,1024,1024]{2,1,0:T(8,128)(2,1)S(1)} copy-done((bf16[1,1024,1024]{2,1,0:T(8,128)(2,1)S(1)}, bf16[1,1024,1024]{2,1,0:T(8,128)(2,1)}, u32[]{:S(2)}) %copy-start) | copy-done | bytes 2097176
  2.2 7.0 %multiply_convert_fusion = (bf16[1024,1024]{1,0:T(8,128)(2,1)S(1)}, f32[1024,1024]{1,0:T(8,128)}) fusion(f32[1024]{0:T(1024)} %param.15, bf16[1024,1024]{1,0:T(8,128)(2,1)} %param.14, bf16[1,1024,1024]{2,1,0:T(8,128)(2,1)S(1)} %copy-done), kind=kOutput, calls=%fused_computation.17 | convolution fusion | flops 2157969408 | bytes 10489856 | tf_op jit(solution)/shard_map/io,ip->op/dot_general | solution.py:27
  9.2 1.3 copy-done.1
  11.1 0.8 copy.58
  11.9 6.0 %all-to-all-start = ((f32[8,100,128]{2,1,0:T(8,128)}), f32[8,100,128]{2,1,0:T(8,128)S(1)}, u32[]{:S(2)}, u32[]{:S(2)}) async-start(f32[8,100,128]{2,1,0:T(8,128)} %bitcast.70), calls=%async_computation | async-start | bytes 851968 | tf_op jit(solution)/shard_map/all_to_all | solution.py:34
  17.9 0.8 dynamic_slice.13
  19.0 1.0 broadcast_multiply_fusion
  19.9 6.7 %all-to-all-done = f32[8,100,128]{2,1,0:T(8,128)S(1)} async-done(((f32[8,100,128]{2,1,0:T(8,128)}), f32[8,100,128]{2,1,0:T(8,128)S(1)}, u32[]{:S(2)}, u32[]{:S(2)}) %all-to-all-start) | async-done | bytes 409632 | tf_op jit(solution)/shard_map/all_to_all | solution.py:34
  26.7 3.3 %fusion.12 = (f32[8,100,128]{2,1,0:T(8,128)S(1)}, f32[8,100,128]{2,1,0:T(8,128)S(1)}) fusion(f32[8,100,128]{2,0,1:T(8,128)S(1)} %copy.40, f32[8,100,128]{2,1,0:T(8,128)S(1)} %all-to-all-done), kind=kLoop, calls=%fused_computation.20 | loop fusion | flops 4710400 | bytes 1638400 | tf_op jit(solution)/shard_map/reduce_sum | solution.py:43
  30.0 1.7 %convert_reduce_fusion.1 = (f32[100]{0:T(128)S(1)}, f32[8,100,128]{2,1,0:T(8,128)}, f32[]{:T(128)}) fusion(f32[8,100,128]{2,1,0:T(8,128)S(1)} %get-tuple-element.31, f32[8,100,128]{2,1,0:T(8,128)S(1)} %all-to-all-done, f32[100,128]{1,0:T(8,128)S(1)} %get-tuple-element.42, f32[100,128]{1,0:T(8,128)S(1)} %get-tuple-element.41, ...), kind=kLoop, calls=%fused_computation.33 | loop fusion | flops 1740699 | bytes 1741204 | tf_op jit(solution)/shard_map/reduce_sum | solution.py:51
  31.7 3.6 %all-to-all-start.1 = ((f32[8,100,128]{2,1,0:T(8,128)}), f32[8,100,128]{2,1,0:T(8,128)S(1)}, u32[]{:S(2)}, u32[]{:S(2)}) async-start(f32[8,100,128]{2,1,0:T(8,128)} %get-tuple-element.33), calls=%async_computation.1 | async-start | bytes 851968 | tf_op jit(solution)/shard_map/all_to_all | solution.py:52
  35.4 0.7 pad_maximum_fusion
  36.3 7.2 %all-to-all-done.1 = f32[8,100,128]{2,1,0:T(8,128)S(1)} async-done(((f32[8,100,128]{2,1,0:T(8,128)}), f32[8,100,128]{2,1,0:T(8,128)S(1)}, u32[]{:S(2)}, u32[]{:S(2)}) %all-to-all-start.1) | async-done | bytes 409632 | tf_op jit(solution)/shard_map/all_to_all | solution.py:52
  43.8 5.3 %convert_reduce_fusion = (f32[1024]{0:T(1024)S(1)}, bf16[1024,1024]{1,0:T(8,128)(2,1)S(1)}) fusion(f32[1024,1024]{1,0:T(8,128)} %get-tuple-element.38, f32[1024]{0:T(1024)S(1)} %copy-done.6, bf16[100,1024]{1,0:T(8,128)(2,1)S(1)} %bitcast.83, bf16[1024,100]{0,1:T(8,128)(2,1)S(1)} %copy-done.2), kind=kOutput, calls=%fused_computation.16 | convolution fusion | flops 233831424 | bytes 6709248 | tf_op jit(solution)/shard_map/ov,vp->op/dot_general | solution.py:54
  49.1 4.4 %fusion.14 = f32[1024,1024]{0,1:T(8,128)} fusion(bf16[1024,1024]{1,0:T(8,128)(2,1)S(1)} %get-tuple-element.40, bf16[1,1024,1024]{2,1,0:T(8,128)(2,1)S(1)} %copy-done), kind=kOutput, calls=%fused_computation.24 | convolution fusion | flops 2147483648 | bytes 8388608 | tf_op jit(solution)/shard_map/ip,op->io/dot_general | solution.py:56
  53.8 3.1 %fusion.19 = f32[4,4,2,4,8,100]{5,4,3,2,1,0:T(8,128)} fusion(bf16[4,4,2,4,8,1024]{5,4,3,2,1,0:T(8,128)(2,1)} %bitcast.71, bf16[100,1024,1,1,1,1]{1,0,2,3,4,5:T(8,128)(2,1)S(1)} %reshape.93), kind=kOutput, calls=%fused_computation.40 | convolution fusion | flops 209715200 | bytes 2711552 | tf_op jit(solution)/shard_map/op,vp->ov/dot_general | solution.py:57
  57.0 0.9 broadcast_in_dim.9
  57.9 6.2 %concatenate.14 = f32[4,4,2,4,8,1152]{5,4,3,2,1,0:T(8,128)} concatenate(f32[4,4,2,4,8,1024]{5,4,3,2,1,0:T(8,128)} %bitcast.73, f32[4,4,2,4,8,100]{5,4,3,2,1,0:T(8,128)} %fusion.19, f32[4,4,2,4,8,1]{5,4,3,2,1,0:T(8,128)S(1)} %concatenate.15, f32[4,4,2,4,8,4]{5,4,3,2,1,0:T(8,128)S(1)} %tile.10, f32[4,4,2,4,8,23]{5,4,3,2,1,0:T(8,128)} %broadcast_in_dim.9), dimensions={5} | concatenate | bytes 9437184 | tf_op jit(solution)/shard_map/concatenate | solution.py:64
  64.1 2.7 %constant_dynamic-slice_fusion.1 = (f32[4,4,1,4,8,1152]{5,4,3,2,1,0:T(8,128)S(1)}, f32[4,4,1,4,8,1152]{5,4,3,2,1,0:T(8,128)S(1)}) fusion(f32[4,4,2,4,8,1152]{5,4,3,2,1,0:T(8,128)} %concatenate.14, s32[]{:T(128)S(6)} %select_n.12, s32[]{:T(128)S(6)} %select_n.13), kind=kLoop, calls=%fused_computation.50 | loop fusion | bytes 9437192 | tf_op jit(solution)/shard_map/jit(dynamic_index_in_dim)/dynamic_slice | solution.py:69
  67.2 4.5 %collective-permute-done = f32[4,4,4,8,1152]{4,3,1,0,2:T(8,128)S(1)} collective-permute-done((f32[4,4,4,8,1152]{4,3,1,0,2:T(8,128)S(1)}, f32[4,4,4,8,1152]{4,3,1,0,2:T(8,128)S(1)}, u32[]{:S(2)}, u32[]{:S(2)}) %collective-permute-start) | collective-permute-done | bytes 2359328 | tf_op jit(solution)/shard_map/ppermute | solution.py:71
  72.0 35.5 %all_to_all.25 = f32[16,4,8,1152]{3,2,1,0:T(8,128)} all-to-all(f32[16,4,8,1152]{3,2,1,0:T(8,128)S(1)} %bitcast.72), channel_id=1, replica_groups=mesh['zl'=2,'y'=4,'x'=4,'zh'=4,'c'=2] {'y','x'}, dimensions={0} | all-to-all | bytes 4718592 | tf_op jit(solution)/shard_map/all_to_all | solution.py:74
  107.5 1.8 %reduce_sum.77 = f32[4,8,1152]{2,1,0:T(8,128)S(1)} reduce(f32[16,4,8,1152]{3,2,1,0:T(8,128)} %all_to_all.25, f32[]{:T(128)} %constant.62.clone.1), dimensions={0}, to_apply=%region_5.6 | reduce | flops 552960 | bytes 2506756 | tf_op jit(solution)/shard_map/reduce_sum | solution.py:74
  109.3 16.4 %all_to_all.26 = f32[4,8,1152]{2,1,0:T(8,128)S(1)} all-to-all(f32[4,8,1152]{2,1,0:T(8,128)S(1)} %reduce_sum.77), channel_id=1, replica_groups=mesh['zl'=2,'y'=4,'x'=4,'zh'=4,'c'=2] {'zh'}, dimensions={0} | all-to-all | bytes 294912 | tf_op jit(solution)/shard_map/all_to_all | solution.py:75
  125.7 0.8 broadcast_in_dim.10
  126.5 3.4 %all-to-all-start.4 = ((f32[8,8,1152]{2,1,0:T(8,128)}), f32[8,8,1152]{2,1,0:T(8,128)S(1)}, u32[]{:S(2)}, u32[]{:S(2)}) async-start(f32[8,8,1152]{2,1,0:T(8,128)} %broadcast_in_dim.10), calls=%async_computation.4 | async-start | bytes 589824 | tf_op jit(solution)/shard_map/all_to_all | solution.py:76
  129.9 6.0 %convert_bitcast_fusion = bf16[1,1024,1024]{1,2,0:T(8,128)(2,1)} fusion(bf16[1024,1024]{1,0:T(8,128)(2,1)} %copy-done.7, bf16[1024,1024]{1,0:T(8,128)(2,1)} %param.14), kind=kOutput, calls=%fused_computation.28 | convolution fusion | flops 2148532224 | bytes 6291456 | tf_op jit(solution)/shard_map/io,op->ip/dot_general | solution.py:72
  135.9 3.9 %copy.48 = bf16[1,1024,1024]{2,1,0:T(8,128)(2,1)} copy(bf16[1,1024,1024]{1,2,0:T(8,128)(2,1)} %convert_bitcast_fusion) | data formatting | bytes 4194304
  139.8 0.7 slice_multiply_fusion
  140.7 0.6 slice.19
  141.3 0.5 slice_multiply_fusion.3
  141.8 0.6 slice_multiply_fusion.1
  142.5 0.7 fusion.22
  (39 shorter events, 2.7 us)
Async XLA Ops:
  0.6 1.6 %copy-start = (bf16[1,1024,1024]{2,1,0:T(8,128)(2,1)S(1)}, bf16[1,1024,1024]{2,1,0:T(8,128)(2,1)}, u32[]{:S(2)}) copy-start(bf16[1,1024,1024]{2,1,0:T(8,128)(2,1)} %param.9) | copy-start | bytes 6291460
  0.6 9.9 %copy-start.2 = (bf16[1024,100]{0,1:T(8,128)(2,1)S(1)}, bf16[1024,100]{0,1:T(8,128)(2,1)}, u32[]{:S(2)}) copy-start(bf16[1024,100]{0,1:T(8,128)(2,1)} %param.16) | copy-start | bytes 614404
  0.7 9.9 %copy-start.4 = (f32[100]{0:T(128)S(1)}, f32[100]{0:T(128)}, u32[]{:S(2)}) copy-start(f32[100]{0:T(128)} %param.17) | copy-start | bytes 1204
  9.2 1.3 copy-start.1
  9.2 8.7 %copy-start.3 = (f32[721]{0:T(1024)S(1)}, f32[721]{0:T(1024)}, u32[]{:S(2)}) copy-start(f32[721]{0:T(1024)} %param.12) | copy-start | bytes 8656
  9.2 9.8 %copy-start.5 = (f32[100]{0:T(128)S(1)}, f32[100]{0:T(128)}, u32[]{:S(2)}) copy-start(f32[100]{0:T(128)} %param.13) | copy-start | bytes 1204
  11.9 31.8 %copy-start.6 = (f32[1024]{0:T(1024)S(1)}, f32[1024]{0:T(1024)}, u32[]{:S(2)}) copy-start(f32[1024]{0:T(1024)} %param.15) | copy-start | bytes 12292
  11.9 14.7 %all-to-all-start = ((f32[8,100,128]{2,1,0:T(8,128)}), f32[8,100,128]{2,1,0:T(8,128)S(1)}, u32[]{:S(2)}, u32[]{:S(2)}) async-start(f32[8,100,128]{2,1,0:T(8,128)} %bitcast.70), calls=%async_computation | async-start | bytes 851968 | tf_op jit(solution)/shard_map/all_to_all | solution.py:34
  31.7 11.8 %all-to-all-start.1 = ((f32[8,100,128]{2,1,0:T(8,128)}), f32[8,100,128]{2,1,0:T(8,128)S(1)}, u32[]{:S(2)}, u32[]{:S(2)}) async-start(f32[8,100,128]{2,1,0:T(8,128)} %get-tuple-element.33), calls=%async_computation.1 | async-start | bytes 851968 | tf_op jit(solution)/shard_map/all_to_all | solution.py:52
  49.1 4.4 %copy-start.7 = (bf16[1024,1024]{1,0:T(8,128)(2,1)}, bf16[1024,1024]{1,0:T(8,128)(2,1)S(1)}, u32[]{:S(2)}) copy-start(bf16[1024,1024]{1,0:T(8,128)(2,1)S(1)} %get-tuple-element.40) | copy-start | bytes 6291460
  67.1 4.6 %collective-permute-start = (f32[4,4,4,8,1152]{4,3,1,0,2:T(8,128)S(1)}, f32[4,4,4,8,1152]{4,3,1,0,2:T(8,128)S(1)}, u32[]{:S(2)}, u32[]{:S(2)}) collective-permute-start(f32[4,4,4,8,1152]{4,3,1,0,2:T(8,128)S(1)} %bitcast.75), channel_id=1, source_target_pairs={{0,1},{1,0},{2,3},{3,2},{4,5},{5,4},{6,7},{7,6},{8,9},{9,8},{10,11... | collective-permute-start | bytes 7077896 | tf_op jit(solution)/shard_map/ppermute | solution.py:71
  126.5 13.3 %all-to-all-start.4 = ((f32[8,8,1152]{2,1,0:T(8,128)}), f32[8,8,1152]{2,1,0:T(8,128)S(1)}, u32[]{:S(2)}, u32[]{:S(2)}) async-start(f32[8,8,1152]{2,1,0:T(8,128)} %broadcast_in_dim.10), calls=%async_computation.4 | async-start | bytes 589824 | tf_op jit(solution)/shard_map/all_to_all | solution.py:76

commit v2 on v1

v2 whole, which is shorter than its diff:
```python
import functools
import math

import jax
import jax.numpy as jnp
from jax import lax
from jax.experimental import pallas as pl
from jax.experimental.pallas import tpu as pltpu
from jax.sharding import Mesh, PartitionSpec as P

smoothing = 0.0025
loss_scale = 64.0
ens = ("zl", "y")
space = ("x", "zh", "c")
plane = ("y", "x", "c")
lanes = 128
tile = 256
f32, bf16 = jnp.float32, jnp.bfloat16
root = math.sqrt(2.0 / math.pi)
cubic = 0.044715


def dot(a, b, contract):
    return lax.dot_general(a, b, (contract, ((), ())), preferred_element_type=f32)


hbm = pl.BlockSpec(memory_space=pltpu.HBM)
near = pl.BlockSpec(memory_space=pltpu.VMEM)


def call(kernel, out_shape, ins, outs, scratch=(), flops=0, limit=24):
    return pl.pallas_call(
        kernel,
        out_shape=out_shape,
        in_specs=ins,
        out_specs=outs,
        scratch_shapes=scratch,
        compiler_params=pltpu.CompilerParams(vmem_limit_bytes=limit * 2**20),
        cost_estimate=pl.CostEstimate(flops=flops, bytes_accessed=2**22, transcendentals=0),
    )


def columns_of(row, width):
    return jnp.transpose(jnp.broadcast_to(row, (width, row.shape[1])))


def arrive(pairs, sems):
    copies = [pltpu.make_async_copy(s, d, sems.at[i]) for i, (s, d) in enumerate(pairs)]
    for c in copies:
        c.start()
    return copies


def turn(w, wt):
    for j in range(0, w.shape[1], tile):
        wt[j : j + tile, :] = jnp.transpose(w[:, j : j + tile])


def forward_kernel(
    f_hbm, w_hbm, b1_hbm, w2_hbm, b2_hbm, x_ref, wt_hbm, f, w, b1, w2, b2, wt, sems, outs
):
    channels = w.shape[1]
    parts = [pl.ds(j, tile) for j in range(0, channels, tile)]
    copies = arrive(
        [(w_hbm.at[:, p], w.at[:, p]) for p in parts]
        + [(f_hbm, f), (b1_hbm, b1), (w2_hbm, w2), (b2_hbm, b2)],
        sems,
    )
    sent = []
    for j, p in enumerate(parts):
        copies[j].wait()
        wt[p, :] = jnp.transpose(w[:, p])
        c = pltpu.make_async_copy(wt.at[p, :], wt_hbm.at[p, :], outs.at[j])
        c.start()
        sent.append(c)
    for c in copies[len(parts) :]:
        c.wait()
    shift = columns_of(b1[...], lanes)
    bias = columns_of(b2[...], lanes)
    pre = dot(wt[...], f[...], ((1,), (0,))) + jnp.tile(shift, (1, f.shape[1] // lanes))
    t = jnp.tanh(pre * (root + (root * cubic) * (pre * pre)))
    z = (0.5 * pre * (1.0 + t)).astype(bf16)
    x = dot(w2[...], z, ((1,), (0,)))
    for m in range(x_ref.shape[0]):
        x_ref[m] = x[:, m * lanes : (m + 1) * lanes] + bias
    for c in sent:
        c.wait()


def again_kernel(x_hbm, f_hbm, wt_hbm, b1_hbm, z_hbm, g_hbm, f, wt, b1, z, g, sems, outs):
    points = f.shape[1]
    parts = [pl.ds(q, tile) for q in range(0, points, tile)]
    copies = arrive(
        [(b1_hbm, b1), (wt_hbm, wt)] + [(f_hbm.at[:, p], f.at[:, p]) for p in parts], sems
    )
    copies[0].wait()
    shift = jnp.tile(columns_of(b1[...], lanes), (1, tile // lanes))
    copies[1].wait()
    sent = []
    for k, here in enumerate(parts):
        copies[2 + k].wait()
        pre = dot(wt[...], f[:, here], ((1,), (0,))) + shift
        square = pre * pre
        t = jnp.tanh(pre * (root + (root * cubic) * square))
        z[:, here] = (0.5 * pre * (1.0 + t)).astype(bf16)
        inner = root + (3.0 * root * cubic) * square
        g[:, here] = (0.5 * ((1.0 + t) + (pre * inner) * (1.0 - t * t))).astype(bf16)
        for i, (s, d) in enumerate(((z, z_hbm), (g, g_hbm))):
            c = pltpu.make_async_copy(s.at[:, here], d.at[:, here], outs.at[k, i])
            c.start()
            sent.append(c)
    for c in sent:
        c.wait()


def pair_kernel(
    z_hbm, x_ref, goal_hbm, index_hbm, table_hbm, weight_hbm, dx_ref, misc_ref,
    col, goal_ref, index_ref, table_ref, weight_ref, sems,
):
    members, variables, slab = x_ref.shape
    me = lax.axis_index(ens)
    here = pl.ds(pl.multiple_of(me * slab, slab), slab)
    rows = table_ref.shape[1]
    copies = arrive(
        [
            (index_hbm, index_ref),
            (table_hbm, table_ref),
            (weight_hbm, weight_ref),
            (goal_hbm.at[:, here], goal_ref),
        ],
        sems,
    )
    fields = [x_ref[m] for m in range(members)]
    pull = [None] * members
    spread = None
    for a in range(members):
        for b in range(a + 1, members):
            d = fields[a] - fields[b]
            square = d * d + smoothing
            inverse = lax.rsqrt(square)
            spread = square * inverse if spread is None else spread + square * inverse
            term = d * inverse
            pull[a] = term if pull[a] is None else pull[a] + term
            pull[b] = -term if pull[b] is None else pull[b] - term
    spread = 2.0 * spread + members * math.sqrt(smoothing)
    for c in copies:
        c.wait()
    hot = lax.broadcasted_iota(jnp.int32, (rows, slab), 0) == index_ref[:, here]
    area = lax.dot_general(
        table_ref[...],
        hot.astype(f32),
        (((1,), (0,)), ((), ())),
        precision=lax.Precision.HIGHEST,
        preferred_element_type=f32,
    )
    coef = columns_of(weight_ref[...], slab) * area
    goal = goal_ref[...]
    pairs = members * (members - 1)
    skills = None
    total = None
    for m in range(members):
        miss = fields[m] - goal
        square = miss * miss + smoothing
        inverse = lax.rsqrt(square)
        skills = square * inverse if skills is None else skills + square * inverse
        slope = miss * inverse * (1.0 / members) - pull[m] * (1.0 / pairs)
        grad = (loss_scale * coef * slope).astype(bf16).astype(f32)
        dx_ref[m] = grad
        total = grad if total is None else total + grad
    crps = coef * (skills * (1.0 / members) - spread * (0.5 / pairs))
    col[...] = jnp.zeros_like(col)
    col[:variables, :] = jnp.broadcast_to(jnp.sum(total, axis=1, keepdims=True), (variables, lanes))
    loss = jnp.sum(jnp.sum(crps, axis=0, keepdims=True), axis=1, keepdims=True)
    col[variables : variables + 1, :] = jnp.broadcast_to(loss, (1, lanes))
    share = misc_ref.shape[0]
    lane = lax.broadcasted_iota(jnp.int32, (share, lanes), 1)
    out = jnp.zeros((share, lanes), f32)
    for g in range(lanes // share):
        out = jnp.where(lane == variables + 1 + g, col[g * share : (g + 1) * share, :], out)
    misc_ref[...] = out


def scatter_rows(first, put, nx, nzh, ny, rows):
    for y in range(ny):
        for zh in range(nzh):
            for x in range(nx):
                r = ((x * nzh + zh) * ny + y) * rows
                put(y, x, zh, first[r : r + rows])


def send_kernel(
    back_ref, w2_ref, misc_ref, g_hbm, z_hbm, f_hbm, dpre_ref, send_ref, keep_ref, dx, g, z, f, piece, sems
):
    members, variables, slab = back_ref.shape
    ny, nx, nzh, rows, _ = send_ref.shape
    channels, points = z.shape
    share = ny * rows
    core = lax.axis_index("c")
    steps = channels // tile
    copies = []
    for j in range(steps):
        here = pl.ds(j * tile, tile)
        copies += [(g_hbm.at[here, :], g.at[here, :]), (z_hbm.at[here, :], z.at[here, :])]
        if j == 0:
            copies.append((f_hbm.at[:, 1 - core], f))
    copies = arrive(copies, sems)
    dx[...] = jnp.zeros_like(dx)
    for m in range(members):
        dx[:variables, m * slab : (m + 1) * slab] = back_ref[m].astype(bf16)
    lane = lax.broadcasted_iota(jnp.int32, (tile, lanes), 1)
    extra = jnp.tile(misc_ref[...], (tile // share, 1))
    half = None
    for j in range(steps):
        here = slice(j * tile, (j + 1) * tile)
        w2j = jnp.transpose(w2_ref[:, here])
        copies[0 if j == 0 else 2 * j + 1].wait()
        dz = dot(w2j, dx[:variables, :], ((1,), (0,)))
        d = (dz * g[here, :].astype(f32)).astype(bf16)
        dpre_ref[here, :] = d
        sums = jnp.sum(d.astype(f32), axis=1, keepdims=True)
        copies[1 if j == 0 else 2 * j + 2].wait()
        second = dot(z[here, :], dx[...], ((1,), (1,)))
        second = jnp.where(lane == variables, sums, second + extra)
        piece[...] = second.reshape(nzh, 2, share, lanes)
        go, stay = piece[:, 1 - core], piece[:, core]
        if j == 0:
            copies[2].wait()
            half = f[...].reshape(f.shape[0] * share, points)
        first = dot(half, d, ((1,), (1,)))
        for y in range(ny):
            for zh in range(nzh):
                send_ref[y, j, zh, :, channels:] = go[zh, y * rows : (y + 1) * rows]
                keep_ref[y, j, zh] = stay[zh, y * rows : (y + 1) * rows]

        def put(y, x, zh, value):
            send_ref[y, x, zh, :, here] = value

        scatter_rows(first, put, nx, nzh, ny, rows)


def window_kernel(d_ref, w_hbm, f_hbm, own_ref, grad_hbm, w, f, grad, sems, outs):
    ny, nx, nzh, rows, channels = own_ref.shape
    points = d_ref.shape[1]
    share = ny * rows
    core = lax.axis_index("c")
    copies = arrive([(f_hbm.at[:, core], f), (w_hbm, w)], sems)
    copies[0].wait()
    half = f[...].reshape(f.shape[0] * share, points)
    first = dot(half, d_ref[...], ((1,), (1,)))

    def put(y, x, zh, value):
        own_ref[y, x, zh] = value

    scatter_rows(first, put, nx, nzh, ny, rows)
    copies[1].wait()
    sent = []
    side = channels // 2
    for k in range(2):
        here = pl.ds(k * side, side)
        grad[here, :] = dot(w[here, :], d_ref[...], ((1,), (0,))).astype(bf16)
        c = pltpu.make_async_copy(grad.at[here, :], grad_hbm.at[here, :], outs.at[k])
        c.start()
        sent.append(c)
    for c in sent:
        c.wait()


def add_kernel(own_ref, keep_ref, other_ref, out_ref):
    ny, nx, nzh, rows, channels = own_ref.shape
    core = lax.axis_index("c")
    for y in range(ny):
        for x in range(nx):
            a = jnp.where(core == 0, y, x)
            b = jnp.where(core == 0, x, y)
            for zh in range(nzh):
                here = pl.ds(zh * rows, rows)
                out_ref[a, b, here, :channels] = (
                    own_ref[y, x, zh] + other_ref[y, x, zh, :, :channels]
                )
                out_ref[a, b, here, channels:] = (
                    keep_ref[y, x, zh] + other_ref[y, x, zh, :, channels:]
                )


def deal_kernel(axes, in_ref, *out_refs):
    core = lax.axis_index("c")
    me = jnp.where(core == 0, lax.axis_index(axes[0]), lax.axis_index(axes[1]))
    n = len(out_refs)
    for d in range(n):
        k = lax.rem(me + d, n)
        total = in_ref[0, k]
        for i in range(1, in_ref.shape[0]):
            total = total + in_ref[i, k]
        out_refs[d][...] = total


def redeal_kernel(axis, *refs):
    n = len(refs) // 2
    me = lax.axis_index(axis)
    rows = refs[n].shape[0]
    for d in range(n):
        here = pl.ds(pl.multiple_of(lax.rem(me + d, n) * rows, rows), rows)
        total = refs[0][here, :]
        for i in range(1, n):
            total = total + refs[i][here, :]
        refs[n + d][...] = total


def spread_kernel(*refs):
    out_ref = refs[-1]
    total = refs[0][...]
    for r in refs[1:-1]:
        total = total + r[...]
    for i in range(out_ref.shape[0]):
        out_ref[i] = total


def finish_kernel(factor, points, in_ref, w1_ref, b1_ref, w2_ref, b2_ref, loss_ref, part):
    ny = in_ref.shape[0] // 2
    rows = in_ref.shape[1]
    share, channels = w1_ref.shape
    variables = w2_ref.shape[1]
    part[...] = jnp.zeros_like(part)
    for y in range(ny):
        here = slice(y * rows, (y + 1) * rows)
        w1_ref[here, :] = (in_ref[y, :, :channels] + in_ref[ny + y, :, :channels]) * factor
        part[here, :] = in_ref[y, :, channels:] + in_ref[ny + y, :, channels:]
    w2_ref[...] = part[:share, :variables] * factor
    turned = jnp.transpose(part[...])
    b1_ref[...] = turned[variables : variables + 1, :share] * factor
    line = turned[variables + 1 : variables + 2, :]
    for g in range(1, lanes // share):
        line = line + pltpu.roll(turned[variables + 1 + g : variables + 2 + g, :], g * share, 1)
    b2_ref[...] = line[:, :variables] * factor
    loss_ref[...] = line[:, variables : variables + 1] * (1.0 / points)


def lines(ny, nx):
    at = lambda y, x, c: (y * nx + x) * 2 + c
    down = [[at(y, x, 0) for y in range(ny)] for x in range(nx)]
    along = [[at(y, x, 1) for x in range(nx)] for y in range(ny)]
    return down + along


def shifts(ny, nx, d):
    at = lambda y, x, c: (y * nx + x) * 2 + c
    pairs = [(at(y, x, 0), at(y, (x + d) % nx, 0)) for y in range(ny) for x in range(nx)]
    return pairs + [(at(y, x, 1), at((y + d) % ny, x, 1)) for y in range(ny) for x in range(nx)]


def on_device(
    hidden, target, area_index, area_table, var_weight, w_first, b_first, w_second, b_second
):
    members = lax.axis_size(ens)
    columns = hidden.shape[2]
    variables = target.shape[0]
    channels = w_first.shape[0]
    slab = columns // members
    nx, nzh, nc, ny = (lax.axis_size(a) for a in ("x", "zh", "c", "y"))
    share = channels // (nx * nzh * nc)
    rows = share // ny
    wide = channels + lanes
    shape = jax.ShapeDtypeStruct
    features = hidden[0]
    grouped = features.reshape(nx * nzh, nc, share, columns)
    w2t = w_second.T
    square = (channels, columns)
    dma = pltpu.SemaphoreType.DMA
    mine, wt = call(
        forward_kernel,
        (shape((members, variables, slab), f32), shape((channels, channels), bf16)),
        [hbm] * 5,
        (near, hbm),
        scratch=[
            pltpu.VMEM(square, bf16),
            pltpu.VMEM((channels, channels), bf16),
            pltpu.VMEM((1, channels), f32),
            pltpu.VMEM((variables, channels), bf16),
            pltpu.VMEM((1, variables), f32),
            pltpu.VMEM((channels, channels), bf16),
            dma((8,)),
            dma((4,)),
        ],
        flops=2 * channels * channels * columns,
        limit=60,
    )(features, w_first, b_first[None], w2t, b_second[None])
    fields = lax.all_to_all(mine, ens, 0, 0)
    z, g = call(
        again_kernel,
        (shape(square, bf16), shape(square, bf16)),
        [pl.BlockSpec(memory_space=pl.ANY)] + [hbm] * 3,
        (hbm, hbm),
        scratch=[
            pltpu.VMEM(square, bf16),
            pltpu.VMEM((channels, channels), bf16),
            pltpu.VMEM((1, channels), f32),
            pltpu.VMEM(square, bf16),
            pltpu.VMEM(square, bf16),
            dma((6,)),
            dma((4, 2)),
        ],
        flops=2 * channels * channels * columns,
        limit=60,
    )(mine, features, wt, b_first[None])
    dx, misc = call(
        pair_kernel,
        (shape((members, variables, slab), f32), shape((share, lanes), f32)),
        [pl.BlockSpec(memory_space=pl.ANY), near] + [hbm] * 4,
        (near, near),
        scratch=[
            pltpu.VMEM((lanes, lanes), f32),
            pltpu.VMEM((variables, slab), f32),
            pltpu.VMEM((1, columns), jnp.int32),
            pltpu.VMEM((1, area_table.shape[0]), f32),
            pltpu.VMEM((1, variables), f32),
            dma((4,)),
        ],
        limit=60,
    )(z, fields, target, area_index[None], area_table[None], var_weight[None])
    back = lax.all_to_all(dx, ens, 0, 0)
    part = (ny, nx, nzh, rows)
    dpre, send, keep = call(
        send_kernel,
        (shape(square, bf16), shape(part + (wide,), f32), shape(part + (lanes,), f32)),
        [near] * 3 + [hbm] * 3,
        (near, near, near),
        scratch=[
            pltpu.VMEM((lanes, columns), bf16),
            pltpu.VMEM(square, bf16),
            pltpu.VMEM(square, bf16),
            pltpu.VMEM((nx * nzh, share, columns), bf16),
            pltpu.VMEM((nzh, nc, share, lanes), f32),
            dma((9,)),
        ],
        flops=channels * channels * columns,
        limit=24,
    )(back, w2t, misc, g, z, grouped)
    other = lax.ppermute(send, "c", [(0, 1), (1, 0)])
    own, grad_feat = call(
        window_kernel,
        (shape(part + (channels,), f32), shape(square, bf16)),
        [near, hbm, hbm],
        (near, hbm),
        scratch=[
            pltpu.VMEM((channels, channels), bf16),
            pltpu.VMEM((nx * nzh, share, columns), bf16),
            pltpu.VMEM(square, bf16),
            dma((2,)),
            dma((2,)),
        ],
        flops=3 * channels * channels * columns,
        limit=24,
    )(dpre, w_first, grouped)
    half = call(
        add_kernel, shape((ny, nx, nzh * rows, wide), f32), [near] * 3, near
    )(own, keep, other)
    half = lax.all_to_all(half, plane, 0, 0, axis_index_groups=lines(ny, nx))
    blocks = call(
        functools.partial(deal_kernel, ("x", "y")),
        (shape((nzh * rows, wide), f32),) * nx,
        [near],
        (near,) * nx,
    )(half)
    blocks = (blocks[0],) + tuple(
        lax.ppermute(blocks[d], plane, shifts(ny, nx, d)) for d in range(1, nx)
    )
    blocks = call(
        functools.partial(redeal_kernel, "zh"),
        (shape((rows, wide), f32),) * nzh,
        [near] * nx,
        (near,) * nzh,
    )(*blocks)
    blocks = (blocks[0],) + tuple(
        lax.ppermute(blocks[d], "zh", [(i, (i + d) % nzh) for i in range(nzh)])
        for d in range(1, nzh)
    )
    whole = call(spread_kernel, shape((members, rows, wide), f32), [near] * nzh, near)(*blocks)
    whole = lax.all_to_all(whole, ens, 0, 0)
    total_points = columns * lax.axis_size(space)
    factor = 1.0 / math.sqrt(members * total_points)
    w1, b1, w2, b2, loss = call(
        functools.partial(finish_kernel, factor, total_points),
        (
            shape((share, channels), f32),
            shape((1, share), f32),
            shape((share, variables), f32),
            shape((1, variables), f32),
            shape((1, 1), f32),
        ),
        [near],
        (near,) * 5,
        scratch=[pltpu.VMEM((lanes, lanes), f32)],
    )(whole)
    return (loss[0, 0], grad_feat[None], w1, b1[0], w2, b2[0])


def solution(mesh):
    fine = Mesh(mesh.devices.reshape(2, 4, 4, 4, 2), ("zl", "y", "x", "zh", "c"))
    in_specs = (P(ens, None, space), P(None, space), P(space), P(), P(), P(), P(), P(), P())
    out_specs = (P(), P(ens, None, space), P(space, None), P(space), P(space, None), P())
    return jax.shard_map(
        on_device, mesh=fine, in_specs=in_specs, out_specs=out_specs, check_vma=False
    )
```

time: 147 us -> 110 us (0.75); the launches traced: 145 us -> 110 us
  Pallas kernels: 0 us -> 30.5 us
  matrix products: 26.5 us -> 0 us
  local copies, waits for them, and re-layouts: 21 us -> 5.25 us
  other arithmetic: 11.3 us -> 0 us
  waiting for transfers between devices: 18.4 us -> 7.25 us
  starting transfers between devices: 13.1 us -> 21.3 us
  blocking collectives: 51.9 us -> 44.6 us
  between operations: 2.64 us -> 0.77 us
    pallas_call x0 -> x10, Pallas kernels: none -> 30.5 us  [the longest x1 9.19 us: on_device(): call(again_kernel, (shape(square, bf16), shape(square, bf16)), [pl.BlockS...]
    dot_general x7 -> x0, matrix products: 26.5 us -> none  [the longest x1 6.97 us: on_device(): jnp.einsum('io,ip->op', w_first, features, preferred_element_type=f32)]
    ppermute x0 -> x6, starting transfers between devices: none -> 15.3 us  [the longest x3 10.5 us: on_device(): lax.ppermute(blocks[d], 'zh', [(i, (i + d) % nzh) for i in range(nzh)])]
    all_to_all x3 -> x1, waiting for transfers between devices: 13.9 us -> 0.01 us  [on_device(): fields = lax.all_to_all(mine, ens, 0, 0)]
    all_to_all x2 -> x3, blocking collectives: 51.9 us -> 44.6 us  [the longest x1 20.4 us: on_device(): half = lax.all_to_all(half, plane, 0, 0, axis_index_groups=lines(ny, nx))]
    ppermute x0 -> x6, waiting for transfers between devices: none -> 7.25 us  [the longest x3 4.57 us: on_device(): lax.ppermute(blocks[d], plane, shifts(ny, nx, d))]
    all_to_all x3 -> x1, starting transfers between devices: 13 us -> 5.84 us  [on_device(): fields = lax.all_to_all(mine, ens, 0, 0)]
    reduce_sum x5 -> x0, other arithmetic: 6.81 us -> none  [the longest x1 3.31 us: on_device(): spread = jnp.sum(radius, axis=1)]
  transfers between devices with their start and end apart: 4 -> 8, of which waited for: 3 -> 5; matrix products, arithmetic and copies ran while one was open for 9% -> 1% of each run, Pallas kernels for 0% -> 13%
where the time goes in v2:
time: 110 us
  blocking collectives  44.6 us (41%)
  Pallas kernels  30.5 us (28%)
  starting transfers between devices  21.3 us (19%)
  waiting for transfers between devices  7.25 us (7%)
  local copies, waits for them, and re-layouts  5.25 us (5%)
    all_to_all x1, blocking collectives, on_device(): half = lax.all_to_all(half, plane, 0, 0, axis_index_groups=lines(ny, nx))  20.4 us
    all_to_all x1, blocking collectives, on_device(): back = lax.all_to_all(dx, ens, 0, 0)  14.2 us
    ppermute x3, starting transfers between devices, on_device(): lax.ppermute(blocks[d], 'zh', [(i, (i + d) % nzh) for i in range(nzh)])  10.5 us
    all_to_all x1, blocking collectives, on_device(): whole = lax.all_to_all(whole, ens, 0, 0)  10 us
    pallas_call x1, Pallas kernels, on_device(): call(again_kernel, (shape(square, bf16), shape(square, bf16)), [pl.BlockS...  9.19 us
    pallas_call x1, Pallas kernels, on_device(): call(forward_kernel, (shape((members, variables, slab), f32), shape((chan...  6.44 us
    all_to_all x1, starting transfers between devices, on_device(): fields = lax.all_to_all(mine, ens, 0, 0)  5.84 us
    pallas_call x1, Pallas kernels, on_device(): call(send_kernel, (shape(square, bf16), shape(part + (wide,), f32), shape...  5.61 us
  transfers between devices with their start and end apart: 8, of which 5 were waited for; matrix products, arithmetic and copies ran while one was open for 1% of the time, Pallas kernels for 13%

profile of v2, /device:TPU:2, one launch (start us, length us, event | category | flops | bytes accessed | tf_op | source)
XLA Modules:
  0.0 109.7 jit_solution(17002487723705415445)
XLA Ops:
  0.6 6.4 %shard_map.136 = (f32[8,100,128]{2,1,0:T(8,128)}, bf16[1024,1024]{1,0:T(8,128)(2,1)}) custom-call(bf16[1024,1024]{1,0:T(8,128)(2,1)} %bitcast.11, bf16[1024,1024]{1,0:T(8,128)(2,1)} %w_hbm.3, f32[1,1024]{1,0:T(1,128)} %bitcast.19, bf16[100,1024]{1,0:T(8,128)(2,1)} %bitcast.15, f32[1,100]{1,0:T(1,128)} %bitcast.21), custom_call_target="tpu_custom_call" | custom-call | flops 2147483648 | bytes 4194304 | tf_op jit(solution)/shard_map/pallas_call | solution.py:369
  7.1 5.8 %all-to-all-start = ((f32[8,100,128]{2,1,0:T(8,128)}), f32[8,100,128]{2,1,0:T(8,128)S(1)}, u32[]{:S(2)}, u32[]{:S(2)}) async-start(f32[8,100,128]{2,1,0:T(8,128)} %get-tuple-element.30.x_hbm), calls=%async_computation | async-start | bytes 851968 | tf_op jit(solution)/shard_map/all_to_all | solution.py:387
  12.9 0.6 broadcast_in_dim.22.table_hbm
  13.5 9.2 %shard_map.137 = (bf16[1024,1024]{1,0:T(8,128)(2,1)}, bf16[1024,1024]{1,0:T(8,128)(2,1)}) custom-call(f32[8,100,128]{2,1,0:T(8,128)} %get-tuple-element.30.x_hbm, bf16[1024,1024]{1,0:T(8,128)(2,1)} %bitcast.12, bf16[1024,1024]{1,0:T(8,128)(2,1)} %get-tuple-element.31.wt_hbm, f32[1,1024]{1,0:T(1,128)} %bitcast.20), custom_call_target="tpu_custom_call" | custom-call | flops 2147483648 | bytes 4194304 | tf_op jit(solution)/shard_map/pallas_call | solution.py:388
  22.7 0.0 copy-start.3
  22.7 0.0 all-to-all-done.x_ref
  22.7 0.0 copy-start.6
  22.8 0.7 copy-done.6
  23.5 3.2 %shard_map.138 = (f32[8,100,128]{2,1,0:T(8,128)}, f32[32,128]{1,0:T(8,128)}) custom-call(bf16[1024,1024]{1,0:T(8,128)(2,1)} %get-tuple-element.32.z_hbm, f32[8,100,128]{2,1,0:T(8,128)} %copy-done.6, f32[100,1024]{1,0:T(8,128)} %goal_hbm.1, s32[1,1024]{1,0:T(1,128)} %bitcast.17, f32[1,721]{1,0:T(1,128)} %broadcast_in_dim.22.table_hbm, f32[1,100]{1,0:T(1,128)} %bitcast.18), custom_call_target="tpu_custom_call" | custom-call | bytes 4194304 | tf_op jit(solution)/shard_map/pallas_call | solution.py:405
  26.7 14.2 %all_to_all.20.back_ref = f32[8,100,128]{2,1,0:T(8,128)S(1)} all-to-all(f32[8,100,128]{2,1,0:T(8,128)} %get-tuple-element.33), channel_id=1, replica_groups=mesh['zl'=2,'y'=4,'x'=4,'zh'=4,'c'=2] {'zl','y'}, dimensions={0} | all-to-all | bytes 819200 | tf_op jit(solution)/shard_map/all_to_all | solution.py:420
  40.9 1.6 %copy-done.1 = bf16[1,1024,1024]{2,1,0:T(8,128)(2,1)S(1)} copy-done((bf16[1,1024,1024]{2,1,0:T(8,128)(2,1)S(1)}, bf16[1,1024,1024]{2,1,0:T(8,128)(2,1)}, u32[]{:S(2)}) %copy-start.1) | copy-done | bytes 2097176
  42.5 1.6 %copy-done.2 = bf16[1024,1024]{1,0:T(8,128)(2,1)S(1)} copy-done((bf16[1024,1024]{1,0:T(8,128)(2,1)S(1)}, bf16[1024,1024]{1,0:T(8,128)(2,1)}, u32[]{:S(2)}) %copy-start.2) | copy-done | bytes 2097176
  44.1 0.7 copy-done.4
  44.8 5.6 %shard_map.139 = (bf16[1024,1024]{1,0:T(8,128)(2,1)S(1)}, f32[4,4,4,8,1152]{4,3,2,1,0:T(8,128)S(1)}, f32[4,4,4,8,128]{4,3,2,1,0:T(8,128)S(1)}) custom-call(f32[8,100,128]{2,1,0:T(8,128)S(1)} %all_to_all.20.back_ref, bf16[100,1024]{1,0:T(8,128)(2,1)S(1)} %bitcast.16, f32[32,128]{1,0:T(8,128)S(1)} %copy-done.4, bf16[1024,1024]{1,0:T(8,128)(2,1)S(1)} %copy-done.2, ...), custom_call_target="tpu_custom_call" | custom-call | flops 1073741824 | bytes 4194304 | tf_op jit(solution)/shard_map/pallas_call | solution.py:422
  50.4 0.1 collective-permute-start
  50.5 4.8 %shard_map.140 = (f32[4,4,4,8,1024]{4,3,2,1,0:T(8,128)S(1)}, bf16[1024,1024]{1,0:T(8,128)(2,1)}) custom-call(bf16[1024,1024]{1,0:T(8,128)(2,1)S(1)} %get-tuple-element.36.d_ref, bf16[1024,1024]{1,0:T(8,128)(2,1)S(1)} %copy-done.5, bf16[16,2,32,1024]{3,2,1,0:T(8,128)(2,1)S(1)} %bitcast.14), custom_call_target="tpu_custom_call" | custom-call | flops 3221225472 | bytes 4194304 | tf_op jit(solution)/shard_map/pallas_call | solution.py:439
  55.4 0.2 shard_map.141
  55.6 20.4 %all_to_all.21.in_ref = f32[4,4,32,1152]{3,2,1,0:T(8,128)S(1)} all-to-all(f32[4,4,32,1152]{3,2,1,0:T(8,128)S(1)} %shard_map.141), channel_id=1, replica_groups={{0,32,64,96},{8,40,72,104},{16,48,80,112},{24,56,88,120},{1,9,17,25},{3..., dimensions={0} | all-to-all | bytes 4718592 | tf_op jit(solution)/shard_map/all_to_all | solution.py:457
  76.0 0.1 shard_map.142
  76.1 1.6 %collective-permute-start.1 = (f32[32,1152]{1,0:T(8,128)S(1)}, f32[32,1152]{1,0:T(8,128)S(1)}, u32[]{:S(2)}, u32[]{:S(2)}) collective-permute-start(f32[32,1152]{1,0:T(8,128)S(1)} %get-tuple-element.41), channel_id=1, source_target_pairs={{0,8},{8,16},{16,24},{24,0},{32,40},{40,48},{48,56},{56,32},{64,72... | collective-permute-start | bytes 442376 | tf_op jit(solution)/shard_map/ppermute | solution.py:465
  77.7 1.1 %collective-permute-start.2 = (f32[32,1152]{1,0:T(8,128)S(1)}, f32[32,1152]{1,0:T(8,128)S(1)}, u32[]{:S(2)}, u32[]{:S(2)}) collective-permute-start(f32[32,1152]{1,0:T(8,128)S(1)} %get-tuple-element.42), channel_id=1, source_target_pairs={{0,16},{8,24},{16,0},{24,8},{32,48},{40,56},{48,32},{56,40},{64,80... | collective-permute-start | bytes 442376 | tf_op jit(solution)/shard_map/ppermute | solution.py:465
  78.8 2.2 %collective-permute-start.3 = (f32[32,1152]{1,0:T(8,128)S(1)}, f32[32,1152]{1,0:T(8,128)S(1)}, u32[]{:S(2)}, u32[]{:S(2)}) collective-permute-start(f32[32,1152]{1,0:T(8,128)S(1)} %get-tuple-element.43), channel_id=1, source_target_pairs={{0,24},{8,0},{16,8},{24,16},{32,56},{40,32},{48,40},{56,48},{64,88... | collective-permute-start | bytes 442376 | tf_op jit(solution)/shard_map/ppermute | solution.py:465
  80.9 0.4 collective-permute-done.1.refs_1_
  81.3 3.1 %collective-permute-done.2.refs_2_ = f32[32,1152]{1,0:T(8,128)S(1)} collective-permute-done((f32[32,1152]{1,0:T(8,128)S(1)}, f32[32,1152]{1,0:T(8,128)S(1)}, u32[]{:S(2)}, u32[]{:S(2)}) %collective-permute-start.2) | collective-permute-done | bytes 147488 | tf_op jit(solution)/shard_map/ppermute | solution.py:465
  84.4 1.1 collective-permute-done.3.refs_3_
  85.6 3.3 %collective-permute-start.4 = (f32[8,1152]{1,0:T(8,128)S(1)}, f32[8,1152]{1,0:T(8,128)S(1)}, u32[]{:S(2)}, u32[]{:S(2)}) collective-permute-start(f32[8,1152]{1,0:T(8,128)S(1)} %get-tuple-element.45), channel_id=1, source_target_pairs={{0,2},{2,4},{4,6},{6,0},{1,3},{3,5},{5,7},{7,1},{8,10},{10,12},{12... | collective-permute-start | bytes 110600 | tf_op jit(solution)/shard_map/ppermute | solution.py:474
  88.9 4.5 %collective-permute-start.5 = (f32[8,1152]{1,0:T(8,128)S(1)}, f32[8,1152]{1,0:T(8,128)S(1)}, u32[]{:S(2)}, u32[]{:S(2)}) collective-permute-start(f32[8,1152]{1,0:T(8,128)S(1)} %get-tuple-element.46), channel_id=1, source_target_pairs={{0,4},{2,6},{4,0},{6,2},{1,5},{3,7},{5,1},{7,3},{8,12},{10,14},{12... | collective-permute-start | bytes 110600 | tf_op jit(solution)/shard_map/ppermute | solution.py:474
  93.4 2.7 %collective-permute-start.6 = (f32[8,1152]{1,0:T(8,128)S(1)}, f32[8,1152]{1,0:T(8,128)S(1)}, u32[]{:S(2)}, u32[]{:S(2)}) collective-permute-start(f32[8,1152]{1,0:T(8,128)S(1)} %get-tuple-element.47), channel_id=1, source_target_pairs={{0,6},{2,0},{4,2},{6,4},{1,7},{3,1},{5,3},{7,5},{8,14},{10,8},{12,... | collective-permute-start | bytes 110600 | tf_op jit(solution)/shard_map/ppermute | solution.py:474
  96.1 0.9 collective-permute-done.5.refs_2_
  97.0 1.8 %collective-permute-done.6.refs_3_ = f32[8,1152]{1,0:T(8,128)S(1)} collective-permute-done((f32[8,1152]{1,0:T(8,128)S(1)}, f32[8,1152]{1,0:T(8,128)S(1)}, u32[]{:S(2)}, u32[]{:S(2)}) %collective-permute-start.6) | collective-permute-done | bytes 36896 | tf_op jit(solution)/shard_map/ppermute | solution.py:474
  98.8 10.0 %all_to_all.22.in_ref = f32[8,8,1152]{2,1,0:T(8,128)S(1)} all-to-all(f32[8,8,1152]{2,1,0:T(8,128)S(1)} %shard_map.144), channel_id=1, replica_groups=mesh['zl'=2,'y'=4,'x'=4,'zh'=4,'c'=2] {'zl','y'}, dimensions={0} | all-to-all | bytes 589824 | tf_op jit(solution)/shard_map/all_to_all | solution.py:478
  108.8 0.8 shard_map.145
  (14 shorter events, 0.1 us)
Async XLA Ops:
  0.6 12.3 %copy-start.7 = (f32[721]{0:T(1024)S(1)}, f32[721]{0:T(1024)}, u32[]{:S(2)}) copy-start(f32[721]{0:T(1024)} %param.12) | copy-start | bytes 8656
  7.1 15.7 %all-to-all-start = ((f32[8,100,128]{2,1,0:T(8,128)}), f32[8,100,128]{2,1,0:T(8,128)S(1)}, u32[]{:S(2)}, u32[]{:S(2)}) async-start(f32[8,100,128]{2,1,0:T(8,128)} %get-tuple-element.30.x_hbm), calls=%async_computation | async-start | bytes 851968 | tf_op jit(solution)/shard_map/all_to_all | solution.py:387
  22.7 18.1 %copy-start = (bf16[1024,1024]{1,0:T(8,128)(2,1)S(1)}, bf16[1024,1024]{1,0:T(8,128)(2,1)}, u32[]{:S(2)}) copy-start(bf16[1024,1024]{1,0:T(8,128)(2,1)} %get-tuple-element.32.z_hbm) | copy-start | bytes 6291460
  22.7 18.1 %copy-start.3 = (bf16[1024,100]{0,1:T(8,128)(2,1)S(1)}, bf16[1024,100]{0,1:T(8,128)(2,1)}, u32[]{:S(2)}) copy-start(bf16[1024,100]{0,1:T(8,128)(2,1)} %param.16) | copy-start | bytes 614404
  22.7 0.8 copy-start.6
  40.9 1.6 %copy-start.1 = (bf16[1,1024,1024]{2,1,0:T(8,128)(2,1)S(1)}, bf16[1,1024,1024]{2,1,0:T(8,128)(2,1)}, u32[]{:S(2)}) copy-start(bf16[1,1024,1024]{2,1,0:T(8,128)(2,1)} %param.9) | copy-start | bytes 6291460
  42.5 1.6 %copy-start.2 = (bf16[1024,1024]{1,0:T(8,128)(2,1)S(1)}, bf16[1024,1024]{1,0:T(8,128)(2,1)}, u32[]{:S(2)}) copy-start(bf16[1024,1024]{1,0:T(8,128)(2,1)} %get-tuple-element.35.g_hbm) | copy-start | bytes 6291460
  44.1 0.7 copy-start.4
  44.8 5.7 %copy-start.5 = (bf16[1024,1024]{1,0:T(8,128)(2,1)S(1)}, bf16[1024,1024]{1,0:T(8,128)(2,1)}, u32[]{:S(2)}) copy-start(bf16[1024,1024]{1,0:T(8,128)(2,1)} %w_hbm.3) | copy-start | bytes 6291460
  50.4 5.0 %collective-permute-start = (f32[4,4,4,8,1152]{4,3,2,1,0:T(8,128)S(1)}, f32[4,4,4,8,1152]{4,3,2,1,0:T(8,128)S(1)}, u32[]{:S(2)}, u32[]{:S(2)}) collective-permute-start(f32[4,4,4,8,1152]{4,3,2,1,0:T(8,128)S(1)} %get-tuple-element.39), channel_id=1, source_target_pairs={{0,1},{1,0},{2,3},{3,2},{4,5},{5,4},{6,7},{7,6},{8,9},{9,8},{10,11... | collective-permute-start | bytes 7077896 | tf_op jit(solution)/shard_map/ppermute | solution.py:438
  76.1 5.2 %collective-permute-start.1 = (f32[32,1152]{1,0:T(8,128)S(1)}, f32[32,1152]{1,0:T(8,128)S(1)}, u32[]{:S(2)}, u32[]{:S(2)}) collective-permute-start(f32[32,1152]{1,0:T(8,128)S(1)} %get-tuple-element.41), channel_id=1, source_target_pairs={{0,8},{8,16},{16,24},{24,0},{32,40},{40,48},{48,56},{56,32},{64,72... | collective-permute-start | bytes 442376 | tf_op jit(solution)/shard_map/ppermute | solution.py:465
  77.7 6.8 %collective-permute-start.2 = (f32[32,1152]{1,0:T(8,128)S(1)}, f32[32,1152]{1,0:T(8,128)S(1)}, u32[]{:S(2)}, u32[]{:S(2)}) collective-permute-start(f32[32,1152]{1,0:T(8,128)S(1)} %get-tuple-element.42), channel_id=1, source_target_pairs={{0,16},{8,24},{16,0},{24,8},{32,48},{40,56},{48,32},{56,40},{64,80... | collective-permute-start | bytes 442376 | tf_op jit(solution)/shard_map/ppermute | solution.py:465
  78.8 6.7 %collective-permute-start.3 = (f32[32,1152]{1,0:T(8,128)S(1)}, f32[32,1152]{1,0:T(8,128)S(1)}, u32[]{:S(2)}, u32[]{:S(2)}) collective-permute-start(f32[32,1152]{1,0:T(8,128)S(1)} %get-tuple-element.43), channel_id=1, source_target_pairs={{0,24},{8,0},{16,8},{24,16},{32,56},{40,32},{48,40},{56,48},{64,88... | collective-permute-start | bytes 442376 | tf_op jit(solution)/shard_map/ppermute | solution.py:465
  85.6 10.5 %collective-permute-start.4 = (f32[8,1152]{1,0:T(8,128)S(1)}, f32[8,1152]{1,0:T(8,128)S(1)}, u32[]{:S(2)}, u32[]{:S(2)}) collective-permute-start(f32[8,1152]{1,0:T(8,128)S(1)} %get-tuple-element.45), channel_id=1, source_target_pairs={{0,2},{2,4},{4,6},{6,0},{1,3},{3,5},{5,7},{7,1},{8,10},{10,12},{12... | collective-permute-start | bytes 110600 | tf_op jit(solution)/shard_map/ppermute | solution.py:474
  88.9 8.1 %collective-permute-start.5 = (f32[8,1152]{1,0:T(8,128)S(1)}, f32[8,1152]{1,0:T(8,128)S(1)}, u32[]{:S(2)}, u32[]{:S(2)}) collective-permute-start(f32[8,1152]{1,0:T(8,128)S(1)} %get-tuple-element.46), channel_id=1, source_target_pairs={{0,4},{2,6},{4,0},{6,2},{1,5},{3,7},{5,1},{7,3},{8,12},{10,14},{12... | collective-permute-start | bytes 110600 | tf_op jit(solution)/shard_map/ppermute | solution.py:474
  93.4 5.4 %collective-permute-start.6 = (f32[8,1152]{1,0:T(8,128)S(1)}, f32[8,1152]{1,0:T(8,128)S(1)}, u32[]{:S(2)}, u32[]{:S(2)}) collective-permute-start(f32[8,1152]{1,0:T(8,128)S(1)} %get-tuple-element.47), channel_id=1, source_target_pairs={{0,6},{2,0},{4,2},{6,4},{1,7},{3,1},{5,3},{7,5},{8,14},{10,8},{12,... | collective-permute-start | bytes 110600 | tf_op jit(solution)/shard_map/ppermute | solution.py:474

commit v3 on v2

--- a/solution.py
+++ b/solution.py
@@ -56,25 +56,25 @@
         wt[j : j + tile, :] = jnp.transpose(w[:, j : j + tile])
 
 
-def forward_kernel(
-    f_hbm, w_hbm, b1_hbm, w2_hbm, b2_hbm, x_ref, wt_hbm, f, w, b1, w2, b2, wt, sems, outs
-):
-    channels = w.shape[1]
-    parts = [pl.ds(j, tile) for j in range(0, channels, tile)]
-    copies = arrive(
-        [(w_hbm.at[:, p], w.at[:, p]) for p in parts]
-        + [(f_hbm, f), (b1_hbm, b1), (w2_hbm, w2), (b2_hbm, b2)],
-        sems,
-    )
-    sent = []
-    for j, p in enumerate(parts):
-        copies[j].wait()
-        wt[p, :] = jnp.transpose(w[:, p])
-        c = pltpu.make_async_copy(wt.at[p, :], wt_hbm.at[p, :], outs.at[j])
-        c.start()
-        sent.append(c)
-    for c in copies[len(parts) :]:
+def arrive_rows(pairs, count, sems):
+    cut = []
+    for src, dst in pairs:
+        step = src.shape[0] // count
+        cut += [(src.at[pl.ds(i * step, step)], dst.at[pl.ds(i * step, step)]) for i in range(count)]
+    return arrive(cut, sems)
+
+
+def turn(w, wt):
+    for j in range(0, w.shape[1], tile):
+        wt[j : j + tile, :] = jnp.transpose(w[:, j : j + tile])
+
+
+def forward_kernel(f_hbm, w_hbm, b1_hbm, w2_hbm, b2_hbm, x_ref, f, w, b1, w2, b2, wt, big, small):
+    copies = arrive_rows([(w_hbm, w), (f_hbm, f)], 4, big)
+    copies += arrive([(b1_hbm, b1), (w2_hbm, w2), (b2_hbm, b2)], small)
+    for c in copies:
         c.wait()
+    turn(w, wt)
     shift = columns_of(b1[...], lanes)
     bias = columns_of(b2[...], lanes)
     pre = dot(wt[...], f[...], ((1,), (0,))) + jnp.tile(shift, (1, f.shape[1] // lanes))
@@ -83,30 +83,27 @@
     x = dot(w2[...], z, ((1,), (0,)))
     for m in range(x_ref.shape[0]):
         x_ref[m] = x[:, m * lanes : (m + 1) * lanes] + bias
-    for c in sent:
+
+
+def again_kernel(x_hbm, f_hbm, w_hbm, b1_hbm, z_hbm, g_hbm, done_ref, f, w, b1, wt, z, g, big, small, outs):
+    copies = arrive_rows([(w_hbm, w), (f_hbm, f)], 4, big) + arrive([(b1_hbm, b1)], small)
+    for c in copies:
         c.wait()
-
-
-def again_kernel(x_hbm, f_hbm, wt_hbm, b1_hbm, z_hbm, g_hbm, f, wt, b1, z, g, sems, outs):
-    points = f.shape[1]
-    parts = [pl.ds(q, tile) for q in range(0, points, tile)]
-    copies = arrive(
-        [(b1_hbm, b1), (wt_hbm, wt)] + [(f_hbm.at[:, p], f.at[:, p]) for p in parts], sems
-    )
-    copies[0].wait()
-    shift = jnp.tile(columns_of(b1[...], lanes), (1, tile // lanes))
-    copies[1].wait()
+    done_ref[...] = jnp.zeros_like(done_ref)
+    turn(w, wt)
+    half = f.shape[1] // 2
+    shift = jnp.tile(columns_of(b1[...], lanes), (1, half // lanes))
     sent = []
-    for k, here in enumerate(parts):
-        copies[2 + k].wait()
+    for k in range(2):
+        here = pl.ds(k * half, half)
         pre = dot(wt[...], f[:, here], ((1,), (0,))) + shift
         square = pre * pre
         t = jnp.tanh(pre * (root + (root * cubic) * square))
         z[:, here] = (0.5 * pre * (1.0 + t)).astype(bf16)
         inner = root + (3.0 * root * cubic) * square
         g[:, here] = (0.5 * ((1.0 + t) + (pre * inner) * (1.0 - t * t))).astype(bf16)
-        for i, (s, d) in enumerate(((z, z_hbm), (g, g_hbm))):
-            c = pltpu.make_async_copy(s.at[:, here], d.at[:, here], outs.at[k, i])
+        for i, (src, dst) in enumerate(((z, z_hbm), (g, g_hbm))):
+            c = pltpu.make_async_copy(src.at[:, here], dst.at[:, here], outs.at[k, i])
             c.start()
             sent.append(c)
     for c in sent:
@@ -114,7 +111,7 @@
 
 
 def pair_kernel(
-    z_hbm, x_ref, goal_hbm, index_hbm, table_hbm, weight_hbm, dx_ref, misc_ref,
+    done_ref, x_ref, goal_hbm, index_hbm, table_hbm, weight_hbm, dx_ref, misc_ref,
     col, goal_ref, index_ref, table_ref, weight_ref, sems,
 ):
     members, variables, slab = x_ref.shape
@@ -189,43 +186,29 @@
 
 
 def send_kernel(
-    back_ref, w2_ref, misc_ref, g_hbm, z_hbm, f_hbm, dpre_ref, send_ref, keep_ref, dx, g, z, f, piece, sems
+    back_ref, w2_ref, misc_ref, g_ref, z_ref, f_ref, dpre_ref, send_ref, keep_ref, dx, piece
 ):
     members, variables, slab = back_ref.shape
     ny, nx, nzh, rows, _ = send_ref.shape
-    channels, points = z.shape
+    channels, points = z_ref.shape
     share = ny * rows
     core = lax.axis_index("c")
-    steps = channels // tile
-    copies = []
-    for j in range(steps):
-        here = pl.ds(j * tile, tile)
-        copies += [(g_hbm.at[here, :], g.at[here, :]), (z_hbm.at[here, :], z.at[here, :])]
-        if j == 0:
-            copies.append((f_hbm.at[:, 1 - core], f))
-    copies = arrive(copies, sems)
     dx[...] = jnp.zeros_like(dx)
     for m in range(members):
         dx[:variables, m * slab : (m + 1) * slab] = back_ref[m].astype(bf16)
     lane = lax.broadcasted_iota(jnp.int32, (tile, lanes), 1)
     extra = jnp.tile(misc_ref[...], (tile // share, 1))
-    half = None
-    for j in range(steps):
+    half = f_ref[:, 1 - core].reshape(nx * nzh * share, points)
+    for j in range(channels // tile):
         here = slice(j * tile, (j + 1) * tile)
-        w2j = jnp.transpose(w2_ref[:, here])
-        copies[0 if j == 0 else 2 * j + 1].wait()
-        dz = dot(w2j, dx[:variables, :], ((1,), (0,)))
-        d = (dz * g[here, :].astype(f32)).astype(bf16)
+        dz = dot(jnp.transpose(w2_ref[:, here]), dx[:variables, :], ((1,), (0,)))
+        d = (dz * g_ref[here, :].astype(f32)).astype(bf16)
         dpre_ref[here, :] = d
         sums = jnp.sum(d.astype(f32), axis=1, keepdims=True)
-        copies[1 if j == 0 else 2 * j + 2].wait()
-        second = dot(z[here, :], dx[...], ((1,), (1,)))
+        second = dot(z_ref[here, :], dx[...], ((1,), (1,)))
         second = jnp.where(lane == variables, sums, second + extra)
         piece[...] = second.reshape(nzh, 2, share, lanes)
         go, stay = piece[:, 1 - core], piece[:, core]
-        if j == 0:
-            copies[2].wait()
-            half = f[...].reshape(f.shape[0] * share, points)
         first = dot(half, d, ((1,), (1,)))
         for y in range(ny):
             for zh in range(nzh):
@@ -238,29 +221,24 @@
         scatter_rows(first, put, nx, nzh, ny, rows)
 
 
-def window_kernel(d_ref, w_hbm, f_hbm, own_ref, grad_hbm, w, f, grad, sems, outs):
+def window_kernel(d_ref, w_ref, f_ref, own_ref, grad_hbm, grad, outs):
     ny, nx, nzh, rows, channels = own_ref.shape
-    points = d_ref.shape[1]
-    share = ny * rows
     core = lax.axis_index("c")
-    copies = arrive([(f_hbm.at[:, core], f), (w_hbm, w)], sems)
-    copies[0].wait()
-    half = f[...].reshape(f.shape[0] * share, points)
-    first = dot(half, d_ref[...], ((1,), (1,)))
-
-    def put(y, x, zh, value):
-        own_ref[y, x, zh] = value
-
-    scatter_rows(first, put, nx, nzh, ny, rows)
-    copies[1].wait()
     sent = []
     side = channels // 2
     for k in range(2):
         here = pl.ds(k * side, side)
-        grad[here, :] = dot(w[here, :], d_ref[...], ((1,), (0,))).astype(bf16)
+        grad[here, :] = dot(w_ref[here, :], d_ref[...], ((1,), (0,))).astype(bf16)
         c = pltpu.make_async_copy(grad.at[here, :], grad_hbm.at[here, :], outs.at[k])
         c.start()
         sent.append(c)
+    half = f_ref[:, core].reshape(nx * nzh * ny * rows, d_ref.shape[1])
+    first = dot(half, d_ref[...], ((1,), (1,)))
+
+    def put(y, x, zh, value):
+        own_ref[y, x, zh] = value
+
+    scatter_rows(first, put, nx, nzh, ny, rows)
     for c in sent:
         c.wait()
 
@@ -366,11 +344,11 @@
     w2t = w_second.T
     square = (channels, columns)
     dma = pltpu.SemaphoreType.DMA
-    mine, wt = call(
+    mine = call(
         forward_kernel,
-        (shape((members, variables, slab), f32), shape((channels, channels), bf16)),
+        shape((members, variables, slab), f32),
         [hbm] * 5,
-        (near, hbm),
+        near,
         scratch=[
             pltpu.VMEM(square, bf16),
             pltpu.VMEM((channels, channels), bf16),
@@ -379,33 +357,35 @@
             pltpu.VMEM((1, variables), f32),
             pltpu.VMEM((channels, channels), bf16),
             dma((8,)),
-            dma((4,)),
+            dma((3,)),
         ],
         flops=2 * channels * channels * columns,
         limit=60,
     )(features, w_first, b_first[None], w2t, b_second[None])
     fields = lax.all_to_all(mine, ens, 0, 0)
-    z, g = call(
+    z, g, done = call(
         again_kernel,
-        (shape(square, bf16), shape(square, bf16)),
+        (shape(square, bf16), shape(square, bf16), shape((8, lanes), f32)),
         [pl.BlockSpec(memory_space=pl.ANY)] + [hbm] * 3,
-        (hbm, hbm),
+        (hbm, hbm, near),
         scratch=[
             pltpu.VMEM(square, bf16),
             pltpu.VMEM((channels, channels), bf16),
             pltpu.VMEM((1, channels), f32),
+            pltpu.VMEM((channels, channels), bf16),
             pltpu.VMEM(square, bf16),
             pltpu.VMEM(square, bf16),
-            dma((6,)),
-            dma((4, 2)),
+            dma((8,)),
+            dma((1,)),
+            dma((2, 2)),
         ],
         flops=2 * channels * channels * columns,
         limit=60,
-    )(mine, features, wt, b_first[None])
+    )(mine, features, w_first, b_first[None])
     dx, misc = call(
         pair_kernel,
         (shape((members, variables, slab), f32), shape((share, lanes), f32)),
-        [pl.BlockSpec(memory_space=pl.ANY), near] + [hbm] * 4,
+        [near] * 2 + [hbm] * 4,
         (near, near),
         scratch=[
             pltpu.VMEM((lanes, lanes), f32),
@@ -415,23 +395,16 @@
             pltpu.VMEM((1, variables), f32),
             dma((4,)),
         ],
-        limit=60,
-    )(z, fields, target, area_index[None], area_table[None], var_weight[None])
+        flops=2**34,
+    )(done, fields, target, area_index[None], area_table[None], var_weight[None])
     back = lax.all_to_all(dx, ens, 0, 0)
     part = (ny, nx, nzh, rows)
     dpre, send, keep = call(
         send_kernel,
         (shape(square, bf16), shape(part + (wide,), f32), shape(part + (lanes,), f32)),
-        [near] * 3 + [hbm] * 3,
+        [near] * 6,
         (near, near, near),
-        scratch=[
-            pltpu.VMEM((lanes, columns), bf16),
-            pltpu.VMEM(square, bf16),
-            pltpu.VMEM(square, bf16),
-            pltpu.VMEM((nx * nzh, share, columns), bf16),
-            pltpu.VMEM((nzh, nc, share, lanes), f32),
-            dma((9,)),
-        ],
+        scratch=[pltpu.VMEM((lanes, columns), bf16), pltpu.VMEM((nzh, nc, share, lanes), f32)],
         flops=channels * channels * columns,
         limit=24,
     )(back, w2t, misc, g, z, grouped)
@@ -439,15 +412,9 @@
     own, grad_feat = call(
         window_kernel,
         (shape(part + (channels,), f32), shape(square, bf16)),
-        [near, hbm, hbm],
+        [near] * 3,
         (near, hbm),
-        scratch=[
-            pltpu.VMEM((channels, channels), bf16),
-            pltpu.VMEM((nx * nzh, share, columns), bf16),
-            pltpu.VMEM(square, bf16),
-            dma((2,)),
-            dma((2,)),
-        ],
+        scratch=[pltpu.VMEM(square, bf16), dma((2,))],
         flops=3 * channels * channels * columns,
         limit=24,
     )(dpre, w_first, grouped)

time: 110 us -> 99.3 us (0.903)
  Pallas kernels: 30.5 us -> 23.2 us
  local copies, waits for them, and re-layouts: 5.25 us -> 0.73 us
  waiting for transfers between devices: 7.25 us -> 8.49 us
    unnamed x16 -> x20, local copies, waits for them, and re-layouts: 4.67 us -> 0.73 us
    pallas_call x1, Pallas kernels: 5.61 us -> 2.65 us  [on_device(): call(send_kernel, (shape(square, bf16), shape(part + (wide,), f32), shape...]
    pallas_call x1, Pallas kernels: 3.18 us -> 1.2 us  [on_device(): call(pair_kernel, (shape((members, variables, slab), f32), shape((share,...]
    pallas_call x1, Pallas kernels: 4.84 us -> 3.45 us  [on_device(): call(window_kernel, (shape(part + (channels,), f32), shape(square, bf16))...]
  transfers between devices with their start and end apart: 8 -> 8, of which waited for: 5 -> 7; matrix products, arithmetic and copies ran while one was open for 1% -> 0% of each run, Pallas kernels for 13% -> 12%
where the time goes in v3:
time: 99.3 us; the launch traced here: 99 us
  blocking collectives  44.3 us (45%)
  Pallas kernels  23.2 us (23%)
  starting transfers between devices  21.5 us (22%)
  waiting for transfers between devices  8.49 us (9%)
    all_to_all x1, blocking collectives, on_device(): half = lax.all_to_all(half, plane, 0, 0, axis_index_groups=lines(ny, nx))  20.4 us
    all_to_all x1, blocking collectives, on_device(): back = lax.all_to_all(dx, ens, 0, 0)  13.9 us
    ppermute x3, starting transfers between devices, on_device(): lax.ppermute(blocks[d], 'zh', [(i, (i + d) % nzh) for i in range(nzh)])  10.5 us
    all_to_all x1, blocking collectives, on_device(): whole = lax.all_to_all(whole, ens, 0, 0)  10 us
    pallas_call x1, Pallas kernels, on_device(): call(again_kernel, (shape(square, bf16), shape(square, bf16), shape((8, l...  8.49 us
    pallas_call x1, Pallas kernels, on_device(): call(forward_kernel, shape((members, variables, slab), f32), [hbm] * 5, n...  6.15 us
    all_to_all x1, starting transfers between devices, on_device(): fields = lax.all_to_all(mine, ens, 0, 0)  5.84 us
    ppermute x3, starting transfers between devices, on_device(): lax.ppermute(blocks[d], plane, shifts(ny, nx, d))  4.85 us
  transfers between devices with their start and end apart: 8, of which 7 were waited for; matrix products, arithmetic and copies ran while one was open for 0% of the time, Pallas kernels for 12%

profile of v3, /device:TPU:2, one launch (start us, length us, event | category | flops | bytes accessed | tf_op | source)
XLA Modules:
  0.0 99.0 jit_solution(10657713653680310060)
XLA Ops:
  0.6 6.2 %shard_map.136.x_hbm = f32[8,100,128]{2,1,0:T(8,128)} custom-call(bf16[1024,1024]{1,0:T(8,128)(2,1)} %bitcast.11, bf16[1024,1024]{1,0:T(8,128)(2,1)} %w_ref.1, f32[1,1024]{1,0:T(1,128)} %bitcast.19, bf16[100,1024]{1,0:T(8,128)(2,1)} %bitcast.15, f32[1,100]{1,0:T(1,128)} %bitcast.21), custom_call_target="tpu_custom_call" | custom-call | flops 2147483648 | bytes 4194304 | tf_op jit(solution)/shard_map/pallas_call | solution.py:347
  6.8 5.8 %all-to-all-start = ((f32[8,100,128]{2,1,0:T(8,128)}), f32[8,100,128]{2,1,0:T(8,128)S(1)}, u32[]{:S(2)}, u32[]{:S(2)}) async-start(f32[8,100,128]{2,1,0:T(8,128)} %shard_map.136.x_hbm), calls=%async_computation | async-start | bytes 851968 | tf_op jit(solution)/shard_map/all_to_all | solution.py:365
  12.7 0.0 copy-start.5
  12.7 0.0 copy-start.6
  12.7 0.0 copy-start.7
  12.7 8.5 %shard_map.137 = (bf16[1024,1024]{1,0:T(8,128)(2,1)}, bf16[1024,1024]{1,0:T(8,128)(2,1)}, f32[8,128]{1,0:T(8,128)}) custom-call(f32[8,100,128]{2,1,0:T(8,128)} %shard_map.136.x_hbm, bf16[1024,1024]{1,0:T(8,128)(2,1)} %bitcast.12, bf16[1024,1024]{1,0:T(8,128)(2,1)} %w_ref.1, f32[1,1024]{1,0:T(1,128)} %bitcast.20), custom_call_target="tpu_custom_call" | custom-call | flops 2147483648 | bytes 4194304 | tf_op jit(solution)/shard_map/pallas_call | solution.py:366
  21.2 0.2 all-to-all-done.x_ref
  21.4 0.0 copy-start.8
  21.4 0.7 copy-done.8
  22.1 1.2 %shard_map.138 = (f32[8,100,128]{2,1,0:T(8,128)S(1)}, f32[32,128]{1,0:T(8,128)S(1)}) custom-call(f32[8,128]{1,0:T(8,128)S(1)} %copy-done.8, f32[8,100,128]{2,1,0:T(8,128)S(1)} %all-to-all-done.x_ref, f32[100,1024]{1,0:T(8,128)S(1)} %copy-done.5, s32[1,1024]{1,0:T(1,128)S(1)} %bitcast.17, f32[1,721]{1,0:T(1,128)S(1)} %broadcast_in_dim.22.table_hbm, ...), custom_call_target="tpu_custom_call" | custom-call | flops 17179869184 | bytes 4194304 | tf_op jit(solution)/shard_map/pallas_call | solution.py:385
  23.3 13.9 %all_to_all.20.back_ref = f32[8,100,128]{2,1,0:T(8,128)S(1)} all-to-all(f32[8,100,128]{2,1,0:T(8,128)S(1)} %get-tuple-element.30), channel_id=1, replica_groups=mesh['zl'=2,'y'=4,'x'=4,'zh'=4,'c'=2] {'zl','y'}, dimensions={0} | all-to-all | bytes 819200 | tf_op jit(solution)/shard_map/all_to_all | solution.py:400
  37.2 0.0 copy-start.4
  37.3 2.6 %shard_map.139 = (bf16[1024,1024]{1,0:T(8,128)(2,1)S(1)}, f32[4,4,4,8,1152]{4,3,2,1,0:T(8,128)S(1)}, f32[4,4,4,8,128]{4,3,2,1,0:T(8,128)S(1)}) custom-call(f32[8,100,128]{2,1,0:T(8,128)S(1)} %all_to_all.20.back_ref, bf16[100,1024]{1,0:T(8,128)(2,1)S(1)} %bitcast.16, f32[32,128]{1,0:T(8,128)S(1)} %get-tuple-element.31.misc_ref, ...), custom_call_target="tpu_custom_call" | custom-call | flops 1073741824 | bytes 4194304 | tf_op jit(solution)/shard_map/pallas_call | solution.py:402
  39.9 0.3 collective-permute-start
  40.2 3.4 %shard_map.140 = (f32[4,4,4,8,1024]{4,3,2,1,0:T(8,128)S(1)}, bf16[1024,1024]{1,0:T(8,128)(2,1)}) custom-call(bf16[1024,1024]{1,0:T(8,128)(2,1)S(1)} %get-tuple-element.34.d_ref, bf16[1024,1024]{1,0:T(8,128)(2,1)S(1)} %copy-done.4, bf16[16,2,32,1024]{3,2,1,0:T(8,128)(2,1)S(1)} %bitcast.14), custom_call_target="tpu_custom_call" | custom-call | flops 3221225472 | bytes 4194304 | tf_op jit(solution)/shard_map/pallas_call | solution.py:412
  43.7 1.1 %collective-permute-done.other_ref = f32[4,4,4,8,1152]{4,3,2,1,0:T(8,128)S(1)} collective-permute-done((f32[4,4,4,8,1152]{4,3,2,1,0:T(8,128)S(1)}, f32[4,4,4,8,1152]{4,3,2,1,0:T(8,128)S(1)}, u32[]{:S(2)}, u32[]{:S(2)}) %collective-permute-start) | collective-permute-done | bytes 2359328 | tf_op jit(solution)/shard_map/ppermute | solution.py:411
  44.7 0.2 shard_map.141
  44.9 20.4 %all_to_all.21.in_ref = f32[4,4,32,1152]{3,2,1,0:T(8,128)S(1)} all-to-all(f32[4,4,32,1152]{3,2,1,0:T(8,128)S(1)} %shard_map.141), channel_id=1, replica_groups={{0,32,64,96},{8,40,72,104},{16,48,80,112},{24,56,88,120},{1,9,17,25},{3..., dimensions={0} | all-to-all | bytes 4718592 | tf_op jit(solution)/shard_map/all_to_all | solution.py:424
  65.3 0.1 shard_map.142
  65.4 1.6 %collective-permute-start.1 = (f32[32,1152]{1,0:T(8,128)S(1)}, f32[32,1152]{1,0:T(8,128)S(1)}, u32[]{:S(2)}, u32[]{:S(2)}) collective-permute-start(f32[32,1152]{1,0:T(8,128)S(1)} %get-tuple-element.39), channel_id=1, source_target_pairs={{0,8},{8,16},{16,24},{24,0},{32,40},{40,48},{48,56},{56,32},{64,72... | collective-permute-start | bytes 442376 | tf_op jit(solution)/shard_map/ppermute | solution.py:432
  67.0 1.1 %collective-permute-start.2 = (f32[32,1152]{1,0:T(8,128)S(1)}, f32[32,1152]{1,0:T(8,128)S(1)}, u32[]{:S(2)}, u32[]{:S(2)}) collective-permute-start(f32[32,1152]{1,0:T(8,128)S(1)} %get-tuple-element.40), channel_id=1, source_target_pairs={{0,16},{8,24},{16,0},{24,8},{32,48},{40,56},{48,32},{56,40},{64,80... | collective-permute-start | bytes 442376 | tf_op jit(solution)/shard_map/ppermute | solution.py:432
  68.1 2.2 %collective-permute-start.3 = (f32[32,1152]{1,0:T(8,128)S(1)}, f32[32,1152]{1,0:T(8,128)S(1)}, u32[]{:S(2)}, u32[]{:S(2)}) collective-permute-start(f32[32,1152]{1,0:T(8,128)S(1)} %get-tuple-element.41), channel_id=1, source_target_pairs={{0,24},{8,0},{16,8},{24,16},{32,56},{40,32},{48,40},{56,48},{64,88... | collective-permute-start | bytes 442376 | tf_op jit(solution)/shard_map/ppermute | solution.py:432
  70.3 0.4 collective-permute-done.1.refs_1_
  70.7 3.1 %collective-permute-done.2.refs_2_ = f32[32,1152]{1,0:T(8,128)S(1)} collective-permute-done((f32[32,1152]{1,0:T(8,128)S(1)}, f32[32,1152]{1,0:T(8,128)S(1)}, u32[]{:S(2)}, u32[]{:S(2)}) %collective-permute-start.2) | collective-permute-done | bytes 147488 | tf_op jit(solution)/shard_map/ppermute | solution.py:432
  73.8 1.1 %collective-permute-done.3.refs_3_ = f32[32,1152]{1,0:T(8,128)S(1)} collective-permute-done((f32[32,1152]{1,0:T(8,128)S(1)}, f32[32,1152]{1,0:T(8,128)S(1)}, u32[]{:S(2)}, u32[]{:S(2)}) %collective-permute-start.3) | collective-permute-done | bytes 147488 | tf_op jit(solution)/shard_map/ppermute | solution.py:432
  74.9 3.3 %collective-permute-start.4 = (f32[8,1152]{1,0:T(8,128)S(1)}, f32[8,1152]{1,0:T(8,128)S(1)}, u32[]{:S(2)}, u32[]{:S(2)}) collective-permute-start(f32[8,1152]{1,0:T(8,128)S(1)} %get-tuple-element.43), channel_id=1, source_target_pairs={{0,2},{2,4},{4,6},{6,0},{1,3},{3,5},{5,7},{7,1},{8,10},{10,12},{12... | collective-permute-start | bytes 110600 | tf_op jit(solution)/shard_map/ppermute | solution.py:441
  78.2 4.5 %collective-permute-start.5 = (f32[8,1152]{1,0:T(8,128)S(1)}, f32[8,1152]{1,0:T(8,128)S(1)}, u32[]{:S(2)}, u32[]{:S(2)}) collective-permute-start(f32[8,1152]{1,0:T(8,128)S(1)} %get-tuple-element.44), channel_id=1, source_target_pairs={{0,4},{2,6},{4,0},{6,2},{1,5},{3,7},{5,1},{7,3},{8,12},{10,14},{12... | collective-permute-start | bytes 110600 | tf_op jit(solution)/shard_map/ppermute | solution.py:441
  82.8 2.7 %collective-permute-start.6 = (f32[8,1152]{1,0:T(8,128)S(1)}, f32[8,1152]{1,0:T(8,128)S(1)}, u32[]{:S(2)}, u32[]{:S(2)}) collective-permute-start(f32[8,1152]{1,0:T(8,128)S(1)} %get-tuple-element.45), channel_id=1, source_target_pairs={{0,6},{2,0},{4,2},{6,4},{1,7},{3,1},{5,3},{7,5},{8,14},{10,8},{12,... | collective-permute-start | bytes 110600 | tf_op jit(solution)/shard_map/ppermute | solution.py:441
  85.4 0.9 collective-permute-done.5.refs_2_
  86.4 1.8 %collective-permute-done.6.refs_3_ = f32[8,1152]{1,0:T(8,128)S(1)} collective-permute-done((f32[8,1152]{1,0:T(8,128)S(1)}, f32[8,1152]{1,0:T(8,128)S(1)}, u32[]{:S(2)}, u32[]{:S(2)}) %collective-permute-start.6) | collective-permute-done | bytes 36896 | tf_op jit(solution)/shard_map/ppermute | solution.py:441
  88.1 10.0 %all_to_all.22.in_ref = f32[8,8,1152]{2,1,0:T(8,128)S(1)} all-to-all(f32[8,8,1152]{2,1,0:T(8,128)S(1)} %shard_map.144), channel_id=1, replica_groups=mesh['zl'=2,'y'=4,'x'=4,'zh'=4,'c'=2] {'zl','y'}, dimensions={0} | all-to-all | bytes 589824 | tf_op jit(solution)/shard_map/all_to_all | solution.py:445
  98.2 0.8 shard_map.145
  (18 shorter events, 0.1 us)
Async XLA Ops:
  0.6 12.0 %copy-start.9 = (f32[721]{0:T(1024)S(1)}, f32[721]{0:T(1024)}, u32[]{:S(2)}) copy-start(f32[721]{0:T(1024)} %param.12) | copy-start | bytes 8656
  6.8 14.6 %all-to-all-start = ((f32[8,100,128]{2,1,0:T(8,128)}), f32[8,100,128]{2,1,0:T(8,128)S(1)}, u32[]{:S(2)}, u32[]{:S(2)}) async-start(f32[8,100,128]{2,1,0:T(8,128)} %shard_map.136.x_hbm), calls=%async_computation | async-start | bytes 851968 | tf_op jit(solution)/shard_map/all_to_all | solution.py:365
  12.7 8.7 %copy-start.5 = (f32[100,1024]{1,0:T(8,128)S(1)}, f32[100,1024]{1,0:T(8,128)}, u32[]{:S(2)}) copy-start(f32[100,1024]{1,0:T(8,128)} %goal_hbm.1) | copy-start | bytes 1228804
  12.7 8.7 %copy-start.6 = (s32[1024]{0:T(1024)S(1)}, s32[1024]{0:T(1024)}, u32[]{:S(2)}) copy-start(s32[1024]{0:T(1024)} %param.11) | copy-start | bytes 12292
  12.7 8.7 %copy-start.7 = (f32[100]{0:T(128)S(1)}, f32[100]{0:T(128)}, u32[]{:S(2)}) copy-start(f32[100]{0:T(128)} %param.13) | copy-start | bytes 1204
  21.4 0.7 copy-start.8
  22.1 15.1 %copy-start = (bf16[1,1024,1024]{2,1,0:T(8,128)(2,1)S(1)}, bf16[1,1024,1024]{2,1,0:T(8,128)(2,1)}, u32[]{:S(2)}) copy-start(bf16[1,1024,1024]{2,1,0:T(8,128)(2,1)} %param.9) | copy-start | bytes 6291460
  22.1 15.1 %copy-start.1 = (bf16[1024,1024]{1,0:T(8,128)(2,1)S(1)}, bf16[1024,1024]{1,0:T(8,128)(2,1)}, u32[]{:S(2)}) copy-start(bf16[1024,1024]{1,0:T(8,128)(2,1)} %get-tuple-element.33.z_ref) | copy-start | bytes 6291460
  22.1 15.1 %copy-start.2 = (bf16[1024,1024]{1,0:T(8,128)(2,1)S(1)}, bf16[1024,1024]{1,0:T(8,128)(2,1)}, u32[]{:S(2)}) copy-start(bf16[1024,1024]{1,0:T(8,128)(2,1)} %get-tuple-element.32.g_ref) | copy-start | bytes 6291460
  22.1 15.1 %copy-start.3 = (bf16[1024,100]{0,1:T(8,128)(2,1)S(1)}, bf16[1024,100]{0,1:T(8,128)(2,1)}, u32[]{:S(2)}) copy-start(bf16[1024,100]{0,1:T(8,128)(2,1)} %param.16) | copy-start | bytes 614404
  37.2 2.9 %copy-start.4 = (bf16[1024,1024]{1,0:T(8,128)(2,1)S(1)}, bf16[1024,1024]{1,0:T(8,128)(2,1)}, u32[]{:S(2)}) copy-start(bf16[1024,1024]{1,0:T(8,128)(2,1)} %w_ref.1) | copy-start | bytes 6291460
  39.9 4.8 %collective-permute-start = (f32[4,4,4,8,1152]{4,3,2,1,0:T(8,128)S(1)}, f32[4,4,4,8,1152]{4,3,2,1,0:T(8,128)S(1)}, u32[]{:S(2)}, u32[]{:S(2)}) collective-permute-start(f32[4,4,4,8,1152]{4,3,2,1,0:T(8,128)S(1)} %get-tuple-element.37), channel_id=1, source_target_pairs={{0,1},{1,0},{2,3},{3,2},{4,5},{5,4},{6,7},{7,6},{8,9},{9,8},{10,11... | collective-permute-start | bytes 7077896 | tf_op jit(solution)/shard_map/ppermute | solution.py:411
  65.4 5.2 %collective-permute-start.1 = (f32[32,1152]{1,0:T(8,128)S(1)}, f32[32,1152]{1,0:T(8,128)S(1)}, u32[]{:S(2)}, u32[]{:S(2)}) collective-permute-start(f32[32,1152]{1,0:T(8,128)S(1)} %get-tuple-element.39), channel_id=1, source_target_pairs={{0,8},{8,16},{16,24},{24,0},{32,40},{40,48},{48,56},{56,32},{64,72... | collective-permute-start | bytes 442376 | tf_op jit(solution)/shard_map/ppermute | solution.py:432
  67.0 6.8 %collective-permute-start.2 = (f32[32,1152]{1,0:T(8,128)S(1)}, f32[32,1152]{1,0:T(8,128)S(1)}, u32[]{:S(2)}, u32[]{:S(2)}) collective-permute-start(f32[32,1152]{1,0:T(8,128)S(1)} %get-tuple-element.40), channel_id=1, source_target_pairs={{0,16},{8,24},{16,0},{24,8},{32,48},{40,56},{48,32},{56,40},{64,80... | collective-permute-start | bytes 442376 | tf_op jit(solution)/shard_map/ppermute | solution.py:432
  68.1 6.7 %collective-permute-start.3 = (f32[32,1152]{1,0:T(8,128)S(1)}, f32[32,1152]{1,0:T(8,128)S(1)}, u32[]{:S(2)}, u32[]{:S(2)}) collective-permute-start(f32[32,1152]{1,0:T(8,128)S(1)} %get-tuple-element.41), channel_id=1, source_target_pairs={{0,24},{8,0},{16,8},{24,16},{32,56},{40,32},{48,40},{56,48},{64,88... | collective-permute-start | bytes 442376 | tf_op jit(solution)/shard_map/ppermute | solution.py:432
  74.9 10.5 %collective-permute-start.4 = (f32[8,1152]{1,0:T(8,128)S(1)}, f32[8,1152]{1,0:T(8,128)S(1)}, u32[]{:S(2)}, u32[]{:S(2)}) collective-permute-start(f32[8,1152]{1,0:T(8,128)S(1)} %get-tuple-element.43), channel_id=1, source_target_pairs={{0,2},{2,4},{4,6},{6,0},{1,3},{3,5},{5,7},{7,1},{8,10},{10,12},{12... | collective-permute-start | bytes 110600 | tf_op jit(solution)/shard_map/ppermute | solution.py:441
  78.2 8.1 %collective-permute-start.5 = (f32[8,1152]{1,0:T(8,128)S(1)}, f32[8,1152]{1,0:T(8,128)S(1)}, u32[]{:S(2)}, u32[]{:S(2)}) collective-permute-start(f32[8,1152]{1,0:T(8,128)S(1)} %get-tuple-element.44), channel_id=1, source_target_pairs={{0,4},{2,6},{4,0},{6,2},{1,5},{3,7},{5,1},{7,3},{8,12},{10,14},{12... | collective-permute-start | bytes 110600 | tf_op jit(solution)/shard_map/ppermute | solution.py:441
  82.8 5.4 %collective-permute-start.6 = (f32[8,1152]{1,0:T(8,128)S(1)}, f32[8,1152]{1,0:T(8,128)S(1)}, u32[]{:S(2)}, u32[]{:S(2)}) collective-permute-start(f32[8,1152]{1,0:T(8,128)S(1)} %get-tuple-element.45), channel_id=1, source_target_pairs={{0,6},{2,0},{4,2},{6,4},{1,7},{3,1},{5,3},{7,5},{8,14},{10,8},{12,... | collective-permute-start | bytes 110600 | tf_op jit(solution)/shard_map/ppermute | solution.py:441

commit v4 on v3

--- a/solution.py
+++ b/solution.py
@@ -98,10 +98,10 @@
         here = pl.ds(k * half, half)
         pre = dot(wt[...], f[:, here], ((1,), (0,))) + shift
         square = pre * pre
-        t = jnp.tanh(pre * (root + (root * cubic) * square))
-        z[:, here] = (0.5 * pre * (1.0 + t)).astype(bf16)
-        inner = root + (3.0 * root * cubic) * square
-        g[:, here] = (0.5 * ((1.0 + t) + (pre * inner) * (1.0 - t * t))).astype(bf16)
+        rise = 0.5 + 0.5 * jnp.tanh(pre * (root + (root * cubic) * square))
+        z[:, here] = (pre * rise).astype(bf16)
+        inner = 2.0 * root + (6.0 * root * cubic) * square
+        g[:, here] = (rise + (pre * inner) * (rise * (1.0 - rise))).astype(bf16)
         for i, (src, dst) in enumerate(((z, z_hbm), (g, g_hbm))):
             c = pltpu.make_async_copy(src.at[:, here], dst.at[:, here], outs.at[k, i])
             c.start()
@@ -117,7 +117,7 @@
     members, variables, slab = x_ref.shape
     me = lax.axis_index(ens)
     here = pl.ds(pl.multiple_of(me * slab, slab), slab)
-    rows = table_ref.shape[1]
+    rows = table_ref.shape[0]
     copies = arrive(
         [
             (index_hbm, index_ref),
@@ -144,7 +144,7 @@
         c.wait()
     hot = lax.broadcasted_iota(jnp.int32, (rows, slab), 0) == index_ref[:, here]
     area = lax.dot_general(
-        table_ref[...],
+        table_ref[...].reshape(1, rows),
         hot.astype(f32),
         (((1,), (0,)), ((), ())),
         precision=lax.Precision.HIGHEST,
@@ -185,66 +185,112 @@
                 put(y, x, zh, first[r : r + rows])
 
 
-def send_kernel(
-    back_ref, w2_ref, misc_ref, g_ref, z_ref, f_ref, dpre_ref, send_ref, keep_ref, dx, piece
+def gradient_rows(w2_ref, g_ref, dx, here):
+    dz = dot(jnp.transpose(w2_ref[:, here]), dx, ((1,), (0,)))
+    return (dz * g_ref[here, :].astype(f32)).astype(bf16)
+
+
+def first_kernel(back_ref, w2_ref, g_ref, f_ref, d_ref, dx_ref, send_ref):
+    members, variables, slab = back_ref.shape
+    ny, nx, nzh, rows, wide = send_ref.shape
+    core = lax.axis_index("c")
+    dx_ref[...] = jnp.zeros_like(dx_ref)
+    for m in range(members):
+        dx_ref[:variables, m * slab : (m + 1) * slab] = back_ref[m].astype(bf16)
+    half = f_ref[:, 1 - core].reshape(nx * nzh * ny * rows, dx_ref.shape[1])
+    for j in range(wide // tile):
+        here = slice(j * tile, (j + 1) * tile)
+        d = gradient_rows(w2_ref, g_ref, dx_ref[:variables, :], here)
+        d_ref[here, :] = d
+        first = dot(half, d, ((1,), (1,)))
+
+        def put(y, x, zh, value):
+            send_ref[y, x, zh, :, here] = value
+
+        scatter_rows(first, put, nx, nzh, ny, rows)
+
+
+def second_kernel(
+    d1_ref, dx_ref, w2_ref, misc_ref, g_ref, z_ref, f_ref, d_ref, send_ref, keep_ref, piece
 ):
-    members, variables, slab = back_ref.shape
-    ny, nx, nzh, rows, _ = send_ref.shape
+    ny, nx, nzh, rows, wide = send_ref.shape
+    wide = wide - lanes
+    variables = w2_ref.shape[0]
     channels, points = z_ref.shape
     share = ny * rows
     core = lax.axis_index("c")
-    dx[...] = jnp.zeros_like(dx)
-    for m in range(members):
-        dx[:variables, m * slab : (m + 1) * slab] = back_ref[m].astype(bf16)
+    half = f_ref[:, 1 - core].reshape(nx * nzh * share, points)
+    base = channels - wide
+    for j in range(wide // tile):
+        here = slice(j * tile, (j + 1) * tile)
+        there = slice(base + j * tile, base + (j + 1) * tile)
+        d = gradient_rows(w2_ref, g_ref, dx_ref[:variables, :], there)
+        d_ref[here, :] = d
+        first = dot(half, d, ((1,), (1,)))
+
+        def put(y, x, zh, value):
+            send_ref[y, x, zh, :, here] = value
+
+        scatter_rows(first, put, nx, nzh, ny, rows)
     lane = lax.broadcasted_iota(jnp.int32, (tile, lanes), 1)
     extra = jnp.tile(misc_ref[...], (tile // share, 1))
-    half = f_ref[:, 1 - core].reshape(nx * nzh * share, points)
     for j in range(channels // tile):
         here = slice(j * tile, (j + 1) * tile)
-        dz = dot(jnp.transpose(w2_ref[:, here]), dx[:variables, :], ((1,), (0,)))
-        d = (dz * g_ref[here, :].astype(f32)).astype(bf16)
-        dpre_ref[here, :] = d
+        d = d1_ref[here, :] if j * tile < base else d_ref[j * tile - base : (j + 1) * tile - base, :]
         sums = jnp.sum(d.astype(f32), axis=1, keepdims=True)
-        second = dot(z_ref[here, :], dx[...], ((1,), (1,)))
+        second = dot(z_ref[here, :], dx_ref[...], ((1,), (1,)))
         second = jnp.where(lane == variables, sums, second + extra)
         piece[...] = second.reshape(nzh, 2, share, lanes)
         go, stay = piece[:, 1 - core], piece[:, core]
-        first = dot(half, d, ((1,), (1,)))
         for y in range(ny):
             for zh in range(nzh):
-                send_ref[y, j, zh, :, channels:] = go[zh, y * rows : (y + 1) * rows]
+                send_ref[y, j, zh, :, wide:] = go[zh, y * rows : (y + 1) * rows]
                 keep_ref[y, j, zh] = stay[zh, y * rows : (y + 1) * rows]
 
-        def put(y, x, zh, value):
-            send_ref[y, x, zh, :, here] = value
-
-        scatter_rows(first, put, nx, nzh, ny, rows)
-
-
-def window_kernel(d_ref, w_ref, f_ref, own_ref, grad_hbm, grad, outs):
+
+def after_kernel(left_ref, right_ref, out_ref):
+    pass
+
+
+def own_kernel(d1_ref, d2_ref, f_ref, left_ref, own_ref):
     ny, nx, nzh, rows, channels = own_ref.shape
     core = lax.axis_index("c")
+    cut, points = d1_ref.shape
+    half = f_ref[:, core].reshape(nx * nzh * ny * rows, points)
+    for j in range(channels // tile):
+        here = slice(j * tile, (j + 1) * tile)
+        early = j * tile < cut
+        d = d1_ref[here, :] if early else d2_ref[j * tile - cut : (j + 1) * tile - cut, :]
+        first = dot(half, d, ((1,), (1,)))
+
+        def put(y, x, zh, value):
+            own_ref[y, x, zh, :, here] = value + left_ref[y, x, zh, :, here] if early else value
+
+        scatter_rows(first, put, nx, nzh, ny, rows)
+
+
+def grad_kernel(late_ref, d1_ref, d2_ref, w_ref, grad_hbm, done_ref, d, grad, outs):
+    done_ref[...] = jnp.zeros_like(done_ref)
+    channels = w_ref.shape[0]
+    split = d1_ref.shape[0]
+    d[:split, :] = d1_ref[...]
+    d[split:, :] = d2_ref[...]
     sent = []
     side = channels // 2
     for k in range(2):
         here = pl.ds(k * side, side)
-        grad[here, :] = dot(w_ref[here, :], d_ref[...], ((1,), (0,))).astype(bf16)
+        grad[here, :] = dot(w_ref[here, :], d[...], ((1,), (0,))).astype(bf16)
         c = pltpu.make_async_copy(grad.at[here, :], grad_hbm.at[here, :], outs.at[k])
         c.start()
         sent.append(c)
-    half = f_ref[:, core].reshape(nx * nzh * ny * rows, d_ref.shape[1])
-    first = dot(half, d_ref[...], ((1,), (1,)))
-
-    def put(y, x, zh, value):
-        own_ref[y, x, zh] = value
-
-    scatter_rows(first, put, nx, nzh, ny, rows)
     for c in sent:
         c.wait()
 
 
-def add_kernel(own_ref, keep_ref, other_ref, out_ref):
+def add_kernel(own_ref, keep_ref, right_ref, out_ref):
     ny, nx, nzh, rows, channels = own_ref.shape
+    width = right_ref.shape[4] - keep_ref.shape[4]
+    cut = channels - width
     core = lax.axis_index("c")
     for y in range(ny):
         for x in range(nx):
@@ -252,11 +298,12 @@
             b = jnp.where(core == 0, x, y)
             for zh in range(nzh):
                 here = pl.ds(zh * rows, rows)
-                out_ref[a, b, here, :channels] = (
-                    own_ref[y, x, zh] + other_ref[y, x, zh, :, :channels]
+                out_ref[a, b, here, :cut] = own_ref[y, x, zh, :, :cut]
+                out_ref[a, b, here, cut:channels] = (
+                    own_ref[y, x, zh, :, cut:] + right_ref[y, x, zh, :, :width]
                 )
                 out_ref[a, b, here, channels:] = (
-                    keep_ref[y, x, zh] + other_ref[y, x, zh, :, channels:]
+                    keep_ref[y, x, zh] + right_ref[y, x, zh, :, width:]
                 )
 
 
@@ -272,7 +319,7 @@
         out_refs[d][...] = total
 
 
-def redeal_kernel(axis, *refs):
+def redeal_kernel(axis, done_ref, *refs):
     n = len(refs) // 2
     me = lax.axis_index(axis)
     rows = refs[n].shape[0]
@@ -391,36 +438,54 @@
             pltpu.VMEM((lanes, lanes), f32),
             pltpu.VMEM((variables, slab), f32),
             pltpu.VMEM((1, columns), jnp.int32),
-            pltpu.VMEM((1, area_table.shape[0]), f32),
+            pltpu.VMEM(area_table.shape, f32),
             pltpu.VMEM((1, variables), f32),
             dma((4,)),
         ],
         flops=2**34,
-    )(done, fields, target, area_index[None], area_table[None], var_weight[None])
+    )(done, fields, target, area_index[None], area_table, var_weight[None])
     back = lax.all_to_all(dx, ens, 0, 0)
     part = (ny, nx, nzh, rows)
-    dpre, send, keep = call(
-        send_kernel,
-        (shape(square, bf16), shape(part + (wide,), f32), shape(part + (lanes,), f32)),
-        [near] * 6,
-        (near, near, near),
-        scratch=[pltpu.VMEM((lanes, columns), bf16), pltpu.VMEM((nzh, nc, share, lanes), f32)],
-        flops=channels * channels * columns,
-        limit=24,
-    )(back, w2t, misc, g, z, grouped)
-    other = lax.ppermute(send, "c", [(0, 1), (1, 0)])
-    own, grad_feat = call(
-        window_kernel,
-        (shape(part + (channels,), f32), shape(square, bf16)),
-        [near] * 3,
-        (near, hbm),
-        scratch=[pltpu.VMEM(square, bf16), dma((2,))],
-        flops=3 * channels * channels * columns,
-        limit=24,
-    )(dpre, w_first, grouped)
+    cut = channels // 2
+    mirror = [(0, 1), (1, 0)]
+    d1, dxs, left = call(
+        first_kernel,
+        (shape((cut, columns), bf16), shape((lanes, columns), bf16), shape(part + (cut,), f32)),
+        [near] * 4,
+        (near,) * 3,
+        flops=channels * channels * columns // 2,
+    )(back, w2t, g, grouped)
+    left = lax.ppermute(left, "c", mirror)
+    d2, right, keep = call(
+        second_kernel,
+        (
+            shape((channels - cut, columns), bf16),
+            shape(part + (channels - cut + lanes,), f32),
+            shape(part + (lanes,), f32),
+        ),
+        [near] * 7,
+        (near,) * 3,
+        scratch=[pltpu.VMEM((nzh, nc, share, lanes), f32)],
+        flops=channels * channels * columns // 2,
+    )(d1, dxs, w2t, misc, g, z, grouped)
+    right = pl.pallas_call(
+        after_kernel,
+        out_shape=shape(right.shape, f32),
+        in_specs=[pl.BlockSpec(memory_space=pl.ANY)] * 2,
+        out_specs=pl.BlockSpec(memory_space=pl.ANY),
+        input_output_aliases={1: 0},
+        compiler_params=pltpu.CompilerParams(vmem_limit_bytes=2**20),
+    )(left, right)
+    right = lax.ppermute(right, "c", mirror)
+    own = call(
+        own_kernel,
+        shape(part + (channels,), f32),
+        [near] * 4,
+        near,
+    )(d1, d2, grouped, left)
     half = call(
         add_kernel, shape((ny, nx, nzh * rows, wide), f32), [near] * 3, near
-    )(own, keep, other)
+    )(own, keep, right)
     half = lax.all_to_all(half, plane, 0, 0, axis_index_groups=lines(ny, nx))
     blocks = call(
         functools.partial(deal_kernel, ("x", "y")),
@@ -428,15 +493,23 @@
         [near],
         (near,) * nx,
     )(half)
+    grad_feat, built = call(
+        grad_kernel,
+        (shape(square, bf16), shape((8, lanes), f32)),
+        [near] * 4,
+        (hbm, near),
+        scratch=[pltpu.VMEM(square, bf16), pltpu.VMEM(square, bf16), dma((2,))],
+        flops=2 * channels * channels * columns,
+    )(blocks[0], d1, d2, w_first)
     blocks = (blocks[0],) + tuple(
         lax.ppermute(blocks[d], plane, shifts(ny, nx, d)) for d in range(1, nx)
     )
     blocks = call(
         functools.partial(redeal_kernel, "zh"),
         (shape((rows, wide), f32),) * nzh,
-        [near] * nx,
+        [near] * (1 + nx),
         (near,) * nzh,
-    )(*blocks)
+    )(built, *blocks)
     blocks = (blocks[0],) + tuple(
         lax.ppermute(blocks[d], "zh", [(i, (i + d) % nzh) for i in range(nzh)])
         for d in range(1, nzh)

time: 99.3 us -> 98.5 us (level)
  waiting for transfers between devices: 8.49 us -> 6.37 us
  Pallas kernels: 23.2 us -> 24.3 us
    ppermute x3, waiting for transfers between devices: 4.55 us -> 1.24 us  [on_device(): lax.ppermute(blocks[d], plane, shifts(ny, nx, d))]
    pallas_call x2 -> x5, Pallas kernels: 6.09 us -> 7.44 us  [the longest x1 3.32 us: on_device(): call(grad_kernel, (shape(square, bf16), shape((8, lanes), f32)), [near] *...]
    ppermute x1 -> x2, waiting for transfers between devices: 1.06 us -> 2.07 us  [the longest x1 1.61 us: on_device(): right = lax.ppermute(right, 'c', mirror)]
  transfers between devices with their start and end apart: 8 -> 9, of which waited for: 7 -> 7; matrix products, arithmetic and copies ran while one was open for 0% -> 0% of each run, Pallas kernels for 12% -> 15%
where the time goes in v4:
time: 98.5 us; the launch traced here: 98.2 us
  blocking collectives  44.2 us (45%)
  Pallas kernels  24.3 us (25%)
  starting transfers between devices  21.4 us (22%)
  waiting for transfers between devices  6.37 us (6%)
  local copies, waits for them, and re-layouts  1.14 us (1%)
    all_to_all x1, blocking collectives, on_device(): half = lax.all_to_all(half, plane, 0, 0, axis_index_groups=lines(ny, nx))  20.4 us
    all_to_all x1, blocking collectives, on_device(): back = lax.all_to_all(dx, ens, 0, 0)  13.8 us
    ppermute x3, starting transfers between devices, on_device(): lax.ppermute(blocks[d], 'zh', [(i, (i + d) % nzh) for i in range(nzh)])  10.5 us
    all_to_all x1, blocking collectives, on_device(): whole = lax.all_to_all(whole, ens, 0, 0)  10 us
    pallas_call x1, Pallas kernels, on_device(): call(again_kernel, (shape(square, bf16), shape(square, bf16), shape((8, l...  8.34 us
    pallas_call x1, Pallas kernels, on_device(): call(forward_kernel, shape((members, variables, slab), f32), [hbm] * 5, n...  6.16 us
    all_to_all x1, starting transfers between devices, on_device(): fields = lax.all_to_all(mine, ens, 0, 0)  5.83 us
    ppermute x3, starting transfers between devices, on_device(): lax.ppermute(blocks[d], plane, shifts(ny, nx, d))  4.83 us
  transfers between devices with their start and end apart: 9, of which 7 were waited for; matrix products, arithmetic and copies ran while one was open for 0% of the time, Pallas kernels for 15%

profile of v4, /device:TPU:2, one launch (start us, length us, event | category | flops | bytes accessed | tf_op | source)
XLA Modules:
  0.0 98.2 jit_solution(8372557252207195261)
XLA Ops:
  0.6 6.2 %shard_map.136.x_hbm = f32[8,100,128]{2,1,0:T(8,128)} custom-call(bf16[1024,1024]{1,0:T(8,128)(2,1)} %bitcast.11, bf16[1024,1024]{1,0:T(8,128)(2,1)} %w_ref.1, f32[1,1024]{1,0:T(1,128)} %bitcast.21, bf16[100,1024]{1,0:T(8,128)(2,1)} %bitcast.16, f32[1,100]{1,0:T(1,128)} %bitcast.23), custom_call_target="tpu_custom_call" | custom-call | flops 2147483648 | bytes 4194304 | tf_op jit(solution)/shard_map/pallas_call | solution.py:394
  6.8 5.8 %all-to-all-start = ((f32[8,100,128]{2,1,0:T(8,128)}), f32[8,100,128]{2,1,0:T(8,128)S(1)}, u32[]{:S(2)}, u32[]{:S(2)}) async-start(f32[8,100,128]{2,1,0:T(8,128)} %shard_map.136.x_hbm), calls=%async_computation | async-start | bytes 851968 | tf_op jit(solution)/shard_map/all_to_all | solution.py:412
  12.6 0.0 copy-start.6
  12.7 8.3 %shard_map.137 = (bf16[1024,1024]{1,0:T(8,128)(2,1)}, bf16[1024,1024]{1,0:T(8,128)(2,1)}, f32[8,128]{1,0:T(8,128)}) custom-call(f32[8,100,128]{2,1,0:T(8,128)} %shard_map.136.x_hbm, bf16[1024,1024]{1,0:T(8,128)(2,1)} %bitcast.12, bf16[1024,1024]{1,0:T(8,128)(2,1)} %w_ref.1, f32[1,1024]{1,0:T(1,128)} %bitcast.22), custom_call_target="tpu_custom_call" | custom-call | flops 2147483648 | bytes 4194304 | tf_op jit(solution)/shard_map/pallas_call | solution.py:413
  21.0 0.4 all-to-all-done.x_ref
  21.4 0.7 copy-done.9
  22.1 1.2 %shard_map.138 = (f32[8,100,128]{2,1,0:T(8,128)S(1)}, f32[32,128]{1,0:T(8,128)S(1)}) custom-call(f32[8,128]{1,0:T(8,128)S(1)} %copy-done.9, f32[8,100,128]{2,1,0:T(8,128)S(1)} %all-to-all-done.x_ref, f32[100,1024]{1,0:T(8,128)S(1)} %copy-done.5, s32[1,1024]{1,0:T(1,128)S(1)} %bitcast.19, f32[721]{0:T(1024)S(1)} %copy-done.7, f32[1,100]{1,0:T(1,128)S(1)} %bitcast.20), custom_call_target="tpu_custom_call" | custom-call | flops 17179869184 | bytes 4194304 | tf_op jit(solution)/shard_map/pallas_call | solution.py:432
  23.3 13.8 %all_to_all.20.back_ref = f32[8,100,128]{2,1,0:T(8,128)S(1)} all-to-all(f32[8,100,128]{2,1,0:T(8,128)S(1)} %get-tuple-element.33), channel_id=1, replica_groups=mesh['zl'=2,'y'=4,'x'=4,'zh'=4,'c'=2] {'zl','y'}, dimensions={0} | all-to-all | bytes 819200 | tf_op jit(solution)/shard_map/all_to_all | solution.py:447
  37.1 1.1 %shard_map.139 = (bf16[512,1024]{1,0:T(8,128)(2,1)S(1)}, bf16[128,1024]{1,0:T(8,128)(2,1)S(1)}, f32[4,4,4,8,512]{4,3,2,1,0:T(8,128)S(1)}) custom-call(f32[8,100,128]{2,1,0:T(8,128)S(1)} %all_to_all.20.back_ref, bf16[100,1024]{1,0:T(8,128)(2,1)S(1)} %bitcast.17, bf16[1024,1024]{1,0:T(8,128)(2,1)S(1)} %copy-done.1, bf16[16,2,32,1024]{3,2,1,0:T(8,128)(2,1)S(1)} %bitcast.13), custom_call_target="tpu_custom_call" | custom-call | flops 536870912 | bytes 4194304 | tf_op jit(solution)/shard_map/pallas_call | solution.py:451
  38.2 0.1 collective-permute-start
  38.3 0.4 copy-done.2
  38.7 1.8 %shard_map.140 = (bf16[512,1024]{1,0:T(8,128)(2,1)S(1)}, f32[4,4,4,8,640]{4,3,2,1,0:T(8,128)S(1)}, f32[4,4,4,8,128]{4,3,2,1,0:T(8,128)S(1)}) custom-call(bf16[512,1024]{1,0:T(8,128)(2,1)S(1)} %get-tuple-element.35.d1_ref, bf16[128,1024]{1,0:T(8,128)(2,1)S(1)} %get-tuple-element.36.dx_ref, bf16[100,1024]{1,0:T(8,128)(2,1)S(1)} %bitcast.18, ...), custom_call_target="tpu_custom_call" | custom-call | flops 536870912 | bytes 4194304 | tf_op jit(solution)/shard_map/pallas_call | solution.py:459
  40.4 0.5 collective-permute-done.left_ref
  40.9 0.1 collective-permute-start.1
  41.0 1.3 %shard_map.141.own_ref = f32[4,4,4,8,1024]{4,3,2,1,0:T(8,128)S(1)} custom-call(bf16[512,1024]{1,0:T(8,128)(2,1)S(1)} %get-tuple-element.35.d1_ref, bf16[512,1024]{1,0:T(8,128)(2,1)S(1)} %get-tuple-element.39.d2_ref, bf16[16,2,32,1024]{3,2,1,0:T(8,128)(2,1)S(1)} %bitcast.15, f32[4,4,4,8,512]{4,3,2,1,0:T(8,128)S(1)} %collective-permute-done.left_ref), custom_call_target="tpu_custom_call" | custom-call | bytes 4194304 | tf_op jit(solution)/shard_map/pallas_call | solution.py:480
  42.3 1.6 %collective-permute-done.1.right_ref = f32[4,4,4,8,640]{4,3,2,1,0:T(8,128)S(1)} collective-permute-done((f32[4,4,4,8,640]{4,3,2,1,0:T(8,128)S(1)}, f32[4,4,4,8,640]{4,3,2,1,0:T(8,128)S(1)}, u32[]{:S(2)}, u32[]{:S(2)}) %collective-permute-start.1) | collective-permute-done | bytes 1310752 | tf_op jit(solution)/shard_map/ppermute | solution.py:479
  43.9 0.2 shard_map.143
  44.1 20.4 %all_to_all.21.in_ref = f32[4,4,32,1152]{3,2,1,0:T(8,128)S(1)} all-to-all(f32[4,4,32,1152]{3,2,1,0:T(8,128)S(1)} %shard_map.143), channel_id=1, replica_groups={{0,32,64,96},{8,40,72,104},{16,48,80,112},{24,56,88,120},{1,9,17,25},{3..., dimensions={0} | all-to-all | bytes 4718592 | tf_op jit(solution)/shard_map/all_to_all | solution.py:489
  64.5 0.1 shard_map.144
  64.6 1.6 %collective-permute-start.2 = (f32[32,1152]{1,0:T(8,128)S(1)}, f32[32,1152]{1,0:T(8,128)S(1)}, u32[]{:S(2)}, u32[]{:S(2)}) collective-permute-start(f32[32,1152]{1,0:T(8,128)S(1)} %get-tuple-element.45), channel_id=1, source_target_pairs={{0,8},{8,16},{16,24},{24,0},{32,40},{40,48},{48,56},{56,32},{64,72... | collective-permute-start | bytes 442376 | tf_op jit(solution)/shard_map/ppermute | solution.py:505
  66.2 1.1 %collective-permute-start.3 = (f32[32,1152]{1,0:T(8,128)S(1)}, f32[32,1152]{1,0:T(8,128)S(1)}, u32[]{:S(2)}, u32[]{:S(2)}) collective-permute-start(f32[32,1152]{1,0:T(8,128)S(1)} %get-tuple-element.46), channel_id=1, source_target_pairs={{0,16},{8,24},{16,0},{24,8},{32,48},{40,56},{48,32},{56,40},{64,80... | collective-permute-start | bytes 442376 | tf_op jit(solution)/shard_map/ppermute | solution.py:505
  67.3 2.1 %collective-permute-start.4 = (f32[32,1152]{1,0:T(8,128)S(1)}, f32[32,1152]{1,0:T(8,128)S(1)}, u32[]{:S(2)}, u32[]{:S(2)}) collective-permute-start(f32[32,1152]{1,0:T(8,128)S(1)} %get-tuple-element.47), channel_id=1, source_target_pairs={{0,24},{8,0},{16,8},{24,16},{32,56},{40,32},{48,40},{56,48},{64,88... | collective-permute-start | bytes 442376 | tf_op jit(solution)/shard_map/ppermute | solution.py:505
  69.5 3.3 %shard_map.145 = (bf16[1024,1024]{1,0:T(8,128)(2,1)}, f32[8,128]{1,0:T(8,128)S(1)}) custom-call(f32[32,1152]{1,0:T(8,128)S(1)} %get-tuple-element.43.late_ref.refs_0_, bf16[512,1024]{1,0:T(8,128)(2,1)S(1)} %get-tuple-element.35.d1_ref, bf16[512,1024]{1,0:T(8,128)(2,1)S(1)} %get-tuple-element.39.d2_ref, bf16[1024,1024]{1,0:T(8,128)(2,1)S(1)} %copy-done.4), custom_call_target="tpu_custom_call" | custom-call | flops 2147483648 | bytes 4194304 | tf_op jit(solution)/shard_map/pallas_call | solution.py:496
  72.8 0.1 collective-permute-done.3.refs_2_
  73.0 1.1 %collective-permute-done.4.refs_3_ = f32[32,1152]{1,0:T(8,128)S(1)} collective-permute-done((f32[32,1152]{1,0:T(8,128)S(1)}, f32[32,1152]{1,0:T(8,128)S(1)}, u32[]{:S(2)}, u32[]{:S(2)}) %collective-permute-start.4) | collective-permute-done | bytes 147488 | tf_op jit(solution)/shard_map/ppermute | solution.py:505
  74.1 3.3 %collective-permute-start.5 = (f32[8,1152]{1,0:T(8,128)S(1)}, f32[8,1152]{1,0:T(8,128)S(1)}, u32[]{:S(2)}, u32[]{:S(2)}) collective-permute-start(f32[8,1152]{1,0:T(8,128)S(1)} %get-tuple-element.49), channel_id=1, source_target_pairs={{0,2},{2,4},{4,6},{6,0},{1,3},{3,5},{5,7},{7,1},{8,10},{10,12},{12... | collective-permute-start | bytes 110600 | tf_op jit(solution)/shard_map/ppermute | solution.py:514
  77.4 4.5 %collective-permute-start.6 = (f32[8,1152]{1,0:T(8,128)S(1)}, f32[8,1152]{1,0:T(8,128)S(1)}, u32[]{:S(2)}, u32[]{:S(2)}) collective-permute-start(f32[8,1152]{1,0:T(8,128)S(1)} %get-tuple-element.50), channel_id=1, source_target_pairs={{0,4},{2,6},{4,0},{6,2},{1,5},{3,7},{5,1},{7,3},{8,12},{10,14},{12... | collective-permute-start | bytes 110600 | tf_op jit(solution)/shard_map/ppermute | solution.py:514
  81.9 2.7 %collective-permute-start.7 = (f32[8,1152]{1,0:T(8,128)S(1)}, f32[8,1152]{1,0:T(8,128)S(1)}, u32[]{:S(2)}, u32[]{:S(2)}) collective-permute-start(f32[8,1152]{1,0:T(8,128)S(1)} %get-tuple-element.51), channel_id=1, source_target_pairs={{0,6},{2,0},{4,2},{6,4},{1,7},{3,1},{5,3},{7,5},{8,14},{10,8},{12,... | collective-permute-start | bytes 110600 | tf_op jit(solution)/shard_map/ppermute | solution.py:514
  84.6 0.9 collective-permute-done.6.refs_2_
  85.5 1.8 %collective-permute-done.7.refs_3_ = f32[8,1152]{1,0:T(8,128)S(1)} collective-permute-done((f32[8,1152]{1,0:T(8,128)S(1)}, f32[8,1152]{1,0:T(8,128)S(1)}, u32[]{:S(2)}, u32[]{:S(2)}) %collective-permute-start.7) | collective-permute-done | bytes 36896 | tf_op jit(solution)/shard_map/ppermute | solution.py:514
  87.3 10.0 %all_to_all.22.in_ref = f32[8,8,1152]{2,1,0:T(8,128)S(1)} all-to-all(f32[8,8,1152]{2,1,0:T(8,128)S(1)} %shard_map.147), channel_id=1, replica_groups=mesh['zl'=2,'y'=4,'x'=4,'zh'=4,'c'=2] {'zl','y'}, dimensions={0} | all-to-all | bytes 589824 | tf_op jit(solution)/shard_map/all_to_all | solution.py:518
  97.3 0.8 shard_map.148
  (22 shorter events, 0.1 us)
Async XLA Ops:
  6.8 14.6 %all-to-all-start = ((f32[8,100,128]{2,1,0:T(8,128)}), f32[8,100,128]{2,1,0:T(8,128)S(1)}, u32[]{:S(2)}, u32[]{:S(2)}) async-start(f32[8,100,128]{2,1,0:T(8,128)} %shard_map.136.x_hbm), calls=%async_computation | async-start | bytes 851968 | tf_op jit(solution)/shard_map/all_to_all | solution.py:412
  12.6 8.8 %copy-start.5 = (f32[100,1024]{1,0:T(8,128)S(1)}, f32[100,1024]{1,0:T(8,128)}, u32[]{:S(2)}) copy-start(f32[100,1024]{1,0:T(8,128)} %goal_hbm.1) | copy-start | bytes 1228804
  12.6 8.8 %copy-start.6 = (s32[1024]{0:T(1024)S(1)}, s32[1024]{0:T(1024)}, u32[]{:S(2)}) copy-start(s32[1024]{0:T(1024)} %param.11) | copy-start | bytes 12292
  12.7 8.7 %copy-start.7 = (f32[721]{0:T(1024)S(1)}, f32[721]{0:T(1024)}, u32[]{:S(2)}) copy-start(f32[721]{0:T(1024)} %table_hbm.1) | copy-start | bytes 8656
  12.7 8.7 %copy-start.8 = (f32[100]{0:T(128)S(1)}, f32[100]{0:T(128)}, u32[]{:S(2)}) copy-start(f32[100]{0:T(128)} %param.13) | copy-start | bytes 1204
  21.4 0.7 copy-start.9
  22.1 15.0 %copy-start = (bf16[1,1024,1024]{2,1,0:T(8,128)(2,1)S(1)}, bf16[1,1024,1024]{2,1,0:T(8,128)(2,1)}, u32[]{:S(2)}) copy-start(bf16[1,1024,1024]{2,1,0:T(8,128)(2,1)} %param.9) | copy-start | bytes 6291460
  22.1 15.0 %copy-start.1 = (bf16[1024,1024]{1,0:T(8,128)(2,1)S(1)}, bf16[1024,1024]{1,0:T(8,128)(2,1)}, u32[]{:S(2)}) copy-start(bf16[1024,1024]{1,0:T(8,128)(2,1)} %get-tuple-element.34.g_ref) | copy-start | bytes 6291460
  22.1 15.0 %copy-start.3 = (bf16[1024,100]{0,1:T(8,128)(2,1)S(1)}, bf16[1024,100]{0,1:T(8,128)(2,1)}, u32[]{:S(2)}) copy-start(bf16[1024,100]{0,1:T(8,128)(2,1)} %param.16) | copy-start | bytes 614404
  37.1 1.6 %copy-start.2 = (bf16[1024,1024]{1,0:T(8,128)(2,1)S(1)}, bf16[1024,1024]{1,0:T(8,128)(2,1)}, u32[]{:S(2)}) copy-start(bf16[1024,1024]{1,0:T(8,128)(2,1)} %get-tuple-element.38.z_ref) | copy-start | bytes 6291460
  38.2 2.7 %collective-permute-start = (f32[4,4,4,8,512]{4,3,2,1,0:T(8,128)S(1)}, f32[4,4,4,8,512]{4,3,2,1,0:T(8,128)S(1)}, u32[]{:S(2)}, u32[]{:S(2)}) collective-permute-start(f32[4,4,4,8,512]{4,3,2,1,0:T(8,128)S(1)} %get-tuple-element.40), channel_id=1, source_target_pairs={{0,1},{1,0},{2,3},{3,2},{4,5},{5,4},{6,7},{7,6},{8,9},{9,8},{10,11... | collective-permute-start | bytes 3145736 | tf_op jit(solution)/shard_map/ppermute | solution.py:458
  40.9 3.0 %collective-permute-start.1 = (f32[4,4,4,8,640]{4,3,2,1,0:T(8,128)S(1)}, f32[4,4,4,8,640]{4,3,2,1,0:T(8,128)S(1)}, u32[]{:S(2)}, u32[]{:S(2)}) collective-permute-start(f32[4,4,4,8,640]{4,3,2,1,0:T(8,128)S(1)} %shard_map.142), channel_id=1, source_target_pairs={{0,1},{1,0},{2,3},{3,2},{4,5},{5,4},{6,7},{7,6},{8,9},{9,8},{10,11... | collective-permute-start | bytes 3932168 | tf_op jit(solution)/shard_map/ppermute | solution.py:479
  64.5 4.9 %copy-start.4 = (bf16[1024,1024]{1,0:T(8,128)(2,1)S(1)}, bf16[1024,1024]{1,0:T(8,128)(2,1)}, u32[]{:S(2)}) copy-start(bf16[1024,1024]{1,0:T(8,128)(2,1)} %w_ref.1) | copy-start | bytes 6291460
  64.6 8.2 %collective-permute-start.2 = (f32[32,1152]{1,0:T(8,128)S(1)}, f32[32,1152]{1,0:T(8,128)S(1)}, u32[]{:S(2)}, u32[]{:S(2)}) collective-permute-start(f32[32,1152]{1,0:T(8,128)S(1)} %get-tuple-element.45), channel_id=1, source_target_pairs={{0,8},{8,16},{16,24},{24,0},{32,40},{40,48},{48,56},{56,32},{64,72... | collective-permute-start | bytes 442376 | tf_op jit(solution)/shard_map/ppermute | solution.py:505
  66.2 6.8 %collective-permute-start.3 = (f32[32,1152]{1,0:T(8,128)S(1)}, f32[32,1152]{1,0:T(8,128)S(1)}, u32[]{:S(2)}, u32[]{:S(2)}) collective-permute-start(f32[32,1152]{1,0:T(8,128)S(1)} %get-tuple-element.46), channel_id=1, source_target_pairs={{0,16},{8,24},{16,0},{24,8},{32,48},{40,56},{48,32},{56,40},{64,80... | collective-permute-start | bytes 442376 | tf_op jit(solution)/shard_map/ppermute | solution.py:505
  67.3 6.7 %collective-permute-start.4 = (f32[32,1152]{1,0:T(8,128)S(1)}, f32[32,1152]{1,0:T(8,128)S(1)}, u32[]{:S(2)}, u32[]{:S(2)}) collective-permute-start(f32[32,1152]{1,0:T(8,128)S(1)} %get-tuple-element.47), channel_id=1, source_target_pairs={{0,24},{8,0},{16,8},{24,16},{32,56},{40,32},{48,40},{56,48},{64,88... | collective-permute-start | bytes 442376 | tf_op jit(solution)/shard_map/ppermute | solution.py:505
  74.1 10.5 %collective-permute-start.5 = (f32[8,1152]{1,0:T(8,128)S(1)}, f32[8,1152]{1,0:T(8,128)S(1)}, u32[]{:S(2)}, u32[]{:S(2)}) collective-permute-start(f32[8,1152]{1,0:T(8,128)S(1)} %get-tuple-element.49), channel_id=1, source_target_pairs={{0,2},{2,4},{4,6},{6,0},{1,3},{3,5},{5,7},{7,1},{8,10},{10,12},{12... | collective-permute-start | bytes 110600 | tf_op jit(solution)/shard_map/ppermute | solution.py:514
  77.4 8.1 %collective-permute-start.6 = (f32[8,1152]{1,0:T(8,128)S(1)}, f32[8,1152]{1,0:T(8,128)S(1)}, u32[]{:S(2)}, u32[]{:S(2)}) collective-permute-start(f32[8,1152]{1,0:T(8,128)S(1)} %get-tuple-element.50), channel_id=1, source_target_pairs={{0,4},{2,6},{4,0},{6,2},{1,5},{3,7},{5,1},{7,3},{8,12},{10,14},{12... | collective-permute-start | bytes 110600 | tf_op jit(solution)/shard_map/ppermute | solution.py:514
  81.9 5.4 %collective-permute-start.7 = (f32[8,1152]{1,0:T(8,128)S(1)}, f32[8,1152]{1,0:T(8,128)S(1)}, u32[]{:S(2)}, u32[]{:S(2)}) collective-permute-start(f32[8,1152]{1,0:T(8,128)S(1)} %get-tuple-element.51), channel_id=1, source_target_pairs={{0,6},{2,0},{4,2},{6,4},{1,7},{3,1},{5,3},{7,5},{8,14},{10,8},{12,... | collective-permute-start | bytes 110600 | tf_op jit(solution)/shard_map/ppermute | solution.py:514

commit v5 on v4

--- a/solution.py
+++ b/solution.py
@@ -319,16 +319,29 @@
         out_refs[d][...] = total
 
 
-def redeal_kernel(axis, done_ref, *refs):
-    n = len(refs) // 2
-    me = lax.axis_index(axis)
-    rows = refs[n].shape[0]
-    for d in range(n):
-        here = pl.ds(pl.multiple_of(lax.rem(me + d, n) * rows, rows), rows)
-        total = refs[0][here, :]
-        for i in range(1, n):
-            total = total + refs[i][here, :]
-        refs[n + d][...] = total
+def partner(me, d):
+    low, high = lax.rem(me, 2), me // 2
+    low = 1 - low if d % 2 else low
+    high = 1 - high if d // 2 else high
+    return 2 * high + low
+
+
+def halve_kernel(done_ref, *refs):
+    ins, (keep_ref, send_ref) = refs[:-2], refs[-2:]
+    me = lax.axis_index("zh")
+    rows = keep_ref.shape[0] // 2
+    for i, d in enumerate((0, 3, 1, 2)):
+        here = pl.ds(pl.multiple_of(partner(me, d) * rows, rows), rows)
+        total = ins[0][here, :]
+        for r in ins[1:]:
+            total = total + r[here, :]
+        (keep_ref, send_ref)[i // 2][(i % 2) * rows : (i % 2 + 1) * rows, :] = total
+
+
+def quarter_kernel(keep_ref, other_ref, own_ref, send_ref):
+    rows = own_ref.shape[0]
+    own_ref[...] = keep_ref[:rows, :] + other_ref[:rows, :]
+    send_ref[...] = keep_ref[rows:, :] + other_ref[rows:, :]
 
 
 def spread_kernel(*refs):
@@ -504,17 +517,15 @@
     blocks = (blocks[0],) + tuple(
         lax.ppermute(blocks[d], plane, shifts(ny, nx, d)) for d in range(1, nx)
     )
-    blocks = call(
-        functools.partial(redeal_kernel, "zh"),
-        (shape((rows, wide), f32),) * nzh,
-        [near] * (1 + nx),
-        (near,) * nzh,
+    keep, send = call(
+        halve_kernel, (shape((2 * rows, wide), f32),) * 2, [near] * (1 + nx), (near,) * 2
     )(built, *blocks)
-    blocks = (blocks[0],) + tuple(
-        lax.ppermute(blocks[d], "zh", [(i, (i + d) % nzh) for i in range(nzh)])
-        for d in range(1, nzh)
+    send = lax.ppermute(send, "zh", [(i, i ^ 1) for i in range(nzh)])
+    keep, send = call(quarter_kernel, (shape((rows, wide), f32),) * 2, [near] * 2, (near,) * 2)(
+        keep, send
     )
-    whole = call(spread_kernel, shape((members, rows, wide), f32), [near] * nzh, near)(*blocks)
+    blocks = (keep, lax.ppermute(send, "zh", [(i, i ^ 3) for i in range(nzh)]))
+    whole = call(spread_kernel, shape((members, rows, wide), f32), [near] * 2, near)(*blocks)
     whole = lax.all_to_all(whole, ens, 0, 0)
     total_points = columns * lax.axis_size(space)
     factor = 1.0 / math.sqrt(members * total_points)

time: 98.5 us -> 98.7 us (level)
  starting transfers between devices: 21.4 us -> 18.6 us
  waiting for transfers between devices: 6.37 us -> 8.73 us
    ppermute x3 -> x2, starting transfers between devices: 10.5 us -> 7.69 us  [the longest x1 4.35 us: on_device(): blocks = (keep, lax.ppermute(send, 'zh', [(i, i ^ 3) for i in range(nzh)]))]
    ppermute x3 -> x2, waiting for transfers between devices: 2.69 us -> 5.06 us  [the longest x1 3.12 us: on_device(): send = lax.ppermute(send, 'zh', [(i, i ^ 1) for i in range(nzh)])]
  transfers between devices with their start and end apart: 9 -> 8, of which waited for: 7 -> 7; matrix products, arithmetic and copies ran while one was open for 0% -> 0% of each run, Pallas kernels for 15% -> 15%
where the time goes in v5:
time: 98.7 us; the launch traced here: 97.8 us
  blocking collectives  44.2 us (45%)
  Pallas kernels  24.3 us (25%)
  starting transfers between devices  18.6 us (19%)
  waiting for transfers between devices  8.73 us (9%)
  local copies, waits for them, and re-layouts  1.14 us (1%)
    all_to_all x1, blocking collectives, on_device(): half = lax.all_to_all(half, plane, 0, 0, axis_index_groups=lines(ny, nx))  20.4 us
    all_to_all x1, blocking collectives, on_device(): back = lax.all_to_all(dx, ens, 0, 0)  13.8 us
    all_to_all x1, blocking collectives, on_device(): whole = lax.all_to_all(whole, ens, 0, 0)  10 us
    pallas_call x1, Pallas kernels, on_device(): call(again_kernel, (shape(square, bf16), shape(square, bf16), shape((8, l...  8.34 us
    pallas_call x1, Pallas kernels, on_device(): call(forward_kernel, shape((members, variables, slab), f32), [hbm] * 5, n...  6.16 us
    all_to_all x1, starting transfers between devices, on_device(): fields = lax.all_to_all(mine, ens, 0, 0)  5.83 us
    ppermute x3, starting transfers between devices, on_device(): lax.ppermute(blocks[d], plane, shifts(ny, nx, d))  4.83 us
    ppermute x1, starting transfers between devices, on_device(): blocks = (keep, lax.ppermute(send, 'zh', [(i, i ^ 3) for i in range(nzh)]))  4.35 us
  transfers between devices with their start and end apart: 8, of which 7 were waited for; matrix products, arithmetic and copies ran while one was open for 0% of the time, Pallas kernels for 15%

profile of v5, /device:TPU:2, one launch (start us, length us, event | category | flops | bytes accessed | tf_op | source)
XLA Modules:
  0.0 97.8 jit_solution(17104496916077827138)
XLA Ops:
  0.6 6.2 %shard_map.136.x_hbm = f32[8,100,128]{2,1,0:T(8,128)} custom-call(bf16[1024,1024]{1,0:T(8,128)(2,1)} %bitcast.11, bf16[1024,1024]{1,0:T(8,128)(2,1)} %w_ref.1, f32[1,1024]{1,0:T(1,128)} %bitcast.21, bf16[100,1024]{1,0:T(8,128)(2,1)} %bitcast.16, f32[1,100]{1,0:T(1,128)} %bitcast.23), custom_call_target="tpu_custom_call" | custom-call | flops 2147483648 | bytes 4194304 | tf_op jit(solution)/shard_map/pallas_call | solution.py:407
  6.8 5.8 %all-to-all-start = ((f32[8,100,128]{2,1,0:T(8,128)}), f32[8,100,128]{2,1,0:T(8,128)S(1)}, u32[]{:S(2)}, u32[]{:S(2)}) async-start(f32[8,100,128]{2,1,0:T(8,128)} %shard_map.136.x_hbm), calls=%async_computation | async-start | bytes 851968 | tf_op jit(solution)/shard_map/all_to_all | solution.py:425
  12.7 0.0 copy-start.7
  12.7 0.0 copy-start.8
  12.7 8.3 %shard_map.137 = (bf16[1024,1024]{1,0:T(8,128)(2,1)}, bf16[1024,1024]{1,0:T(8,128)(2,1)}, f32[8,128]{1,0:T(8,128)}) custom-call(f32[8,100,128]{2,1,0:T(8,128)} %shard_map.136.x_hbm, bf16[1024,1024]{1,0:T(8,128)(2,1)} %bitcast.12, bf16[1024,1024]{1,0:T(8,128)(2,1)} %w_ref.1, f32[1,1024]{1,0:T(1,128)} %bitcast.22), custom_call_target="tpu_custom_call" | custom-call | flops 2147483648 | bytes 4194304 | tf_op jit(solution)/shard_map/pallas_call | solution.py:426
  21.0 0.4 all-to-all-done.x_ref
  21.4 0.7 copy-done.9
  22.1 1.2 %shard_map.138 = (f32[8,100,128]{2,1,0:T(8,128)S(1)}, f32[32,128]{1,0:T(8,128)S(1)}) custom-call(f32[8,128]{1,0:T(8,128)S(1)} %copy-done.9, f32[8,100,128]{2,1,0:T(8,128)S(1)} %all-to-all-done.x_ref, f32[100,1024]{1,0:T(8,128)S(1)} %copy-done.5, s32[1,1024]{1,0:T(1,128)S(1)} %bitcast.19, f32[721]{0:T(1024)S(1)} %copy-done.7, f32[1,100]{1,0:T(1,128)S(1)} %bitcast.20), custom_call_target="tpu_custom_call" | custom-call | flops 17179869184 | bytes 4194304 | tf_op jit(solution)/shard_map/pallas_call | solution.py:445
  23.3 13.8 %all_to_all.20.back_ref = f32[8,100,128]{2,1,0:T(8,128)S(1)} all-to-all(f32[8,100,128]{2,1,0:T(8,128)S(1)} %get-tuple-element.33), channel_id=1, replica_groups=mesh['zl'=2,'y'=4,'x'=4,'zh'=4,'c'=2] {'zl','y'}, dimensions={0} | all-to-all | bytes 819200 | tf_op jit(solution)/shard_map/all_to_all | solution.py:460
  37.1 1.1 %shard_map.139 = (bf16[512,1024]{1,0:T(8,128)(2,1)S(1)}, bf16[128,1024]{1,0:T(8,128)(2,1)S(1)}, f32[4,4,4,8,512]{4,3,2,1,0:T(8,128)S(1)}) custom-call(f32[8,100,128]{2,1,0:T(8,128)S(1)} %all_to_all.20.back_ref, bf16[100,1024]{1,0:T(8,128)(2,1)S(1)} %bitcast.17, bf16[1024,1024]{1,0:T(8,128)(2,1)S(1)} %copy-done.1, bf16[16,2,32,1024]{3,2,1,0:T(8,128)(2,1)S(1)} %bitcast.13), custom_call_target="tpu_custom_call" | custom-call | flops 536870912 | bytes 4194304 | tf_op jit(solution)/shard_map/pallas_call | solution.py:464
  38.2 0.1 collective-permute-start
  38.3 0.4 copy-done.2
  38.7 1.8 %shard_map.140 = (bf16[512,1024]{1,0:T(8,128)(2,1)S(1)}, f32[4,4,4,8,640]{4,3,2,1,0:T(8,128)S(1)}, f32[4,4,4,8,128]{4,3,2,1,0:T(8,128)S(1)}) custom-call(bf16[512,1024]{1,0:T(8,128)(2,1)S(1)} %get-tuple-element.35.d1_ref, bf16[128,1024]{1,0:T(8,128)(2,1)S(1)} %get-tuple-element.36.dx_ref, bf16[100,1024]{1,0:T(8,128)(2,1)S(1)} %bitcast.18, ...), custom_call_target="tpu_custom_call" | custom-call | flops 536870912 | bytes 4194304 | tf_op jit(solution)/shard_map/pallas_call | solution.py:472
  40.4 0.5 collective-permute-done.left_ref
  40.9 0.1 collective-permute-start.1
  41.0 1.3 %shard_map.141.own_ref = f32[4,4,4,8,1024]{4,3,2,1,0:T(8,128)S(1)} custom-call(bf16[512,1024]{1,0:T(8,128)(2,1)S(1)} %get-tuple-element.35.d1_ref, bf16[512,1024]{1,0:T(8,128)(2,1)S(1)} %get-tuple-element.39.d2_ref, bf16[16,2,32,1024]{3,2,1,0:T(8,128)(2,1)S(1)} %bitcast.15, f32[4,4,4,8,512]{4,3,2,1,0:T(8,128)S(1)} %collective-permute-done.left_ref), custom_call_target="tpu_custom_call" | custom-call | bytes 4194304 | tf_op jit(solution)/shard_map/pallas_call | solution.py:493
  42.3 1.6 %collective-permute-done.1.right_ref = f32[4,4,4,8,640]{4,3,2,1,0:T(8,128)S(1)} collective-permute-done((f32[4,4,4,8,640]{4,3,2,1,0:T(8,128)S(1)}, f32[4,4,4,8,640]{4,3,2,1,0:T(8,128)S(1)}, u32[]{:S(2)}, u32[]{:S(2)}) %collective-permute-start.1) | collective-permute-done | bytes 1310752 | tf_op jit(solution)/shard_map/ppermute | solution.py:492
  43.9 0.2 shard_map.143
  44.1 20.4 %all_to_all.21.in_ref = f32[4,4,32,1152]{3,2,1,0:T(8,128)S(1)} all-to-all(f32[4,4,32,1152]{3,2,1,0:T(8,128)S(1)} %shard_map.143), channel_id=1, replica_groups={{0,32,64,96},{8,40,72,104},{16,48,80,112},{24,56,88,120},{1,9,17,25},{3..., dimensions={0} | all-to-all | bytes 4718592 | tf_op jit(solution)/shard_map/all_to_all | solution.py:502
  64.5 0.1 shard_map.144
  64.6 1.6 %collective-permute-start.2 = (f32[32,1152]{1,0:T(8,128)S(1)}, f32[32,1152]{1,0:T(8,128)S(1)}, u32[]{:S(2)}, u32[]{:S(2)}) collective-permute-start(f32[32,1152]{1,0:T(8,128)S(1)} %get-tuple-element.45), channel_id=1, source_target_pairs={{0,8},{8,16},{16,24},{24,0},{32,40},{40,48},{48,56},{56,32},{64,72... | collective-permute-start | bytes 442376 | tf_op jit(solution)/shard_map/ppermute | solution.py:518
  66.2 1.1 %collective-permute-start.3 = (f32[32,1152]{1,0:T(8,128)S(1)}, f32[32,1152]{1,0:T(8,128)S(1)}, u32[]{:S(2)}, u32[]{:S(2)}) collective-permute-start(f32[32,1152]{1,0:T(8,128)S(1)} %get-tuple-element.46), channel_id=1, source_target_pairs={{0,16},{8,24},{16,0},{24,8},{32,48},{40,56},{48,32},{56,40},{64,80... | collective-permute-start | bytes 442376 | tf_op jit(solution)/shard_map/ppermute | solution.py:518
  67.3 2.1 %collective-permute-start.4 = (f32[32,1152]{1,0:T(8,128)S(1)}, f32[32,1152]{1,0:T(8,128)S(1)}, u32[]{:S(2)}, u32[]{:S(2)}) collective-permute-start(f32[32,1152]{1,0:T(8,128)S(1)} %get-tuple-element.47), channel_id=1, source_target_pairs={{0,24},{8,0},{16,8},{24,16},{32,56},{40,32},{48,40},{56,48},{64,88... | collective-permute-start | bytes 442376 | tf_op jit(solution)/shard_map/ppermute | solution.py:518
  69.5 3.3 %shard_map.145 = (bf16[1024,1024]{1,0:T(8,128)(2,1)}, f32[8,128]{1,0:T(8,128)S(1)}) custom-call(f32[32,1152]{1,0:T(8,128)S(1)} %get-tuple-element.43.late_ref.refs_0_, bf16[512,1024]{1,0:T(8,128)(2,1)S(1)} %get-tuple-element.35.d1_ref, bf16[512,1024]{1,0:T(8,128)(2,1)S(1)} %get-tuple-element.39.d2_ref, bf16[1024,1024]{1,0:T(8,128)(2,1)S(1)} %copy-done.4), custom_call_target="tpu_custom_call" | custom-call | flops 2147483648 | bytes 4194304 | tf_op jit(solution)/shard_map/pallas_call | solution.py:509
  72.8 0.1 collective-permute-done.3.refs_2_
  73.0 1.1 %collective-permute-done.4.refs_3_ = f32[32,1152]{1,0:T(8,128)S(1)} collective-permute-done((f32[32,1152]{1,0:T(8,128)S(1)}, f32[32,1152]{1,0:T(8,128)S(1)}, u32[]{:S(2)}, u32[]{:S(2)}) %collective-permute-start.4) | collective-permute-done | bytes 147488 | tf_op jit(solution)/shard_map/ppermute | solution.py:518
  74.1 3.3 %collective-permute-start.5 = (f32[16,1152]{1,0:T(8,128)S(1)}, f32[16,1152]{1,0:T(8,128)S(1)}, u32[]{:S(2)}, u32[]{:S(2)}) collective-permute-start(f32[16,1152]{1,0:T(8,128)S(1)} %get-tuple-element.49), channel_id=1, source_target_pairs={{0,2},{2,0},{4,6},{6,4},{1,3},{3,1},{5,7},{7,5},{8,10},{10,8},{12,... | collective-permute-start | bytes 221192 | tf_op jit(solution)/shard_map/ppermute | solution.py:523
  77.4 3.1 %collective-permute-done.5.other_ref = f32[16,1152]{1,0:T(8,128)S(1)} collective-permute-done((f32[16,1152]{1,0:T(8,128)S(1)}, f32[16,1152]{1,0:T(8,128)S(1)}, u32[]{:S(2)}, u32[]{:S(2)}) %collective-permute-start.5) | collective-permute-done | bytes 73760 | tf_op jit(solution)/shard_map/ppermute | solution.py:523
  80.6 4.3 %collective-permute-start.6 = (f32[8,1152]{1,0:T(8,128)S(1)}, f32[8,1152]{1,0:T(8,128)S(1)}, u32[]{:S(2)}, u32[]{:S(2)}) collective-permute-start(f32[8,1152]{1,0:T(8,128)S(1)} %get-tuple-element.51), channel_id=1, source_target_pairs={{0,6},{2,4},{4,2},{6,0},{1,7},{3,5},{5,3},{7,1},{8,14},{10,12},{12... | collective-permute-start | bytes 110600 | tf_op jit(solution)/shard_map/ppermute | solution.py:527
  84.9 1.9 %collective-permute-done.6.refs_1_ = f32[8,1152]{1,0:T(8,128)S(1)} collective-permute-done((f32[8,1152]{1,0:T(8,128)S(1)}, f32[8,1152]{1,0:T(8,128)S(1)}, u32[]{:S(2)}, u32[]{:S(2)}) %collective-permute-start.6) | collective-permute-done | bytes 36896 | tf_op jit(solution)/shard_map/ppermute | solution.py:527
  86.9 10.0 %all_to_all.22.in_ref = f32[8,8,1152]{2,1,0:T(8,128)S(1)} all-to-all(f32[8,8,1152]{2,1,0:T(8,128)S(1)} %shard_map.148), channel_id=1, replica_groups=mesh['zl'=2,'y'=4,'x'=4,'zh'=4,'c'=2] {'zl','y'}, dimensions={0} | all-to-all | bytes 589824 | tf_op jit(solution)/shard_map/all_to_all | solution.py:529
  96.9 0.8 shard_map.149
  (21 shorter events, 0.1 us)
Async XLA Ops:
  6.8 14.6 %all-to-all-start = ((f32[8,100,128]{2,1,0:T(8,128)}), f32[8,100,128]{2,1,0:T(8,128)S(1)}, u32[]{:S(2)}, u32[]{:S(2)}) async-start(f32[8,100,128]{2,1,0:T(8,128)} %shard_map.136.x_hbm), calls=%async_computation | async-start | bytes 851968 | tf_op jit(solution)/shard_map/all_to_all | solution.py:425
  12.6 8.8 %copy-start.5 = (f32[100,1024]{1,0:T(8,128)S(1)}, f32[100,1024]{1,0:T(8,128)}, u32[]{:S(2)}) copy-start(f32[100,1024]{1,0:T(8,128)} %goal_hbm.1) | copy-start | bytes 1228804
  12.6 8.8 %copy-start.6 = (s32[1024]{0:T(1024)S(1)}, s32[1024]{0:T(1024)}, u32[]{:S(2)}) copy-start(s32[1024]{0:T(1024)} %param.11) | copy-start | bytes 12292
  12.7 8.7 %copy-start.7 = (f32[721]{0:T(1024)S(1)}, f32[721]{0:T(1024)}, u32[]{:S(2)}) copy-start(f32[721]{0:T(1024)} %table_hbm.1) | copy-start | bytes 8656
  12.7 8.7 %copy-start.8 = (f32[100]{0:T(128)S(1)}, f32[100]{0:T(128)}, u32[]{:S(2)}) copy-start(f32[100]{0:T(128)} %param.13) | copy-start | bytes 1204
  21.4 0.7 copy-start.9
  22.1 15.0 %copy-start = (bf16[1,1024,1024]{2,1,0:T(8,128)(2,1)S(1)}, bf16[1,1024,1024]{2,1,0:T(8,128)(2,1)}, u32[]{:S(2)}) copy-start(bf16[1,1024,1024]{2,1,0:T(8,128)(2,1)} %param.9) | copy-start | bytes 6291460
  22.1 15.0 %copy-start.1 = (bf16[1024,1024]{1,0:T(8,128)(2,1)S(1)}, bf16[1024,1024]{1,0:T(8,128)(2,1)}, u32[]{:S(2)}) copy-start(bf16[1024,1024]{1,0:T(8,128)(2,1)} %get-tuple-element.34.g_ref) | copy-start | bytes 6291460
  22.1 15.0 %copy-start.3 = (bf16[1024,100]{0,1:T(8,128)(2,1)S(1)}, bf16[1024,100]{0,1:T(8,128)(2,1)}, u32[]{:S(2)}) copy-start(bf16[1024,100]{0,1:T(8,128)(2,1)} %param.16) | copy-start | bytes 614404
  37.1 1.6 %copy-start.2 = (bf16[1024,1024]{1,0:T(8,128)(2,1)S(1)}, bf16[1024,1024]{1,0:T(8,128)(2,1)}, u32[]{:S(2)}) copy-start(bf16[1024,1024]{1,0:T(8,128)(2,1)} %get-tuple-element.38.z_ref) | copy-start | bytes 6291460
  38.2 2.7 %collective-permute-start = (f32[4,4,4,8,512]{4,3,2,1,0:T(8,128)S(1)}, f32[4,4,4,8,512]{4,3,2,1,0:T(8,128)S(1)}, u32[]{:S(2)}, u32[]{:S(2)}) collective-permute-start(f32[4,4,4,8,512]{4,3,2,1,0:T(8,128)S(1)} %get-tuple-element.40), channel_id=1, source_target_pairs={{0,1},{1,0},{2,3},{3,2},{4,5},{5,4},{6,7},{7,6},{8,9},{9,8},{10,11... | collective-permute-start | bytes 3145736 | tf_op jit(solution)/shard_map/ppermute | solution.py:471
  40.9 3.0 %collective-permute-start.1 = (f32[4,4,4,8,640]{4,3,2,1,0:T(8,128)S(1)}, f32[4,4,4,8,640]{4,3,2,1,0:T(8,128)S(1)}, u32[]{:S(2)}, u32[]{:S(2)}) collective-permute-start(f32[4,4,4,8,640]{4,3,2,1,0:T(8,128)S(1)} %shard_map.142), channel_id=1, source_target_pairs={{0,1},{1,0},{2,3},{3,2},{4,5},{5,4},{6,7},{7,6},{8,9},{9,8},{10,11... | collective-permute-start | bytes 3932168 | tf_op jit(solution)/shard_map/ppermute | solution.py:492
  64.5 4.9 %copy-start.4 = (bf16[1024,1024]{1,0:T(8,128)(2,1)S(1)}, bf16[1024,1024]{1,0:T(8,128)(2,1)}, u32[]{:S(2)}) copy-start(bf16[1024,1024]{1,0:T(8,128)(2,1)} %w_ref.1) | copy-start | bytes 6291460
  64.6 8.2 %collective-permute-start.2 = (f32[32,1152]{1,0:T(8,128)S(1)}, f32[32,1152]{1,0:T(8,128)S(1)}, u32[]{:S(2)}, u32[]{:S(2)}) collective-permute-start(f32[32,1152]{1,0:T(8,128)S(1)} %get-tuple-element.45), channel_id=1, source_target_pairs={{0,8},{8,16},{16,24},{24,0},{32,40},{40,48},{48,56},{56,32},{64,72... | collective-permute-start | bytes 442376 | tf_op jit(solution)/shard_map/ppermute | solution.py:518
  66.2 6.8 %collective-permute-start.3 = (f32[32,1152]{1,0:T(8,128)S(1)}, f32[32,1152]{1,0:T(8,128)S(1)}, u32[]{:S(2)}, u32[]{:S(2)}) collective-permute-start(f32[32,1152]{1,0:T(8,128)S(1)} %get-tuple-element.46), channel_id=1, source_target_pairs={{0,16},{8,24},{16,0},{24,8},{32,48},{40,56},{48,32},{56,40},{64,80... | collective-permute-start | bytes 442376 | tf_op jit(solution)/shard_map/ppermute | solution.py:518
  67.3 6.7 %collective-permute-start.4 = (f32[32,1152]{1,0:T(8,128)S(1)}, f32[32,1152]{1,0:T(8,128)S(1)}, u32[]{:S(2)}, u32[]{:S(2)}) collective-permute-start(f32[32,1152]{1,0:T(8,128)S(1)} %get-tuple-element.47), channel_id=1, source_target_pairs={{0,24},{8,0},{16,8},{24,16},{32,56},{40,32},{48,40},{56,48},{64,88... | collective-permute-start | bytes 442376 | tf_op jit(solution)/shard_map/ppermute | solution.py:518
  74.1 6.5 %collective-permute-start.5 = (f32[16,1152]{1,0:T(8,128)S(1)}, f32[16,1152]{1,0:T(8,128)S(1)}, u32[]{:S(2)}, u32[]{:S(2)}) collective-permute-start(f32[16,1152]{1,0:T(8,128)S(1)} %get-tuple-element.49), channel_id=1, source_target_pairs={{0,2},{2,0},{4,6},{6,4},{1,3},{3,1},{5,7},{7,5},{8,10},{10,8},{12,... | collective-permute-start | bytes 221192 | tf_op jit(solution)/shard_map/ppermute | solution.py:523
  80.6 6.3 %collective-permute-start.6 = (f32[8,1152]{1,0:T(8,128)S(1)}, f32[8,1152]{1,0:T(8,128)S(1)}, u32[]{:S(2)}, u32[]{:S(2)}) collective-permute-start(f32[8,1152]{1,0:T(8,128)S(1)} %get-tuple-element.51), channel_id=1, source_target_pairs={{0,6},{2,4},{4,2},{6,0},{1,7},{3,5},{5,3},{7,1},{8,14},{10,12},{12... | collective-permute-start | bytes 110600 | tf_op jit(solution)/shard_map/ppermute | solution.py:527

commit v6 on v4

--- a/solution.py
+++ b/solution.py
@@ -287,39 +287,47 @@
         c.wait()
 
 
-def add_kernel(own_ref, keep_ref, right_ref, out_ref):
+def partner(me, d):
+    low, high = lax.rem(me, 2), me // 2
+    low = 1 - low if d % 2 else low
+    high = 1 - high if d // 2 else high
+    return 2 * high + low
+
+
+def add_kernel(own_ref, keep_ref, right_ref, *out_refs):
     ny, nx, nzh, rows, channels = own_ref.shape
     width = right_ref.shape[4] - keep_ref.shape[4]
     cut = channels - width
-    core = lax.axis_index("c")
-    for y in range(ny):
-        for x in range(nx):
-            a = jnp.where(core == 0, y, x)
-            b = jnp.where(core == 0, x, y)
+    first = lax.axis_index("c") == 0
+    me = jnp.where(first, lax.axis_index("y"), lax.axis_index("x"))
+    for d in range(ny):
+        block = partner(me, d)
+        for b in range(nx):
+            y, x = jnp.where(first, block, b), jnp.where(first, b, block)
             for zh in range(nzh):
                 here = pl.ds(zh * rows, rows)
-                out_ref[a, b, here, :cut] = own_ref[y, x, zh, :, :cut]
-                out_ref[a, b, here, cut:channels] = (
+                out_refs[d][b, here, :cut] = own_ref[y, x, zh, :, :cut]
+                out_refs[d][b, here, cut:channels] = (
                     own_ref[y, x, zh, :, cut:] + right_ref[y, x, zh, :, :width]
                 )
-                out_ref[a, b, here, channels:] = (
+                out_refs[d][b, here, channels:] = (
                     keep_ref[y, x, zh] + right_ref[y, x, zh, :, width:]
                 )
 
 
-def deal_kernel(axes, in_ref, *out_refs):
+def deal_kernel(axes, done_ref, *refs):
+    n = len(refs) // 2
     core = lax.axis_index("c")
     me = jnp.where(core == 0, lax.axis_index(axes[0]), lax.axis_index(axes[1]))
-    n = len(out_refs)
     for d in range(n):
         k = lax.rem(me + d, n)
-        total = in_ref[0, k]
-        for i in range(1, in_ref.shape[0]):
-            total = total + in_ref[i, k]
-        out_refs[d][...] = total
-
-
-def redeal_kernel(axis, done_ref, *refs):
+        total = refs[0][k]
+        for i in range(1, n):
+            total = total + refs[i][k]
+        refs[n + d][...] = total
+
+
+def redeal_kernel(axis, *refs):
     n = len(refs) // 2
     me = lax.axis_index(axis)
     rows = refs[n].shape[0]
@@ -360,11 +368,10 @@
     loss_ref[...] = line[:, variables : variables + 1] * (1.0 / points)
 
 
-def lines(ny, nx):
+def swaps(ny, nx, d):
     at = lambda y, x, c: (y * nx + x) * 2 + c
-    down = [[at(y, x, 0) for y in range(ny)] for x in range(nx)]
-    along = [[at(y, x, 1) for x in range(nx)] for y in range(ny)]
-    return down + along
+    pairs = [(at(y, x, 0), at(y ^ d, x, 0)) for y in range(ny) for x in range(nx)]
+    return pairs + [(at(y, x, 1), at(y, x ^ d, 1)) for y in range(ny) for x in range(nx)]
 
 
 def shifts(ny, nx, d):
@@ -483,16 +490,9 @@
         [near] * 4,
         near,
     )(d1, d2, grouped, left)
-    half = call(
-        add_kernel, shape((ny, nx, nzh * rows, wide), f32), [near] * 3, near
+    blocks = call(
+        add_kernel, (shape((nx, nzh * rows, wide), f32),) * ny, [near] * 3, (near,) * ny
     )(own, keep, right)
-    half = lax.all_to_all(half, plane, 0, 0, axis_index_groups=lines(ny, nx))
-    blocks = call(
-        functools.partial(deal_kernel, ("x", "y")),
-        (shape((nzh * rows, wide), f32),) * nx,
-        [near],
-        (near,) * nx,
-    )(half)
     grad_feat, built = call(
         grad_kernel,
         (shape(square, bf16), shape((8, lanes), f32)),
@@ -501,15 +501,23 @@
         scratch=[pltpu.VMEM(square, bf16), pltpu.VMEM(square, bf16), dma((2,))],
         flops=2 * channels * channels * columns,
     )(blocks[0], d1, d2, w_first)
+    moved = {d: lax.ppermute(blocks[d], plane, swaps(ny, nx, d)) for d in (1, 3, 2)}
+    blocks = (blocks[0],) + tuple(moved[d] for d in range(1, ny))
+    blocks = call(
+        functools.partial(deal_kernel, ("x", "y")),
+        (shape((nzh * rows, wide), f32),) * nx,
+        [near] * (1 + ny),
+        (near,) * nx,
+    )(built, *blocks)
     blocks = (blocks[0],) + tuple(
         lax.ppermute(blocks[d], plane, shifts(ny, nx, d)) for d in range(1, nx)
     )
     blocks = call(
         functools.partial(redeal_kernel, "zh"),
         (shape((rows, wide), f32),) * nzh,
-        [near] * (1 + nx),
+        [near] * nx,
         (near,) * nzh,
-    )(built, *blocks)
+    )(*blocks)
     blocks = (blocks[0],) + tuple(
         lax.ppermute(blocks[d], "zh", [(i, (i + d) % nzh) for i in range(nzh)])
         for d in range(1, nzh)

time: 98.5 us -> 99 us (level)
  blocking collectives: 44.2 us -> 25.2 us
  waiting for transfers between devices: 6.37 us -> 21 us
  starting transfers between devices: 21.4 us -> 26.2 us
    all_to_all x1 -> x0, blocking collectives: 20.4 us -> none  [on_device(): half = lax.all_to_all(half, plane, 0, 0, axis_index_groups=lines(ny, nx))]
    ppermute x0 -> x3, waiting for transfers between devices: none -> 11.9 us  [on_device(): lax.ppermute(blocks[d], plane, swaps(ny, nx, d))]
    ppermute x0 -> x3, starting transfers between devices: none -> 4.79 us  [on_device(): lax.ppermute(blocks[d], plane, swaps(ny, nx, d))]
    ppermute x3, waiting for transfers between devices: 1.24 us -> 4.57 us  [on_device(): lax.ppermute(blocks[d], plane, shifts(ny, nx, d))]
    all_to_all x1, blocking collectives: 10 us -> 11.4 us  [on_device(): whole = lax.all_to_all(whole, ens, 0, 0)]
  transfers between devices with their start and end apart: 9 -> 12, of which waited for: 7 -> 11; matrix products, arithmetic and copies ran while one was open for 0% -> 0% of each run, Pallas kernels for 15% -> 15%
where the time goes in v6:
time: 99 us; the launch traced here: 98.7 us
  starting transfers between devices  26.2 us (26%)
  blocking collectives  25.2 us (25%)
  Pallas kernels  24.4 us (25%)
  waiting for transfers between devices  21 us (21%)
  local copies, waits for them, and re-layouts  1.14 us (1%)
    all_to_all x1, blocking collectives, on_device(): back = lax.all_to_all(dx, ens, 0, 0)  13.8 us
    ppermute x3, waiting for transfers between devices, on_device(): lax.ppermute(blocks[d], plane, swaps(ny, nx, d))  11.9 us
    all_to_all x1, blocking collectives, on_device(): whole = lax.all_to_all(whole, ens, 0, 0)  11.4 us
    ppermute x3, starting transfers between devices, on_device(): lax.ppermute(blocks[d], 'zh', [(i, (i + d) % nzh) for i in range(nzh)])  10.5 us
    pallas_call x1, Pallas kernels, on_device(): call(again_kernel, (shape(square, bf16), shape(square, bf16), shape((8, l...  8.36 us
    pallas_call x1, Pallas kernels, on_device(): call(forward_kernel, shape((members, variables, slab), f32), [hbm] * 5, n...  6.17 us
    all_to_all x1, starting transfers between devices, on_device(): fields = lax.all_to_all(mine, ens, 0, 0)  5.83 us
    ppermute x3, starting transfers between devices, on_device(): lax.ppermute(blocks[d], plane, shifts(ny, nx, d))  4.83 us
  transfers between devices with their start and end apart: 12, of which 11 were waited for; matrix products, arithmetic and copies ran while one was open for 0% of the time, Pallas kernels for 15%

profile of v6, /device:TPU:2, one launch (start us, length us, event | category | flops | bytes accessed | tf_op | source)
XLA Modules:
  0.0 98.7 jit_solution(11505441078741893926)
XLA Ops:
  0.6 6.2 %shard_map.136.x_hbm = f32[8,100,128]{2,1,0:T(8,128)} custom-call(bf16[1024,1024]{1,0:T(8,128)(2,1)} %bitcast.11, bf16[1024,1024]{1,0:T(8,128)(2,1)} %w_ref.1, f32[1,1024]{1,0:T(1,128)} %bitcast.21, bf16[100,1024]{1,0:T(8,128)(2,1)} %bitcast.16, f32[1,100]{1,0:T(1,128)} %bitcast.23), custom_call_target="tpu_custom_call" | custom-call | flops 2147483648 | bytes 4194304 | tf_op jit(solution)/shard_map/pallas_call | solution.py:401
  6.8 5.8 %all-to-all-start = ((f32[8,100,128]{2,1,0:T(8,128)}), f32[8,100,128]{2,1,0:T(8,128)S(1)}, u32[]{:S(2)}, u32[]{:S(2)}) async-start(f32[8,100,128]{2,1,0:T(8,128)} %shard_map.136.x_hbm), calls=%async_computation | async-start | bytes 851968 | tf_op jit(solution)/shard_map/all_to_all | solution.py:419
  12.7 8.4 %shard_map.137 = (bf16[1024,1024]{1,0:T(8,128)(2,1)}, bf16[1024,1024]{1,0:T(8,128)(2,1)}, f32[8,128]{1,0:T(8,128)}) custom-call(f32[8,100,128]{2,1,0:T(8,128)} %shard_map.136.x_hbm, bf16[1024,1024]{1,0:T(8,128)(2,1)} %bitcast.12, bf16[1024,1024]{1,0:T(8,128)(2,1)} %w_ref.1, f32[1,1024]{1,0:T(1,128)} %bitcast.22), custom_call_target="tpu_custom_call" | custom-call | flops 2147483648 | bytes 4194304 | tf_op jit(solution)/shard_map/pallas_call | solution.py:420
  21.4 0.7 copy-done.9
  22.1 1.2 %shard_map.138 = (f32[8,100,128]{2,1,0:T(8,128)S(1)}, f32[32,128]{1,0:T(8,128)S(1)}) custom-call(f32[8,128]{1,0:T(8,128)S(1)} %copy-done.9, f32[8,100,128]{2,1,0:T(8,128)S(1)} %all-to-all-done.x_ref, f32[100,1024]{1,0:T(8,128)S(1)} %copy-done.5, s32[1,1024]{1,0:T(1,128)S(1)} %bitcast.19, f32[721]{0:T(1024)S(1)} %copy-done.7, f32[1,100]{1,0:T(1,128)S(1)} %bitcast.20), custom_call_target="tpu_custom_call" | custom-call | flops 17179869184 | bytes 4194304 | tf_op jit(solution)/shard_map/pallas_call | solution.py:439
  23.3 13.8 %all_to_all.15.back_ref = f32[8,100,128]{2,1,0:T(8,128)S(1)} all-to-all(f32[8,100,128]{2,1,0:T(8,128)S(1)} %get-tuple-element.37), channel_id=1, replica_groups=mesh['zl'=2,'y'=4,'x'=4,'zh'=4,'c'=2] {'zl','y'}, dimensions={0} | all-to-all | bytes 819200 | tf_op jit(solution)/shard_map/all_to_all | solution.py:454
  37.1 1.1 %shard_map.139 = (bf16[512,1024]{1,0:T(8,128)(2,1)S(1)}, bf16[128,1024]{1,0:T(8,128)(2,1)S(1)}, f32[4,4,4,8,512]{4,3,2,1,0:T(8,128)S(1)}) custom-call(f32[8,100,128]{2,1,0:T(8,128)S(1)} %all_to_all.15.back_ref, bf16[100,1024]{1,0:T(8,128)(2,1)S(1)} %bitcast.17, bf16[1024,1024]{1,0:T(8,128)(2,1)S(1)} %copy-done.1, bf16[16,2,32,1024]{3,2,1,0:T(8,128)(2,1)S(1)} %bitcast.13), custom_call_target="tpu_custom_call" | custom-call | flops 536870912 | bytes 4194304 | tf_op jit(solution)/shard_map/pallas_call | solution.py:458
  38.3 0.4 copy-done.2
  38.7 1.8 %shard_map.140 = (bf16[512,1024]{1,0:T(8,128)(2,1)S(1)}, f32[4,4,4,8,640]{4,3,2,1,0:T(8,128)S(1)}, f32[4,4,4,8,128]{4,3,2,1,0:T(8,128)S(1)}) custom-call(bf16[512,1024]{1,0:T(8,128)(2,1)S(1)} %get-tuple-element.39.d1_ref, bf16[128,1024]{1,0:T(8,128)(2,1)S(1)} %get-tuple-element.40.dx_ref, bf16[100,1024]{1,0:T(8,128)(2,1)S(1)} %bitcast.18, ...), custom_call_target="tpu_custom_call" | custom-call | flops 536870912 | bytes 4194304 | tf_op jit(solution)/shard_map/pallas_call | solution.py:466
  40.5 0.5 collective-permute-done.left_ref
  41.1 1.3 %shard_map.141.own_ref = f32[4,4,4,8,1024]{4,3,2,1,0:T(8,128)S(1)} custom-call(bf16[512,1024]{1,0:T(8,128)(2,1)S(1)} %get-tuple-element.39.d1_ref, bf16[512,1024]{1,0:T(8,128)(2,1)S(1)} %get-tuple-element.43.d2_ref, bf16[16,2,32,1024]{3,2,1,0:T(8,128)(2,1)S(1)} %bitcast.15, f32[4,4,4,8,512]{4,3,2,1,0:T(8,128)S(1)} %collective-permute-done.left_ref), custom_call_target="tpu_custom_call" | custom-call | bytes 4194304 | tf_op jit(solution)/shard_map/pallas_call | solution.py:487
  42.4 1.6 %collective-permute-done.1.right_ref = f32[4,4,4,8,640]{4,3,2,1,0:T(8,128)S(1)} collective-permute-done((f32[4,4,4,8,640]{4,3,2,1,0:T(8,128)S(1)}, f32[4,4,4,8,640]{4,3,2,1,0:T(8,128)S(1)}, u32[]{:S(2)}, u32[]{:S(2)}) %collective-permute-start.1) | collective-permute-done | bytes 1310752 | tf_op jit(solution)/shard_map/ppermute | solution.py:486
  44.2 0.5 collective-permute-start.2
  44.7 2.1 %collective-permute-start.3 = (f32[4,32,1152]{2,1,0:T(8,128)S(1)}, f32[4,32,1152]{2,1,0:T(8,128)S(1)}, u32[]{:S(2)}, u32[]{:S(2)}) collective-permute-start(f32[4,32,1152]{2,1,0:T(8,128)S(1)} %get-tuple-element.50), channel_id=1, source_target_pairs={{0,64},{8,72},{16,80},{24,88},{32,96},{40,104},{48,112},{56,120},{... | collective-permute-start | bytes 1769480 | tf_op jit(solution)/shard_map/ppermute | solution.py:504
  46.7 2.2 %collective-permute-start.4 = (f32[4,32,1152]{2,1,0:T(8,128)S(1)}, f32[4,32,1152]{2,1,0:T(8,128)S(1)}, u32[]{:S(2)}, u32[]{:S(2)}) collective-permute-start(f32[4,32,1152]{2,1,0:T(8,128)S(1)} %get-tuple-element.51), channel_id=1, source_target_pairs={{0,96},{8,104},{16,112},{24,120},{32,64},{40,72},{48,80},{56,88},{... | collective-permute-start | bytes 1769480 | tf_op jit(solution)/shard_map/ppermute | solution.py:504
  48.9 3.3 %shard_map.144 = (bf16[1024,1024]{1,0:T(8,128)(2,1)}, f32[8,128]{1,0:T(8,128)S(1)}) custom-call(f32[4,32,1152]{2,1,0:T(8,128)S(1)} %get-tuple-element.47.late_ref.refs_0_, bf16[512,1024]{1,0:T(8,128)(2,1)S(1)} %get-tuple-element.39.d1_ref, bf16[512,1024]{1,0:T(8,128)(2,1)S(1)} %get-tuple-element.43.d2_ref, bf16[1024,1024]{1,0:T(8,128)(2,1)S(1)} %copy-done.4), custom_call_target="tpu_custom_call" | custom-call | flops 2147483648 | bytes 4194304 | tf_op jit(solution)/shard_map/pallas_call | solution.py:496
  52.3 1.8 %collective-permute-done.2.refs_1_ = f32[4,32,1152]{2,1,0:T(8,128)S(1)} collective-permute-done((f32[4,32,1152]{2,1,0:T(8,128)S(1)}, f32[4,32,1152]{2,1,0:T(8,128)S(1)}, u32[]{:S(2)}, u32[]{:S(2)}) %collective-permute-start.2) | collective-permute-done | bytes 589856 | tf_op jit(solution)/shard_map/ppermute | solution.py:504
  54.1 6.9 %collective-permute-done.3.refs_2_ = f32[4,32,1152]{2,1,0:T(8,128)S(1)} collective-permute-done((f32[4,32,1152]{2,1,0:T(8,128)S(1)}, f32[4,32,1152]{2,1,0:T(8,128)S(1)}, u32[]{:S(2)}, u32[]{:S(2)}) %collective-permute-start.3) | collective-permute-done | bytes 589856 | tf_op jit(solution)/shard_map/ppermute | solution.py:504
  61.0 3.1 %collective-permute-done.4.refs_3_ = f32[4,32,1152]{2,1,0:T(8,128)S(1)} collective-permute-done((f32[4,32,1152]{2,1,0:T(8,128)S(1)}, f32[4,32,1152]{2,1,0:T(8,128)S(1)}, u32[]{:S(2)}, u32[]{:S(2)}) %collective-permute-start.4) | collective-permute-done | bytes 589856 | tf_op jit(solution)/shard_map/ppermute | solution.py:504
  64.3 1.6 %collective-permute-start.5 = (f32[32,1152]{1,0:T(8,128)S(1)}, f32[32,1152]{1,0:T(8,128)S(1)}, u32[]{:S(2)}, u32[]{:S(2)}) collective-permute-start(f32[32,1152]{1,0:T(8,128)S(1)} %get-tuple-element.53), channel_id=1, source_target_pairs={{0,8},{8,16},{16,24},{24,0},{32,40},{40,48},{48,56},{56,32},{64,72... | collective-permute-start | bytes 442376 | tf_op jit(solution)/shard_map/ppermute | solution.py:513
  65.8 1.1 %collective-permute-start.6 = (f32[32,1152]{1,0:T(8,128)S(1)}, f32[32,1152]{1,0:T(8,128)S(1)}, u32[]{:S(2)}, u32[]{:S(2)}) collective-permute-start(f32[32,1152]{1,0:T(8,128)S(1)} %get-tuple-element.54), channel_id=1, source_target_pairs={{0,16},{8,24},{16,0},{24,8},{32,48},{40,56},{48,32},{56,40},{64,80... | collective-permute-start | bytes 442376 | tf_op jit(solution)/shard_map/ppermute | solution.py:513
  66.9 2.1 %collective-permute-start.7 = (f32[32,1152]{1,0:T(8,128)S(1)}, f32[32,1152]{1,0:T(8,128)S(1)}, u32[]{:S(2)}, u32[]{:S(2)}) collective-permute-start(f32[32,1152]{1,0:T(8,128)S(1)} %get-tuple-element.55), channel_id=1, source_target_pairs={{0,24},{8,0},{16,8},{24,16},{32,56},{40,32},{48,40},{56,48},{64,88... | collective-permute-start | bytes 442376 | tf_op jit(solution)/shard_map/ppermute | solution.py:513
  69.1 0.4 collective-permute-done.5.refs_1_
  69.5 3.1 %collective-permute-done.6.refs_2_ = f32[32,1152]{1,0:T(8,128)S(1)} collective-permute-done((f32[32,1152]{1,0:T(8,128)S(1)}, f32[32,1152]{1,0:T(8,128)S(1)}, u32[]{:S(2)}, u32[]{:S(2)}) %collective-permute-start.6) | collective-permute-done | bytes 147488 | tf_op jit(solution)/shard_map/ppermute | solution.py:513
  72.6 1.1 %collective-permute-done.7.refs_3_ = f32[32,1152]{1,0:T(8,128)S(1)} collective-permute-done((f32[32,1152]{1,0:T(8,128)S(1)}, f32[32,1152]{1,0:T(8,128)S(1)}, u32[]{:S(2)}, u32[]{:S(2)}) %collective-permute-start.7) | collective-permute-done | bytes 147488 | tf_op jit(solution)/shard_map/ppermute | solution.py:513
  73.7 3.3 %collective-permute-start.8 = (f32[8,1152]{1,0:T(8,128)S(1)}, f32[8,1152]{1,0:T(8,128)S(1)}, u32[]{:S(2)}, u32[]{:S(2)}) collective-permute-start(f32[8,1152]{1,0:T(8,128)S(1)} %get-tuple-element.57), channel_id=1, source_target_pairs={{0,2},{2,4},{4,6},{6,0},{1,3},{3,5},{5,7},{7,1},{8,10},{10,12},{12... | collective-permute-start | bytes 110600 | tf_op jit(solution)/shard_map/ppermute | solution.py:522
  77.0 4.5 %collective-permute-start.9 = (f32[8,1152]{1,0:T(8,128)S(1)}, f32[8,1152]{1,0:T(8,128)S(1)}, u32[]{:S(2)}, u32[]{:S(2)}) collective-permute-start(f32[8,1152]{1,0:T(8,128)S(1)} %get-tuple-element.58), channel_id=1, source_target_pairs={{0,4},{2,6},{4,0},{6,2},{1,5},{3,7},{5,1},{7,3},{8,12},{10,14},{12... | collective-permute-start | bytes 110600 | tf_op jit(solution)/shard_map/ppermute | solution.py:522
  81.5 2.7 %collective-permute-start.10 = (f32[8,1152]{1,0:T(8,128)S(1)}, f32[8,1152]{1,0:T(8,128)S(1)}, u32[]{:S(2)}, u32[]{:S(2)}) collective-permute-start(f32[8,1152]{1,0:T(8,128)S(1)} %get-tuple-element.59), channel_id=1, source_target_pairs={{0,6},{2,0},{4,2},{6,4},{1,7},{3,1},{5,3},{7,5},{8,14},{10,8},{12,... | collective-permute-start | bytes 110600 | tf_op jit(solution)/shard_map/ppermute | solution.py:522
  84.2 1.1 %collective-permute-done.9.refs_2_ = f32[8,1152]{1,0:T(8,128)S(1)} collective-permute-done((f32[8,1152]{1,0:T(8,128)S(1)}, f32[8,1152]{1,0:T(8,128)S(1)}, u32[]{:S(2)}, u32[]{:S(2)}) %collective-permute-start.9) | collective-permute-done | bytes 36896 | tf_op jit(solution)/shard_map/ppermute | solution.py:522
  85.3 1.1 %collective-permute-done.10.refs_3_ = f32[8,1152]{1,0:T(8,128)S(1)} collective-permute-done((f32[8,1152]{1,0:T(8,128)S(1)}, f32[8,1152]{1,0:T(8,128)S(1)}, u32[]{:S(2)}, u32[]{:S(2)}) %collective-permute-start.10) | collective-permute-done | bytes 36896 | tf_op jit(solution)/shard_map/ppermute | solution.py:522
  86.4 11.4 %all_to_all.16.in_ref = f32[8,8,1152]{2,1,0:T(8,128)S(1)} all-to-all(f32[8,8,1152]{2,1,0:T(8,128)S(1)} %shard_map.147), channel_id=1, replica_groups=mesh['zl'=2,'y'=4,'x'=4,'zh'=4,'c'=2] {'zl','y'}, dimensions={0} | all-to-all | bytes 589824 | tf_op jit(solution)/shard_map/all_to_all | solution.py:526
  97.9 0.8 shard_map.148
  (27 shorter events, 1.0 us)
Async XLA Ops:
  6.8 14.6 %all-to-all-start = ((f32[8,100,128]{2,1,0:T(8,128)}), f32[8,100,128]{2,1,0:T(8,128)S(1)}, u32[]{:S(2)}, u32[]{:S(2)}) async-start(f32[8,100,128]{2,1,0:T(8,128)} %shard_map.136.x_hbm), calls=%async_computation | async-start | bytes 851968 | tf_op jit(solution)/shard_map/all_to_all | solution.py:419
  12.6 8.8 %copy-start.5 = (f32[100,1024]{1,0:T(8,128)S(1)}, f32[100,1024]{1,0:T(8,128)}, u32[]{:S(2)}) copy-start(f32[100,1024]{1,0:T(8,128)} %goal_hbm.1) | copy-start | bytes 1228804
  12.6 8.8 %copy-start.6 = (s32[1024]{0:T(1024)S(1)}, s32[1024]{0:T(1024)}, u32[]{:S(2)}) copy-start(s32[1024]{0:T(1024)} %param.11) | copy-start | bytes 12292
  12.7 8.7 %copy-start.7 = (f32[721]{0:T(1024)S(1)}, f32[721]{0:T(1024)}, u32[]{:S(2)}) copy-start(f32[721]{0:T(1024)} %table_hbm.1) | copy-start | bytes 8656
  12.7 8.7 %copy-start.8 = (f32[100]{0:T(128)S(1)}, f32[100]{0:T(128)}, u32[]{:S(2)}) copy-start(f32[100]{0:T(128)} %param.13) | copy-start | bytes 1204
  21.4 0.7 copy-start.9
  22.1 15.0 %copy-start = (bf16[1,1024,1024]{2,1,0:T(8,128)(2,1)S(1)}, bf16[1,1024,1024]{2,1,0:T(8,128)(2,1)}, u32[]{:S(2)}) copy-start(bf16[1,1024,1024]{2,1,0:T(8,128)(2,1)} %param.9) | copy-start | bytes 6291460
  22.1 15.0 %copy-start.1 = (bf16[1024,1024]{1,0:T(8,128)(2,1)S(1)}, bf16[1024,1024]{1,0:T(8,128)(2,1)}, u32[]{:S(2)}) copy-start(bf16[1024,1024]{1,0:T(8,128)(2,1)} %get-tuple-element.38.g_ref) | copy-start | bytes 6291460
  22.1 15.0 %copy-start.3 = (bf16[1024,100]{0,1:T(8,128)(2,1)S(1)}, bf16[1024,100]{0,1:T(8,128)(2,1)}, u32[]{:S(2)}) copy-start(bf16[1024,100]{0,1:T(8,128)(2,1)} %param.16) | copy-start | bytes 614404
  37.1 1.6 %copy-start.2 = (bf16[1024,1024]{1,0:T(8,128)(2,1)S(1)}, bf16[1024,1024]{1,0:T(8,128)(2,1)}, u32[]{:S(2)}) copy-start(bf16[1024,1024]{1,0:T(8,128)(2,1)} %get-tuple-element.42.z_ref) | copy-start | bytes 6291460
  38.2 2.7 %collective-permute-start = (f32[4,4,4,8,512]{4,3,2,1,0:T(8,128)S(1)}, f32[4,4,4,8,512]{4,3,2,1,0:T(8,128)S(1)}, u32[]{:S(2)}, u32[]{:S(2)}) collective-permute-start(f32[4,4,4,8,512]{4,3,2,1,0:T(8,128)S(1)} %get-tuple-element.44), channel_id=1, source_target_pairs={{0,1},{1,0},{2,3},{3,2},{4,5},{5,4},{6,7},{7,6},{8,9},{9,8},{10,11... | collective-permute-start | bytes 3145736 | tf_op jit(solution)/shard_map/ppermute | solution.py:465
  40.9 3.0 %collective-permute-start.1 = (f32[4,4,4,8,640]{4,3,2,1,0:T(8,128)S(1)}, f32[4,4,4,8,640]{4,3,2,1,0:T(8,128)S(1)}, u32[]{:S(2)}, u32[]{:S(2)}) collective-permute-start(f32[4,4,4,8,640]{4,3,2,1,0:T(8,128)S(1)} %shard_map.142), channel_id=1, source_target_pairs={{0,1},{1,0},{2,3},{3,2},{4,5},{5,4},{6,7},{7,6},{8,9},{9,8},{10,11... | collective-permute-start | bytes 3932168 | tf_op jit(solution)/shard_map/ppermute | solution.py:486
  42.3 6.6 %copy-start.4 = (bf16[1024,1024]{1,0:T(8,128)(2,1)S(1)}, bf16[1024,1024]{1,0:T(8,128)(2,1)}, u32[]{:S(2)}) copy-start(bf16[1024,1024]{1,0:T(8,128)(2,1)} %w_ref.1) | copy-start | bytes 6291460
  44.2 10.0 %collective-permute-start.2 = (f32[4,32,1152]{2,1,0:T(8,128)S(1)}, f32[4,32,1152]{2,1,0:T(8,128)S(1)}, u32[]{:S(2)}, u32[]{:S(2)}) collective-permute-start(f32[4,32,1152]{2,1,0:T(8,128)S(1)} %get-tuple-element.49), channel_id=1, source_target_pairs={{0,32},{8,40},{16,48},{24,56},{32,0},{40,8},{48,16},{56,24},{64,96... | collective-permute-start | bytes 1769480 | tf_op jit(solution)/shard_map/ppermute | solution.py:504
  44.7 16.3 %collective-permute-start.3 = (f32[4,32,1152]{2,1,0:T(8,128)S(1)}, f32[4,32,1152]{2,1,0:T(8,128)S(1)}, u32[]{:S(2)}, u32[]{:S(2)}) collective-permute-start(f32[4,32,1152]{2,1,0:T(8,128)S(1)} %get-tuple-element.50), channel_id=1, source_target_pairs={{0,64},{8,72},{16,80},{24,88},{32,96},{40,104},{48,112},{56,120},{... | collective-permute-start | bytes 1769480 | tf_op jit(solution)/shard_map/ppermute | solution.py:504
  46.7 17.4 %collective-permute-start.4 = (f32[4,32,1152]{2,1,0:T(8,128)S(1)}, f32[4,32,1152]{2,1,0:T(8,128)S(1)}, u32[]{:S(2)}, u32[]{:S(2)}) collective-permute-start(f32[4,32,1152]{2,1,0:T(8,128)S(1)} %get-tuple-element.51), channel_id=1, source_target_pairs={{0,96},{8,104},{16,112},{24,120},{32,64},{40,72},{48,80},{56,88},{... | collective-permute-start | bytes 1769480 | tf_op jit(solution)/shard_map/ppermute | solution.py:504
  64.3 5.2 %collective-permute-start.5 = (f32[32,1152]{1,0:T(8,128)S(1)}, f32[32,1152]{1,0:T(8,128)S(1)}, u32[]{:S(2)}, u32[]{:S(2)}) collective-permute-start(f32[32,1152]{1,0:T(8,128)S(1)} %get-tuple-element.53), channel_id=1, source_target_pairs={{0,8},{8,16},{16,24},{24,0},{32,40},{40,48},{48,56},{56,32},{64,72... | collective-permute-start | bytes 442376 | tf_op jit(solution)/shard_map/ppermute | solution.py:513
  65.8 6.8 %collective-permute-start.6 = (f32[32,1152]{1,0:T(8,128)S(1)}, f32[32,1152]{1,0:T(8,128)S(1)}, u32[]{:S(2)}, u32[]{:S(2)}) collective-permute-start(f32[32,1152]{1,0:T(8,128)S(1)} %get-tuple-element.54), channel_id=1, source_target_pairs={{0,16},{8,24},{16,0},{24,8},{32,48},{40,56},{48,32},{56,40},{64,80... | collective-permute-start | bytes 442376 | tf_op jit(solution)/shard_map/ppermute | solution.py:513
  66.9 6.7 %collective-permute-start.7 = (f32[32,1152]{1,0:T(8,128)S(1)}, f32[32,1152]{1,0:T(8,128)S(1)}, u32[]{:S(2)}, u32[]{:S(2)}) collective-permute-start(f32[32,1152]{1,0:T(8,128)S(1)} %get-tuple-element.55), channel_id=1, source_target_pairs={{0,24},{8,0},{16,8},{24,16},{32,56},{40,32},{48,40},{56,48},{64,88... | collective-permute-start | bytes 442376 | tf_op jit(solution)/shard_map/ppermute | solution.py:513
  73.7 10.5 %collective-permute-start.8 = (f32[8,1152]{1,0:T(8,128)S(1)}, f32[8,1152]{1,0:T(8,128)S(1)}, u32[]{:S(2)}, u32[]{:S(2)}) collective-permute-start(f32[8,1152]{1,0:T(8,128)S(1)} %get-tuple-element.57), channel_id=1, source_target_pairs={{0,2},{2,4},{4,6},{6,0},{1,3},{3,5},{5,7},{7,1},{8,10},{10,12},{12... | collective-permute-start | bytes 110600 | tf_op jit(solution)/shard_map/ppermute | solution.py:522
  77.0 8.3 %collective-permute-start.9 = (f32[8,1152]{1,0:T(8,128)S(1)}, f32[8,1152]{1,0:T(8,128)S(1)}, u32[]{:S(2)}, u32[]{:S(2)}) collective-permute-start(f32[8,1152]{1,0:T(8,128)S(1)} %get-tuple-element.58), channel_id=1, source_target_pairs={{0,4},{2,6},{4,0},{6,2},{1,5},{3,7},{5,1},{7,3},{8,12},{10,14},{12... | collective-permute-start | bytes 110600 | tf_op jit(solution)/shard_map/ppermute | solution.py:522
  81.5 4.9 %collective-permute-start.10 = (f32[8,1152]{1,0:T(8,128)S(1)}, f32[8,1152]{1,0:T(8,128)S(1)}, u32[]{:S(2)}, u32[]{:S(2)}) collective-permute-start(f32[8,1152]{1,0:T(8,128)S(1)} %get-tuple-element.59), channel_id=1, source_target_pairs={{0,6},{2,0},{4,2},{6,4},{1,7},{3,1},{5,3},{7,5},{8,14},{10,8},{12,... | collective-permute-start | bytes 110600 | tf_op jit(solution)/shard_map/ppermute | solution.py:522
